TPU v7x, 32 devices: a whole 2x2x4 slice. The times are simulated.
32 devices in a mesh: pipe: 2 (over y), dp: 4 (over z), expert: 4 (over x, core).
Axes of the slice: x: 2, y: 2, z: 4, core: 2. Of those that a mesh axis runs over, the one named last changes fastest.
Arguments:
- input_grad: bfloat16 [2, 2048, 2048], P('pipe', ('dp', 'expert')), may hold values from -0.1796875 to 0.1796875
- gate_prob: float32 [2, 2048], P('pipe', ('dp', 'expert')), may hold values from 0.2 to 1
- expert_route: int32 [2, 2048, 1], P('pipe', ('dp', 'expert')), may hold values from 0 to 1; in each aligned block of 128 rows (0 to 127, 128 to 255, ..., all dimensions but the last counted through in order) at most 128 rows name the same one
- saved_hidden: bfloat16 [2, 4, 4, 128, 5632], P('pipe', 'dp', None, None, 'expert'), may hold values from -6 to 6
Outputs:
- down_grad: bfloat16 [2, 2048, 5632], P('pipe', 'dp', 'expert')
Inputs may be any that keep to these rules, and one draw needn't show every extreme that they name: `expert_route`: among the 128 tokens of one index of dp and expert no expert is named more than 128 times, and in every draw some expert is named exactly 128 times by some device's tokens.
All inputs are finite; a program needn't handle non-finite values.
Results may differ from a plain program's by a relative error of at most 0.014.
Values may be sent and summed in bfloat16 or wider, within the bound.
No kernel may reach another device: no remote copies, remote signals or barrier semaphores. Data moves between devices by JAX's collectives and lax.ppermute only.
A program may use at most 64 MiB of HBM per device.

v0:
```python
import jax
import jax.numpy as jnp
from jax import lax
from jax.sharding import PartitionSpec as P


def shifted(value, axis, steps):
    count = lax.axis_size(axis)
    pairs = [(source, (source + steps) % count) for source in range(count)]
    return lax.ppermute(value, axis, pairs)


def swapped(value, axis, apart):
    mask = 2**apart
    pairs = [(source, source ^ mask) for source in range(lax.axis_size(axis))]
    return lax.ppermute(value, axis, pairs)


def body(input_grad, gate_prob, expert_route, saved_hidden):
    grad_rows = shifted(input_grad, "pipe", -1)[0]
    flight_count = lax.axis_size("expert") // 2
    capacity = saved_hidden.shape[3]
    token_count = grad_rows.shape[0]
    model_width = grad_rows.shape[1]
    routes = expert_route[0, :, 0]
    one_hot = (routes[:, None] == jnp.arange(flight_count, dtype=jnp.int32)[None, :]).astype(
        jnp.float32
    )
    row_ids = lax.broadcasted_iota(jnp.int32, (token_count, token_count), 0)
    column_ids = lax.broadcasted_iota(jnp.int32, (token_count, token_count), 1)
    earlier_mask = (column_ids < row_ids).astype(jnp.float32)
    before = jnp.dot(earlier_mask, one_hot, precision=lax.Precision.HIGHEST)
    position = jnp.sum(before * one_hot, axis=1)
    slot_values = jnp.arange(capacity, dtype=jnp.float32)
    slot_hit = one_hot[:, :, None] * (position[:, None, None] == slot_values[None, None, :]).astype(
        jnp.float32
    )
    scaled = (gate_prob[0][:, None] * grad_rows.astype(jnp.float32)).astype(jnp.bfloat16)
    outgoing = jnp.einsum(
        "tec,td->ecd", slot_hit.astype(jnp.bfloat16), scaled, preferred_element_type=jnp.float32
    ).astype(jnp.bfloat16)
    halves = outgoing.reshape(2 * flight_count, capacity // 2, model_width)
    owned_rows = lax.all_to_all(halves, "expert", split_axis=0, concat_axis=0, tiled=True)
    partner_rows = swapped(owned_rows, "expert", 0)
    parity = lax.axis_index("expert") % 2
    first_half = jnp.where(parity == 0, owned_rows, partner_rows)
    second_half = jnp.where(parity == 0, partner_rows, owned_rows)
    received = jnp.concatenate([first_half, second_half], axis=1)
    source_count = received.shape[0]
    flat_rows = received.reshape(source_count * capacity, model_width)
    hidden = saved_hidden.reshape(source_count * capacity, saved_hidden.shape[4])
    summed = lax.psum_scatter(
        lax.dot_general(
            flat_rows, hidden, (((0,), (0,)), ((), ())), preferred_element_type=jnp.float32
        ).astype(jnp.bfloat16),
        "dp",
        scatter_dimension=0,
        tiled=True,
    )
    return summed[None]


def solution(mesh):
    in_specs = (
        P("pipe", ("dp", "expert"), None),
        P("pipe", ("dp", "expert")),
        P("pipe", ("dp", "expert"), None),
        P("pipe", "dp", None, None, "expert"),
    )
    out_specs = P("pipe", "dp", "expert")
    return jax.shard_map(body, mesh=mesh, in_specs=in_specs, out_specs=out_specs, check_vma=False)
```

profile of v0, /device:TPU:0, one launch (start us, length us, event | category | flops | bytes accessed | tf_op | source)
XLA Modules:
  0.0 158.0 jit_solution(2960491651452403637)
XLA Ops:
  6.5 0.0 copy-start
  6.5 0.0 reduce-scatter.2.cloned.1.call-start
  6.5 3.0 %collective-permute-start = (bf16[1,128,2048]{2,1,0:T(8,128)(2,1)}, bf16[1,128,2048]{2,1,0:T(8,128)(2,1)S(1)}, u32[]{:S(2)}, u32[]{:S(2)}) collective-permute-start(bf16[1,128,2048]{2,1,0:T(8,128)(2,1)} %param.4), channel_id=1, source_target_pairs={{0,16},{16,0},{1,17},{17,1},{2,18},{18,2},{3,19},{19,3},{4,20},{20... | collective-permute-start | bytes 1572872 | tf_op jit(solution)/shard_map/ppermute | solution.py:10
  9.5 0.9 fusion
  10.4 0.7 fusion.9
  11.1 10.5 %collective-permute-done = bf16[1,128,2048]{2,1,0:T(8,128)(2,1)S(1)} collective-permute-done((bf16[1,128,2048]{2,1,0:T(8,128)(2,1)}, bf16[1,128,2048]{2,1,0:T(8,128)(2,1)S(1)}, u32[]{:S(2)}, u32[]{:S(2)}) %collective-permute-start) | collective-permute-done | bytes 524320 | tf_op jit(solution)/shard_map/ppermute | solution.py:10
  21.6 1.2 convolution_convert_fusion.1
  22.8 17.2 %all_to_all.5 = bf16[4,64,2048]{2,1,0:T(8,128)(2,1)S(1)} all-to-all(bf16[4,64,2048]{2,1,0:T(8,128)(2,1)S(1)} %bitcast.18), channel_id=1, replica_groups=mesh['pipe'=2,'dp'=4,'expert'=4] {'expert'}, dimensions={0} | all-to-all | bytes 2097152 | tf_op jit(solution)/shard_map/all_to_all | solution.py:43
  40.0 0.0 collective-permute-start.1
  40.1 2.7 %collective-permute-done.1 = bf16[4,64,2048]{2,1,0:T(8,128)(2,1)S(1)} collective-permute-done((bf16[4,64,2048]{2,1,0:T(8,128)(2,1)S(1)}, bf16[4,64,2048]{2,1,0:T(8,128)(2,1)S(1)}, u32[]{:S(2)}, u32[]{:S(2)}) %collective-permute-start.1) | collective-permute-done | bytes 1048608 | tf_op jit(solution)/shard_map/ppermute | solution.py:16
  42.7 0.1 broadcast_select_fusion.1
  42.9 0.1 pad_maximum_fusion
  43.0 0.0 copy-done
  43.0 5.4 %convolution_convert_fusion = bf16[2048,1408]{1,0:T(8,128)(2,1)} fusion(bf16[512,2048]{1,0:T(8,128)(2,1)S(1)} %bitcast.19, bf16[512,1408]{1,0:T(8,128)(2,1)S(1)} %bitcast.17), kind=kOutput, calls=%fused_computation | convolution fusion | flops 2955673600 | bytes 9306112 | tf_op jit(solution)/shard_map/dot_general | solution.py:53
  48.4 0.0 reduce-scatter.2.cloned.1.call-update
  48.4 102.7 %reduce-scatter.2.cloned.1.call-done = bf16[512,1408]{1,0:T(8,128)(2,1)} async-done(((bf16[2048,1408]{1,0:T(8,128)(2,1)}), bf16[512,1408]{1,0:T(8,128)(2,1)}) %reduce-scatter.2.cloned.1.call-update) | async-done | bytes 1441808 | tf_op jit(solution)/shard_map/reduce_scatter | solution.py:52
  (1 shorter events, 0.0 us)
Async XLA Ops:
  6.5 36.5 %copy-start = (bf16[1,1,4,128,1408]{4,3,2,1,0:T(8,128)(2,1)S(1)}, bf16[1,1,4,128,1408]{4,3,2,1,0:T(8,128)(2,1)}, u32[]{:S(2)}) copy-start(bf16[1,1,4,128,1408]{4,3,2,1,0:T(8,128)(2,1)} %param.7) | copy-start | bytes 4325380
  6.5 144.6 %reduce-scatter.2.cloned.1.call-start = ((), (), s32[]{:S(2)}) async-start(), calls=%async_computation.2 | async-start | bytes 7208960 | tf_op jit(solution)/shard_map/reduce_scatter | solution.py:52
  6.5 15.1 %collective-permute-start = (bf16[1,128,2048]{2,1,0:T(8,128)(2,1)}, bf16[1,128,2048]{2,1,0:T(8,128)(2,1)S(1)}, u32[]{:S(2)}, u32[]{:S(2)}) collective-permute-start(bf16[1,128,2048]{2,1,0:T(8,128)(2,1)} %param.4), channel_id=1, source_target_pairs={{0,16},{16,0},{1,17},{17,1},{2,18},{18,2},{3,19},{19,3},{4,20},{20... | collective-permute-start | bytes 1572872 | tf_op jit(solution)/shard_map/ppermute | solution.py:10
  40.0 2.7 %collective-permute-start.1 = (bf16[4,64,2048]{2,1,0:T(8,128)(2,1)S(1)}, bf16[4,64,2048]{2,1,0:T(8,128)(2,1)S(1)}, u32[]{:S(2)}, u32[]{:S(2)}) collective-permute-start(bf16[4,64,2048]{2,1,0:T(8,128)(2,1)S(1)} %all_to_all.5), channel_id=1, source_target_pairs={{0,1},{1,0},{2,3},{3,2},{4,5},{5,4},{6,7},{7,6},{8,9},{9,8},{10,11... | collective-permute-start | bytes 3145736 | tf_op jit(solution)/shard_map/ppermute | solution.py:16
Sparse Core Ops, SparseCore 0:
  48.5 102.5 reduce-scatter.1
where the time goes:
time: 158 us
  waiting for transfers between devices  116 us (73%)
  blocking collectives  17.2 us (11%)
  between operations  13.4 us (8%)
  matrix products  7.39 us (5%)
  starting transfers between devices  2.97 us (2%)
    reduce_scatter x1, waiting for transfers between devices, body(): lax.psum_scatter(lax.dot_general(flat_rows, hidden, (((0,), (0,)), ((), (...  103 us
    all_to_all x1, blocking collectives, body(): lax.all_to_all(halves, 'expert', split_axis=0, concat_axis=0, tiled=True)  17.2 us
    ppermute x1, waiting for transfers between devices, shifted(): return lax.ppermute(value, axis, pairs)  10.5 us
    dot_general x1, matrix products, body(): lax.dot_general(flat_rows, hidden, (((0,), (0,)), ((), ())), preferred_el...  5.36 us
  transfers between devices with their start and end apart: 3, of which 3 were waited for; matrix products, arithmetic and copies ran while one was open for 1% of the time, Pallas kernels for 0%

commit v1 on v0

--- a/solution.py
+++ b/solution.py
@@ -10,13 +10,12 @@
     return lax.ppermute(value, axis, pairs)
 
 
-def swapped(value, axis, apart):
-    mask = 2**apart
+def crossed(value, axis, mask):
     pairs = [(source, source ^ mask) for source in range(lax.axis_size(axis))]
     return lax.ppermute(value, axis, pairs)
 
 
-def body(input_grad, gate_prob, expert_route, saved_hidden):
+def general_body(input_grad, gate_prob, expert_route, saved_hidden):
     grad_rows = shifted(input_grad, "pipe", -1)[0]
     flight_count = lax.axis_size("expert") // 2
     capacity = saved_hidden.shape[3]
@@ -41,7 +40,7 @@
     ).astype(jnp.bfloat16)
     halves = outgoing.reshape(2 * flight_count, capacity // 2, model_width)
     owned_rows = lax.all_to_all(halves, "expert", split_axis=0, concat_axis=0, tiled=True)
-    partner_rows = swapped(owned_rows, "expert", 0)
+    partner_rows = crossed(owned_rows, "expert", 1)
     parity = lax.axis_index("expert") % 2
     first_half = jnp.where(parity == 0, owned_rows, partner_rows)
     second_half = jnp.where(parity == 0, partner_rows, owned_rows)
@@ -60,6 +59,100 @@
     return summed[None]
 
 
+def column_cuts(width, parts):
+    tiles = width // 128
+    edges = [128 * ((tiles * part) // parts) for part in range(parts)] + [width]
+    return list(zip(edges[:-1], edges[1:]))
+
+
+def pair_body(input_grad, gate_prob, expert_route, saved_hidden):
+    bf16, f32 = jnp.bfloat16, jnp.float32
+    replicas, shards = lax.axis_size("dp"), lax.axis_size("expert")
+    replica, shard = lax.axis_index("dp"), lax.axis_index("expert")
+    expert, core = shard // 2, shard % 2
+    tokens, width = input_grad.shape[1], input_grad.shape[2]
+    half = tokens // 2
+    sources, hidden_width = saved_hidden.shape[2], saved_hidden.shape[4]
+    hidden = saved_hidden[0, 0]
+    inner = (replica == 1) | (replica == 2)
+    cuts = column_cuts(hidden_width, 4)
+
+    grad_rows = shifted(input_grad, "pipe", -1)[0]
+    spilled = [crossed(hidden[:, half:, low:high], "expert", 2) for low, high in cuts]
+
+    routes = expert_route[0, :, 0]
+    mine = jnp.sum((routes == 0).astype(f32))
+    lane = lax.broadcasted_iota(jnp.int32, (8, 128), 1)
+    tally = jnp.where(lane == replica * shards + shard, mine, 0.0)
+    tally = tally + crossed(tally, "expert", 1) + crossed(tally, "expert", 2) + crossed(tally, "expert", 3)
+    counts = tally + crossed(tally, "dp", 1) + crossed(tally, "dp", 2) + crossed(tally, "dp", 3)
+
+    def held(table, owner):
+        wanted = lane[:1, :, None] * 0 + lax.broadcasted_iota(jnp.int32, (1, 128, sources), 2)
+        hit = lane[:1, :, None] == owner * shards + wanted
+        zeros = jnp.sum(jnp.where(hit, table[:1, :, None], 0.0), axis=1)[0]
+        own = jnp.where(expert == 0, zeros, tokens - zeros)
+        return jnp.arange(half, dtype=f32)[None, :] < own[:, None]
+
+    keep = held(tally, replica)
+    mirror = (jnp.arange(half)[:, None] + jnp.arange(half)[None, :] == half - 1).astype(bf16)
+    blocks = []
+    for (low, high), spill in zip(cuts, spilled):
+        turned = jnp.einsum("cs,isk->ick", mirror, spill, preferred_element_type=f32).astype(bf16)
+        packed = jnp.where(keep[:, :, None], hidden[:, :half, low:high], turned)
+        packed = packed.reshape(sources * half, high - low)
+        first = crossed(packed, "dp", 1)
+        near = lax.ppermute(packed, "dp", [(1, 2), (2, 1)])
+        far = lax.ppermute(packed, "dp", [(0, 2), (3, 1)])
+        near_out = lax.ppermute(near, "dp", [(2, 3), (1, 0)])
+        far_out = lax.ppermute(far, "dp", [(2, 3), (1, 0)])
+        blocks.append(
+            jnp.concatenate(
+                [packed, first, jnp.where(inner, far, near_out), jnp.where(inner, near, far_out)], axis=0
+            )
+        )
+
+    index = lax.broadcasted_iota(jnp.int32, (tokens, tokens), 0)
+    other = lax.broadcasted_iota(jnp.int32, (tokens, tokens), 1)
+    earlier = (index < other) & (routes[:, None] == routes[None, :])
+    slot = jnp.sum(earlier.astype(jnp.int32), axis=0)
+    place = jnp.where(routes == 0, slot, tokens - 1 - slot)
+    place = jnp.where(place < half, place, tokens + half - 1 - place)
+    pick = (index == place[None, :]).astype(bf16)
+    scaled = (gate_prob[0][:, None] * grad_rows.astype(f32)).astype(bf16)
+    rows = jnp.dot(pick, scaled, preferred_element_type=f32).astype(bf16)
+    part = width // replicas // 2
+    pieces = rows.reshape(2, half, replicas, 2, part).transpose(0, 3, 2, 1, 4)
+    pieces = pieces.reshape(shards, replicas, half, part)
+
+    def piece(values, at):
+        return lax.dynamic_index_in_dim(values, at, 0, keepdims=False)
+
+    got = [piece(pieces, shard)] + [
+        crossed(piece(pieces, shard ^ mask), "expert", mask) for mask in (1, 2, 3)
+    ]
+    got = jnp.stack(got)
+    ordered = jnp.stack([piece(got, shard ^ source) for source in range(sources)], axis=1)
+    arrived = [piece(ordered, replica)] + [
+        crossed(piece(ordered, replica ^ mask), "dp", mask) for mask in (1, 2, 3)
+    ]
+    arrived = jnp.stack(arrived)
+    swapped = crossed(arrived, "expert", 1)
+    left = jnp.where(core == 0, arrived, swapped)
+    right = jnp.where(core == 0, swapped, arrived)
+    grads = jnp.concatenate([left, right], axis=3)
+    ours = jnp.stack([held(counts, replica ^ mask) for mask in range(replicas)])[..., None]
+    both = jnp.concatenate([jnp.where(ours, grads, 0), jnp.where(ours, 0, grads)], axis=3)
+    both = both.reshape(replicas * sources * half, 4 * part)
+
+    outs = []
+    for block in blocks:
+        total = lax.dot_general(both, block, (((0,), (0,)), ((), ())), preferred_element_type=f32)
+        theirs = crossed(total[2 * part :].astype(bf16), "expert", 2)
+        outs.append((total[: 2 * part] + theirs.astype(f32)).astype(bf16))
+    return jnp.concatenate(outs, axis=1)[None]
+
+
 def solution(mesh):
     in_specs = (
         P("pipe", ("dp", "expert"), None),
@@ -68,4 +161,14 @@
         P("pipe", "dp", None, None, "expert"),
     )
     out_specs = P("pipe", "dp", "expert")
-    return jax.shard_map(body, mesh=mesh, in_specs=in_specs, out_specs=out_specs, check_vma=False)
+
+    def run(input_grad, gate_prob, expert_route, saved_hidden):
+        devices = mesh.shape["dp"] * mesh.shape["expert"]
+        tokens = input_grad.shape[1] // devices
+        pairs = mesh.shape["expert"] == 4 and mesh.shape["dp"] == 4
+        body = pair_body if pairs and saved_hidden.shape[3] == tokens else general_body
+        return jax.shard_map(body, mesh=mesh, in_specs=in_specs, out_specs=out_specs, check_vma=False)(
+            input_grad, gate_prob, expert_route, saved_hidden
+        )
+
+    return run

time: 158 us -> 147 us (0.930)
  starting transfers between devices: 2.97 us -> 55.6 us
  waiting for transfers between devices: 116 us -> 73.1 us
  blocking collectives: 17.2 us -> 0 us
  between operations: 13.4 us -> 0.72 us
  other arithmetic: 0.98 us -> 6.92 us
  local copies, waits for them, and re-layouts: 0.01 us -> 4.58 us
  matrix products: 7.39 us -> 5.81 us
    reduce_scatter x1 -> x0, waiting for transfers between devices: 103 us -> none  [body(): lax.psum_scatter(lax.dot_general(flat_rows, hidden, (((0,), (0,)), ((), (...]
    ppermute x1 -> x41, waiting for transfers between devices: 2.66 us -> 73.1 us  [the longest x25 39.4 us: crossed(): return lax.ppermute(value, axis, pairs)]
    ppermute x1 -> x41, starting transfers between devices: 0.01 us -> 54.1 us  [the longest x25 28.1 us: crossed(): return lax.ppermute(value, axis, pairs)]
    all_to_all x1 -> x0, blocking collectives: 17.2 us -> none  [body(): lax.all_to_all(halves, 'expert', split_axis=0, concat_axis=0, tiled=True)]
    ppermute x1, waiting for transfers between devices: 10.5 us -> 0.01 us  [shifted(): return lax.ppermute(value, axis, pairs)]
    select_n x1 -> x15, other arithmetic: 0.14 us -> 3.31 us  [the longest x4 0.75 us: pair_body(): jnp.where(inner, far, near_out)]
    reduce_sum x0 -> x3, other arithmetic: none -> 2.45 us  [the longest x1 1.37 us: pair_body(): mine = jnp.sum((routes == 0).astype(f32))]
    slice x0 -> x8, local copies, waits for them, and re-layouts: none -> 2.3 us  [the longest x2 2.1 us: pair_body(): hidden[:, half:, low:high]]
  transfers between devices with their start and end apart: 3 -> 42, of which waited for: 3 -> 15; matrix products, arithmetic and copies ran while one was open for 1% -> 9% of each run, Pallas kernels for 0% -> 0%
where the time goes in v1:
time: 147 us
  waiting for transfers between devices  73.1 us (50%)
  starting transfers between devices  55.6 us (38%)
  other arithmetic  6.92 us (5%)
  matrix products  5.81 us (4%)
  local copies, waits for them, and re-layouts  4.58 us (3%)
    ppermute x25, waiting for transfers between devices, crossed(): return lax.ppermute(value, axis, pairs)  39.4 us
    ppermute x25, starting transfers between devices, crossed(): return lax.ppermute(value, axis, pairs)  28.1 us
    ppermute x4, waiting for transfers between devices, pair_body(): far_out = lax.ppermute(far, 'dp', [(2, 3), (1, 0)])  21 us
    ppermute x4, starting transfers between devices, pair_body(): far = lax.ppermute(packed, 'dp', [(0, 2), (3, 1)])  13 us
    ppermute x4, waiting for transfers between devices, pair_body(): near_out = lax.ppermute(near, 'dp', [(2, 3), (1, 0)])  12.7 us
    ppermute x4, starting transfers between devices, pair_body(): far_out = lax.ppermute(far, 'dp', [(2, 3), (1, 0)])  5.15 us
    ppermute x4, starting transfers between devices, pair_body(): near_out = lax.ppermute(near, 'dp', [(2, 3), (1, 0)])  5.15 us
    dot_general x4, matrix products, pair_body(): lax.dot_general(both, block, (((0,), (0,)), ((), ())), preferred_element_...  3.8 us
  transfers between devices with their start and end apart: 42, of which 15 were waited for; matrix products, arithmetic and copies ran while one was open for 9% of the time, Pallas kernels for 0%

profile of v1, /device:TPU:0, one launch (start us, length us, event | category | flops | bytes accessed | tf_op | source)
XLA Modules:
  0.0 146.7 jit_solution(10159090006898975446)
XLA Ops:
  0.0 1.4 fusion.59
  2.0 2.4 %collective-permute-start.2 = (f32[8,128]{1,0:T(8,128)S(1)}, f32[8,128]{1,0:T(8,128)S(1)}, u32[]{:S(2)}, u32[]{:S(2)}) collective-permute-start(f32[8,128]{1,0:T(8,128)S(1)} %iota.95), channel_id=1, source_target_pairs={{0,3},{1,2},{2,1},{3,0},{4,7},{5,6},{6,5},{7,4},{8,11},{9,10},{10,... | collective-permute-start | bytes 12296 | tf_op jit(solution)/shard_map/ppermute | solution.py:15
  5.2 1.2 fusion.68
  6.4 1.8 %collective-permute-start.35 = (bf16[4,64,384]{2,1,0:T(8,128)(2,1)S(1)}, bf16[4,64,384]{2,1,0:T(8,128)(2,1)S(1)}, u32[]{:S(2)}, u32[]{:S(2)}) collective-permute-start(bf16[4,64,384]{2,1,0:T(8,128)(2,1)S(1)} %get-tuple-element.11), channel_id=1, source_target_pairs={{0,2},{1,3},{2,0},{3,1},{4,6},{5,7},{6,4},{7,5},{8,10},{9,11},{10,... | collective-permute-start | bytes 589832 | tf_op jit(solution)/shard_map/ppermute | solution.py:15
  8.2 1.5 %collective-permute-start.6 = (bf16[1,128,2048]{2,1,0:T(8,128)(2,1)}, bf16[1,128,2048]{2,1,0:T(8,128)(2,1)S(1)}, u32[]{:S(2)}, u32[]{:S(2)}) collective-permute-start(bf16[1,128,2048]{2,1,0:T(8,128)(2,1)} %param.4), channel_id=1, source_target_pairs={{0,16},{16,0},{1,17},{17,1},{2,18},{18,2},{3,19},{19,3},{4,20},{20... | collective-permute-start | bytes 1572872 | tf_op jit(solution)/shard_map/ppermute | solution.py:10
  9.7 0.8 convert_reduce_fusion
  11.2 0.9 slice.91
  12.2 3.7 %collective-permute-start.5 = (f32[8,128]{1,0:T(8,128)S(1)}, f32[8,128]{1,0:T(8,128)S(1)}, u32[]{:S(2)}, u32[]{:S(2)}) collective-permute-start(f32[8,128]{1,0:T(8,128)S(1)} %add_add_fusion.1), channel_id=1, source_target_pairs={{0,12},{4,8},{8,4},{12,0},{1,13},{5,9},{9,5},{13,1},{2,14},{6,10},... | collective-permute-start | bytes 12296 | tf_op jit(solution)/shard_map/ppermute | solution.py:15
  16.7 1.1 collective-permute-done.5
  18.2 2.2 %collective-permute-done.4 = f32[8,128]{1,0:T(8,128)S(1)} collective-permute-done((f32[8,128]{1,0:T(8,128)S(1)}, f32[8,128]{1,0:T(8,128)S(1)}, u32[]{:S(2)}, u32[]{:S(2)}) %collective-permute-start.4) | collective-permute-done | bytes 4128 | tf_op jit(solution)/shard_map/ppermute | solution.py:15
  21.0 1.5 %collective-permute-start.14 = (bf16[4,64,256]{2,1,0:T(8,128)(2,1)S(1)}, bf16[4,64,256]{2,1,0:T(8,128)(2,1)}, u32[]{:S(2)}, u32[]{:S(2)}) collective-permute-start(bf16[4,64,256]{2,1,0:T(8,128)(2,1)S(1)} %slice.91), channel_id=1, source_target_pairs={{0,2},{1,3},{2,0},{3,1},{4,6},{5,7},{6,4},{7,5},{8,10},{9,11},{10,... | collective-permute-start | bytes 393224 | tf_op jit(solution)/shard_map/ppermute | solution.py:15
  23.2 7.2 %collective-permute-done.14 = bf16[4,64,256]{2,1,0:T(8,128)(2,1)} collective-permute-done((bf16[4,64,256]{2,1,0:T(8,128)(2,1)S(1)}, bf16[4,64,256]{2,1,0:T(8,128)(2,1)}, u32[]{:S(2)}, u32[]{:S(2)}) %collective-permute-start.14) | collective-permute-done | bytes 131104 | tf_op jit(solution)/shard_map/ppermute | solution.py:15
  30.4 1.1 fusion.7
  32.1 5.1 %collective-permute-start.16 = (bf16[256,256]{1,0:T(8,128)(2,1)S(1)}, bf16[256,256]{1,0:T(8,128)(2,1)S(1)}, u32[]{:S(2)}, u32[]{:S(2)}) collective-permute-start(bf16[256,256]{1,0:T(8,128)(2,1)S(1)} %bitcast.106), channel_id=1, source_target_pairs={{0,8},{12,4},{1,9},{13,5},{2,10},{14,6},{3,11},{15,7},{16,24},{28,... | collective-permute-start | bytes 393224 | tf_op jit(solution)/shard_map/ppermute | solution.py:106
  38.4 4.1 %collective-permute-start.37 = (bf16[256,384]{1,0:T(8,128)(2,1)S(1)}, bf16[256,384]{1,0:T(8,128)(2,1)S(1)}, u32[]{:S(2)}, u32[]{:S(2)}) collective-permute-start(bf16[256,384]{1,0:T(8,128)(2,1)S(1)} %bitcast.102), channel_id=1, source_target_pairs={{0,8},{12,4},{1,9},{13,5},{2,10},{14,6},{3,11},{15,7},{16,24},{28,... | collective-permute-start | bytes 589832 | tf_op jit(solution)/shard_map/ppermute | solution.py:106
  42.4 1.3 collective-permute-start.19
  44.6 4.7 %collective-permute-done.19 = bf16[256,256]{1,0:T(8,128)(2,1)S(1)} collective-permute-done((bf16[256,256]{1,0:T(8,128)(2,1)S(1)}, bf16[256,256]{1,0:T(8,128)(2,1)S(1)}, u32[]{:S(2)}, u32[]{:S(2)}) %collective-permute-start.19) | collective-permute-done | bytes 131104 | tf_op jit(solution)/shard_map/ppermute | solution.py:108
  49.3 1.3 collective-permute-start.18
  51.3 4.9 %collective-permute-done.18 = bf16[256,256]{1,0:T(8,128)(2,1)S(1)} collective-permute-done((bf16[256,256]{1,0:T(8,128)(2,1)S(1)}, bf16[256,256]{1,0:T(8,128)(2,1)S(1)}, u32[]{:S(2)}, u32[]{:S(2)}) %collective-permute-start.18) | collective-permute-done | bytes 131104 | tf_op jit(solution)/shard_map/ppermute | solution.py:107
  56.1 1.4 collective-permute-start.30
  58.2 1.3 collective-permute-start.40
  59.5 1.3 collective-permute-start.39
  61.9 3.9 %collective-permute-done.40 = bf16[256,384]{1,0:T(8,128)(2,1)S(1)} collective-permute-done((bf16[256,384]{1,0:T(8,128)(2,1)S(1)}, bf16[256,384]{1,0:T(8,128)(2,1)S(1)}, u32[]{:S(2)}, u32[]{:S(2)}) %collective-permute-start.40) | collective-permute-done | bytes 196640 | tf_op jit(solution)/shard_map/ppermute | solution.py:108
  66.5 1.4 collective-permute-done.39
  67.9 2.4 %collective-permute-start.23 = (bf16[256,384]{1,0:T(8,128)(2,1)S(1)}, bf16[256,384]{1,0:T(8,128)(2,1)S(1)}, u32[]{:S(2)}, u32[]{:S(2)}) collective-permute-start(bf16[256,384]{1,0:T(8,128)(2,1)S(1)} %bitcast.97), channel_id=1, source_target_pairs={{0,8},{12,4},{1,9},{13,5},{2,10},{14,6},{3,11},{15,7},{16,24},{28,... | collective-permute-start | bytes 589832 | tf_op jit(solution)/shard_map/ppermute | solution.py:106
  70.4 1.3 collective-permute-start.33
  71.7 1.3 collective-permute-start.32
  73.3 1.5 collective-permute-start.12
  74.8 2.7 %collective-permute-start.11 = (bf16[4,64,256]{2,1,0:T(8,128)(2,1)S(1)}, bf16[4,64,256]{2,1,0:T(8,128)(2,1)S(1)}, u32[]{:S(2)}, u32[]{:S(2)}) collective-permute-start(bf16[4,64,256]{2,1,0:T(8,128)(2,1)S(1)} %get-tuple-element.19), channel_id=1, source_target_pairs={{0,8},{4,12},{8,0},{12,4},{1,9},{5,13},{9,1},{13,5},{2,10},{6,14},... | collective-permute-start | bytes 393224 | tf_op jit(solution)/shard_map/ppermute | solution.py:15
  77.5 5.4 %collective-permute-done.33 = bf16[256,384]{1,0:T(8,128)(2,1)S(1)} collective-permute-done((bf16[256,384]{1,0:T(8,128)(2,1)S(1)}, bf16[256,384]{1,0:T(8,128)(2,1)S(1)}, u32[]{:S(2)}, u32[]{:S(2)}) %collective-permute-start.33) | collective-permute-done | bytes 196640 | tf_op jit(solution)/shard_map/ppermute | solution.py:108
  82.9 2.1 %collective-permute-start.15 = (bf16[256,256]{1,0:T(8,128)(2,1)S(1)}, bf16[256,256]{1,0:T(8,128)(2,1)S(1)}, u32[]{:S(2)}, u32[]{:S(2)}) collective-permute-start(bf16[256,256]{1,0:T(8,128)(2,1)S(1)} %bitcast.107), channel_id=1, source_target_pairs={{0,4},{4,0},{8,12},{12,8},{1,5},{5,1},{9,13},{13,9},{2,6},{6,2},{1... | collective-permute-start | bytes 393224 | tf_op jit(solution)/shard_map/ppermute | solution.py:15
  85.0 2.1 %collective-permute-start.36 = (bf16[256,384]{1,0:T(8,128)(2,1)S(1)}, bf16[256,384]{1,0:T(8,128)(2,1)S(1)}, u32[]{:S(2)}, u32[]{:S(2)}) collective-permute-start(bf16[256,384]{1,0:T(8,128)(2,1)S(1)} %bitcast.103), channel_id=1, source_target_pairs={{0,4},{4,0},{8,12},{12,8},{1,5},{5,1},{9,13},{13,9},{2,6},{6,2},{1... | collective-permute-start | bytes 589832 | tf_op jit(solution)/shard_map/ppermute | solution.py:15
  87.1 2.3 %collective-permute-done.11 = bf16[4,64,256]{2,1,0:T(8,128)(2,1)S(1)} collective-permute-done((bf16[4,64,256]{2,1,0:T(8,128)(2,1)S(1)}, bf16[4,64,256]{2,1,0:T(8,128)(2,1)S(1)}, u32[]{:S(2)}, u32[]{:S(2)}) %collective-permute-start.11) | collective-permute-done | bytes 131104 | tf_op jit(solution)/shard_map/ppermute | solution.py:15
  90.0 2.7 %collective-permute-done.10 = bf16[4,64,256]{2,1,0:T(8,128)(2,1)S(1)} collective-permute-done((bf16[4,64,256]{2,1,0:T(8,128)(2,1)S(1)}, bf16[4,64,256]{2,1,0:T(8,128)(2,1)S(1)}, u32[]{:S(2)}, u32[]{:S(2)}) %collective-permute-start.10) | collective-permute-done | bytes 131104 | tf_op jit(solution)/shard_map/ppermute | solution.py:15
  92.7 1.3 collective-permute-start.26
  94.2 2.7 %collective-permute-start.29 = (bf16[256,384]{1,0:T(8,128)(2,1)S(1)}, bf16[256,384]{1,0:T(8,128)(2,1)S(1)}, u32[]{:S(2)}, u32[]{:S(2)}) collective-permute-start(bf16[256,384]{1,0:T(8,128)(2,1)S(1)} %bitcast.95), channel_id=1, source_target_pairs={{0,4},{4,0},{8,12},{12,8},{1,5},{5,1},{9,13},{13,9},{2,6},{6,2},{1... | collective-permute-start | bytes 589832 | tf_op jit(solution)/shard_map/ppermute | solution.py:15
  96.9 7.0 %collective-permute-done.26 = bf16[256,384]{1,0:T(8,128)(2,1)S(1)} collective-permute-done((bf16[256,384]{1,0:T(8,128)(2,1)S(1)}, bf16[256,384]{1,0:T(8,128)(2,1)S(1)}, u32[]{:S(2)}, u32[]{:S(2)}) %collective-permute-start.26) | collective-permute-done | bytes 196640 | tf_op jit(solution)/shard_map/ppermute | solution.py:108
  103.9 1.3 collective-permute-start.25
  105.2 6.4 %collective-permute-done.25 = bf16[256,384]{1,0:T(8,128)(2,1)S(1)} collective-permute-done((bf16[256,384]{1,0:T(8,128)(2,1)S(1)}, bf16[256,384]{1,0:T(8,128)(2,1)S(1)}, u32[]{:S(2)}, u32[]{:S(2)}) %collective-permute-start.25) | collective-permute-done | bytes 196640 | tf_op jit(solution)/shard_map/ppermute | solution.py:107
  112.2 1.0 fusion.28
  114.8 1.5 collective-permute-start.20
  116.2 1.0 fusion.20
  118.0 1.0 fusion.12
  119.1 1.5 collective-permute-start.27
  120.6 10.4 %collective-permute-done.20 = bf16[512,256]{0,1:T(8,128)(2,1)S(1)} collective-permute-done((bf16[512,256]{0,1:T(8,128)(2,1)S(1)}, bf16[512,256]{0,1:T(8,128)(2,1)S(1)}, u32[]{:S(2)}, u32[]{:S(2)}) %collective-permute-start.20) | collective-permute-done | bytes 262176 | tf_op jit(solution)/shard_map/ppermute | solution.py:15
  131.2 8.2 %collective-permute-done.34 = bf16[512,384]{0,1:T(8,128)(2,1)S(1)} collective-permute-done((bf16[512,384]{0,1:T(8,128)(2,1)S(1)}, bf16[512,384]{0,1:T(8,128)(2,1)S(1)}, u32[]{:S(2)}, u32[]{:S(2)}) %collective-permute-start.34) | collective-permute-done | bytes 393248 | tf_op jit(solution)/shard_map/ppermute | solution.py:15
  139.6 5.4 %collective-permute-done.27 = bf16[512,384]{0,1:T(8,128)(2,1)S(1)} collective-permute-done((bf16[512,384]{0,1:T(8,128)(2,1)S(1)}, bf16[512,384]{0,1:T(8,128)(2,1)S(1)}, u32[]{:S(2)}, u32[]{:S(2)}) %collective-permute-start.27) | collective-permute-done | bytes 393248 | tf_op jit(solution)/shard_map/ppermute | solution.py:15
  145.2 1.5 %copy.14 = bf16[1,512,1408]{2,1,0:T(8,128)(2,1)} copy(bf16[1,512,1408]{1,2,0:T(8,128)(2,1)S(1)} %maximum_bitcast_fusion) | data formatting | bytes 2883584 | tf_op jit(solution)/shard_map/broadcast_in_dim | solution.py:153
  (107 shorter events, 14.8 us)
Async XLA Ops:
  0.0 30.4 %copy-start = (bf16[1,1,4,128,1408]{4,3,2,1,0:T(8,128)(2,1)S(1)}, bf16[1,1,4,128,1408]{4,3,2,1,0:T(8,128)(2,1)}, u32[]{:S(2)}) copy-start(bf16[1,1,4,128,1408]{4,3,2,1,0:T(8,128)(2,1)} %param.7) | copy-start | bytes 4325380
  2.0 10.2 %collective-permute-start.2 = (f32[8,128]{1,0:T(8,128)S(1)}, f32[8,128]{1,0:T(8,128)S(1)}, u32[]{:S(2)}, u32[]{:S(2)}) collective-permute-start(f32[8,128]{1,0:T(8,128)S(1)} %iota.95), channel_id=1, source_target_pairs={{0,3},{1,2},{2,1},{3,0},{4,7},{5,6},{6,5},{7,4},{8,11},{9,10},{10,... | collective-permute-start | bytes 12296 | tf_op jit(solution)/shard_map/ppermute | solution.py:15
  4.5 7.7 %collective-permute-start.1 = (f32[8,128]{1,0:T(8,128)S(1)}, f32[8,128]{1,0:T(8,128)S(1)}, u32[]{:S(2)}, u32[]{:S(2)}) collective-permute-start(f32[8,128]{1,0:T(8,128)S(1)} %iota.95), channel_id=1, source_target_pairs={{0,2},{1,3},{2,0},{3,1},{4,6},{5,7},{6,4},{7,5},{8,10},{9,11},{10,... | collective-permute-start | bytes 12296 | tf_op jit(solution)/shard_map/ppermute | solution.py:15
  5.1 7.1 %collective-permute-start = (f32[8,128]{1,0:T(8,128)S(1)}, f32[8,128]{1,0:T(8,128)S(1)}, u32[]{:S(2)}, u32[]{:S(2)}) collective-permute-start(f32[8,128]{1,0:T(8,128)S(1)} %iota.95), channel_id=1, source_target_pairs={{0,1},{1,0},{2,3},{3,2},{4,5},{5,4},{6,7},{7,6},{8,9},{9,8},{10,11... | collective-permute-start | bytes 12296 | tf_op jit(solution)/shard_map/ppermute | solution.py:15
  6.4 25.8 %collective-permute-start.35 = (bf16[4,64,384]{2,1,0:T(8,128)(2,1)S(1)}, bf16[4,64,384]{2,1,0:T(8,128)(2,1)S(1)}, u32[]{:S(2)}, u32[]{:S(2)}) collective-permute-start(bf16[4,64,384]{2,1,0:T(8,128)(2,1)S(1)} %get-tuple-element.11), channel_id=1, source_target_pairs={{0,2},{1,3},{2,0},{3,1},{4,6},{5,7},{6,4},{7,5},{8,10},{9,11},{10,... | collective-permute-start | bytes 589832 | tf_op jit(solution)/shard_map/ppermute | solution.py:15
  8.2 52.7 %collective-permute-start.6 = (bf16[1,128,2048]{2,1,0:T(8,128)(2,1)}, bf16[1,128,2048]{2,1,0:T(8,128)(2,1)S(1)}, u32[]{:S(2)}, u32[]{:S(2)}) collective-permute-start(bf16[1,128,2048]{2,1,0:T(8,128)(2,1)} %param.4), channel_id=1, source_target_pairs={{0,16},{16,0},{1,17},{17,1},{2,18},{18,2},{3,19},{19,3},{4,20},{20... | collective-permute-start | bytes 1572872 | tf_op jit(solution)/shard_map/ppermute | solution.py:10
  12.1 48.7 %copy-start.3 = (f32[1,128]{1,0:T(1,128)S(1)}, f32[1,128]{1,0:T(1,128)}, u32[]{:S(2)}) copy-start(f32[1,128]{1,0:T(1,128)} %param.5) | copy-start | bytes 1540
  12.2 5.5 %collective-permute-start.5 = (f32[8,128]{1,0:T(8,128)S(1)}, f32[8,128]{1,0:T(8,128)S(1)}, u32[]{:S(2)}, u32[]{:S(2)}) collective-permute-start(f32[8,128]{1,0:T(8,128)S(1)} %add_add_fusion.1), channel_id=1, source_target_pairs={{0,12},{4,8},{8,4},{12,0},{1,13},{5,9},{9,5},{13,1},{2,14},{6,10},... | collective-permute-start | bytes 12296 | tf_op jit(solution)/shard_map/ppermute | solution.py:15
  15.9 4.5 %collective-permute-start.4 = (f32[8,128]{1,0:T(8,128)S(1)}, f32[8,128]{1,0:T(8,128)S(1)}, u32[]{:S(2)}, u32[]{:S(2)}) collective-permute-start(f32[8,128]{1,0:T(8,128)S(1)} %add_add_fusion.1), channel_id=1, source_target_pairs={{0,8},{4,12},{8,0},{12,4},{1,9},{5,13},{9,1},{13,5},{2,10},{6,14},... | collective-permute-start | bytes 12296 | tf_op jit(solution)/shard_map/ppermute | solution.py:15
  15.9 5.0 %collective-permute-start.3 = (f32[8,128]{1,0:T(8,128)S(1)}, f32[8,128]{1,0:T(8,128)S(1)}, u32[]{:S(2)}, u32[]{:S(2)}) collective-permute-start(f32[8,128]{1,0:T(8,128)S(1)} %add_add_fusion.1), channel_id=1, source_target_pairs={{0,4},{4,0},{8,12},{12,8},{1,5},{5,1},{9,13},{13,9},{2,6},{6,2},{1... | collective-permute-start | bytes 12296 | tf_op jit(solution)/shard_map/ppermute | solution.py:15
  17.8 19.7 %collective-permute-start.28 = (bf16[4,64,384]{2,1,0:T(8,128)(2,1)S(1)}, bf16[4,64,384]{2,1,0:T(8,128)(2,1)S(1)}, u32[]{:S(2)}, u32[]{:S(2)}) collective-permute-start(bf16[4,64,384]{2,1,0:T(8,128)(2,1)S(1)} %get-tuple-element.12), channel_id=1, source_target_pairs={{0,2},{1,3},{2,0},{3,1},{4,6},{5,7},{6,4},{7,5},{8,10},{9,11},{10,... | collective-permute-start | bytes 589832 | tf_op jit(solution)/shard_map/ppermute | solution.py:15
  20.4 17.9 %collective-permute-start.21 = (bf16[4,64,384]{2,1,0:T(8,128)(2,1)S(1)}, bf16[4,64,384]{2,1,0:T(8,128)(2,1)S(1)}, u32[]{:S(2)}, u32[]{:S(2)}) collective-permute-start(bf16[4,64,384]{2,1,0:T(8,128)(2,1)S(1)} %get-tuple-element.10), channel_id=1, source_target_pairs={{0,2},{1,3},{2,0},{3,1},{4,6},{5,7},{6,4},{7,5},{8,10},{9,11},{10,... | collective-permute-start | bytes 589832 | tf_op jit(solution)/shard_map/ppermute | solution.py:15
  21.0 9.4 %collective-permute-start.14 = (bf16[4,64,256]{2,1,0:T(8,128)(2,1)S(1)}, bf16[4,64,256]{2,1,0:T(8,128)(2,1)}, u32[]{:S(2)}, u32[]{:S(2)}) collective-permute-start(bf16[4,64,256]{2,1,0:T(8,128)(2,1)S(1)} %slice.91), channel_id=1, source_target_pairs={{0,2},{1,3},{2,0},{3,1},{4,6},{5,7},{6,4},{7,5},{8,10},{9,11},{10,... | collective-permute-start | bytes 393224 | tf_op jit(solution)/shard_map/ppermute | solution.py:15
  31.4 12.5 %collective-permute-start.17 = (bf16[256,256]{1,0:T(8,128)(2,1)S(1)}, bf16[256,256]{1,0:T(8,128)(2,1)S(1)}, u32[]{:S(2)}, u32[]{:S(2)}) collective-permute-start(bf16[256,256]{1,0:T(8,128)(2,1)S(1)} %bitcast.105), channel_id=1, source_target_pairs={{4,8},{8,4},{5,9},{9,5},{6,10},{10,6},{7,11},{11,7},{20,24},{24,20... | collective-permute-start | bytes 393224 | tf_op jit(solution)/shard_map/ppermute | solution.py:105
  32.1 10.3 %collective-permute-start.16 = (bf16[256,256]{1,0:T(8,128)(2,1)S(1)}, bf16[256,256]{1,0:T(8,128)(2,1)S(1)}, u32[]{:S(2)}, u32[]{:S(2)}) collective-permute-start(bf16[256,256]{1,0:T(8,128)(2,1)S(1)} %bitcast.106), channel_id=1, source_target_pairs={{0,8},{12,4},{1,9},{13,5},{2,10},{14,6},{3,11},{15,7},{16,24},{28,... | collective-permute-start | bytes 393224 | tf_op jit(solution)/shard_map/ppermute | solution.py:106
  37.5 22.1 %collective-permute-start.38 = (bf16[256,384]{1,0:T(8,128)(2,1)S(1)}, bf16[256,384]{1,0:T(8,128)(2,1)S(1)}, u32[]{:S(2)}, u32[]{:S(2)}) collective-permute-start(bf16[256,384]{1,0:T(8,128)(2,1)S(1)} %bitcast.101), channel_id=1, source_target_pairs={{4,8},{8,4},{5,9},{9,5},{6,10},{10,6},{7,11},{11,7},{20,24},{24,20... | collective-permute-start | bytes 589832 | tf_op jit(solution)/shard_map/ppermute | solution.py:105
  38.4 19.9 %collective-permute-start.37 = (bf16[256,384]{1,0:T(8,128)(2,1)S(1)}, bf16[256,384]{1,0:T(8,128)(2,1)S(1)}, u32[]{:S(2)}, u32[]{:S(2)}) collective-permute-start(bf16[256,384]{1,0:T(8,128)(2,1)S(1)} %bitcast.102), channel_id=1, source_target_pairs={{0,8},{12,4},{1,9},{13,5},{2,10},{14,6},{3,11},{15,7},{16,24},{28,... | collective-permute-start | bytes 589832 | tf_op jit(solution)/shard_map/ppermute | solution.py:106
  42.4 6.9 %collective-permute-start.19 = (bf16[256,256]{1,0:T(8,128)(2,1)S(1)}, bf16[256,256]{1,0:T(8,128)(2,1)S(1)}, u32[]{:S(2)}, u32[]{:S(2)}) collective-permute-start(bf16[256,256]{1,0:T(8,128)(2,1)S(1)} %collective-permute-done.16), channel_id=1, source_target_pairs={{8,12},{4,0},{9,13},{5,1},{10,14},{6,2},{11,15},{7,3},{24,28},{20,... | collective-permute-start | bytes 393224 | tf_op jit(solution)/shard_map/ppermute | solution.py:108
  43.9 24.0 %collective-permute-start.31 = (bf16[256,384]{1,0:T(8,128)(2,1)S(1)}, bf16[256,384]{1,0:T(8,128)(2,1)S(1)}, u32[]{:S(2)}, u32[]{:S(2)}) collective-permute-start(bf16[256,384]{1,0:T(8,128)(2,1)S(1)} %bitcast.93), channel_id=1, source_target_pairs={{4,8},{8,4},{5,9},{9,5},{6,10},{10,6},{7,11},{11,7},{20,24},{24,20... | collective-permute-start | bytes 589832 | tf_op jit(solution)/shard_map/ppermute | solution.py:105
  49.3 6.8 %collective-permute-start.18 = (bf16[256,256]{1,0:T(8,128)(2,1)S(1)}, bf16[256,256]{1,0:T(8,128)(2,1)S(1)}, u32[]{:S(2)}, u32[]{:S(2)}) collective-permute-start(bf16[256,256]{1,0:T(8,128)(2,1)S(1)} %collective-permute-done.17), channel_id=1, source_target_pairs={{8,12},{4,0},{9,13},{5,1},{10,14},{6,2},{11,15},{7,3},{24,28},{20,... | collective-permute-start | bytes 393224 | tf_op jit(solution)/shard_map/ppermute | solution.py:107
  56.1 14.2 %collective-permute-start.30 = (bf16[256,384]{1,0:T(8,128)(2,1)S(1)}, bf16[256,384]{1,0:T(8,128)(2,1)S(1)}, u32[]{:S(2)}, u32[]{:S(2)}) collective-permute-start(bf16[256,384]{1,0:T(8,128)(2,1)S(1)} %bitcast.94), channel_id=1, source_target_pairs={{0,8},{12,4},{1,9},{13,5},{2,10},{14,6},{3,11},{15,7},{16,24},{28,... | collective-permute-start | bytes 589832 | tf_op jit(solution)/shard_map/ppermute | solution.py:106
  58.2 7.6 %collective-permute-start.40 = (bf16[256,384]{1,0:T(8,128)(2,1)S(1)}, bf16[256,384]{1,0:T(8,128)(2,1)S(1)}, u32[]{:S(2)}, u32[]{:S(2)}) collective-permute-start(bf16[256,384]{1,0:T(8,128)(2,1)S(1)} %collective-permute-done.37), channel_id=1, source_target_pairs={{8,12},{4,0},{9,13},{5,1},{10,14},{6,2},{11,15},{7,3},{24,28},{20,... | collective-permute-start | bytes 589832 | tf_op jit(solution)/shard_map/ppermute | solution.py:108
  59.5 8.4 %collective-permute-start.39 = (bf16[256,384]{1,0:T(8,128)(2,1)S(1)}, bf16[256,384]{1,0:T(8,128)(2,1)S(1)}, u32[]{:S(2)}, u32[]{:S(2)}) collective-permute-start(bf16[256,384]{1,0:T(8,128)(2,1)S(1)} %collective-permute-done.38), channel_id=1, source_target_pairs={{8,12},{4,0},{9,13},{5,1},{10,14},{6,2},{11,15},{7,3},{24,28},{20,... | collective-permute-start | bytes 589832 | tf_op jit(solution)/shard_map/ppermute | solution.py:107
  61.8 9.9 %collective-permute-start.9 = (bf16[4,64,256]{2,1,0:T(8,128)(2,1)S(1)}, bf16[4,64,256]{2,1,0:T(8,128)(2,1)S(1)}, u32[]{:S(2)}, u32[]{:S(2)}) collective-permute-start(bf16[4,64,256]{2,1,0:T(8,128)(2,1)S(1)} %get-tuple-element.26), channel_id=1, source_target_pairs={{0,3},{1,2},{2,1},{3,0},{4,7},{5,6},{6,5},{7,4},{8,11},{9,10},{10,... | collective-permute-start | bytes 393224 | tf_op jit(solution)/shard_map/ppermute | solution.py:15
  65.8 7.2 %collective-permute-start.8 = (bf16[4,64,256]{2,1,0:T(8,128)(2,1)S(1)}, bf16[4,64,256]{2,1,0:T(8,128)(2,1)S(1)}, u32[]{:S(2)}, u32[]{:S(2)}) collective-permute-start(bf16[4,64,256]{2,1,0:T(8,128)(2,1)S(1)} %get-tuple-element.27), channel_id=1, source_target_pairs={{0,2},{1,3},{2,0},{3,1},{4,6},{5,7},{6,4},{7,5},{8,10},{9,11},{10,... | collective-permute-start | bytes 393224 | tf_op jit(solution)/shard_map/ppermute | solution.py:15
  67.9 5.1 %collective-permute-start.7 = (bf16[4,64,256]{2,1,0:T(8,128)(2,1)S(1)}, bf16[4,64,256]{2,1,0:T(8,128)(2,1)S(1)}, u32[]{:S(2)}, u32[]{:S(2)}) collective-permute-start(bf16[4,64,256]{2,1,0:T(8,128)(2,1)S(1)} %get-tuple-element.28), channel_id=1, source_target_pairs={{0,1},{1,0},{2,3},{3,2},{4,5},{5,4},{6,7},{7,6},{8,9},{9,8},{10,11... | collective-permute-start | bytes 393224 | tf_op jit(solution)/shard_map/ppermute | solution.py:15
  67.9 14.9 %collective-permute-start.23 = (bf16[256,384]{1,0:T(8,128)(2,1)S(1)}, bf16[256,384]{1,0:T(8,128)(2,1)S(1)}, u32[]{:S(2)}, u32[]{:S(2)}) collective-permute-start(bf16[256,384]{1,0:T(8,128)(2,1)S(1)} %bitcast.97), channel_id=1, source_target_pairs={{0,8},{12,4},{1,9},{13,5},{2,10},{14,6},{3,11},{15,7},{16,24},{28,... | collective-permute-start | bytes 589832 | tf_op jit(solution)/shard_map/ppermute | solution.py:106
  70.4 12.4 %collective-permute-start.33 = (bf16[256,384]{1,0:T(8,128)(2,1)S(1)}, bf16[256,384]{1,0:T(8,128)(2,1)S(1)}, u32[]{:S(2)}, u32[]{:S(2)}) collective-permute-start(bf16[256,384]{1,0:T(8,128)(2,1)S(1)} %collective-permute-done.30), channel_id=1, source_target_pairs={{8,12},{4,0},{9,13},{5,1},{10,14},{6,2},{11,15},{7,3},{24,28},{20,... | collective-permute-start | bytes 589832 | tf_op jit(solution)/shard_map/ppermute | solution.py:108
  71.7 22.3 %collective-permute-start.32 = (bf16[256,384]{1,0:T(8,128)(2,1)S(1)}, bf16[256,384]{1,0:T(8,128)(2,1)S(1)}, u32[]{:S(2)}, u32[]{:S(2)}) collective-permute-start(bf16[256,384]{1,0:T(8,128)(2,1)S(1)} %collective-permute-done.31), channel_id=1, source_target_pairs={{8,12},{4,0},{9,13},{5,1},{10,14},{6,2},{11,15},{7,3},{24,28},{20,... | collective-permute-start | bytes 589832 | tf_op jit(solution)/shard_map/ppermute | solution.py:107
  73.3 11.7 %collective-permute-start.12 = (bf16[4,64,256]{2,1,0:T(8,128)(2,1)S(1)}, bf16[4,64,256]{2,1,0:T(8,128)(2,1)S(1)}, u32[]{:S(2)}, u32[]{:S(2)}) collective-permute-start(bf16[4,64,256]{2,1,0:T(8,128)(2,1)S(1)} %get-tuple-element.18), channel_id=1, source_target_pairs={{0,12},{4,8},{8,4},{12,0},{1,13},{5,9},{9,5},{13,1},{2,14},{6,10},... | collective-permute-start | bytes 393224 | tf_op jit(solution)/shard_map/ppermute | solution.py:15
  74.8 14.6 %collective-permute-start.11 = (bf16[4,64,256]{2,1,0:T(8,128)(2,1)S(1)}, bf16[4,64,256]{2,1,0:T(8,128)(2,1)S(1)}, u32[]{:S(2)}, u32[]{:S(2)}) collective-permute-start(bf16[4,64,256]{2,1,0:T(8,128)(2,1)S(1)} %get-tuple-element.19), channel_id=1, source_target_pairs={{0,8},{4,12},{8,0},{12,4},{1,9},{5,13},{9,1},{13,5},{2,10},{6,14},... | collective-permute-start | bytes 393224 | tf_op jit(solution)/shard_map/ppermute | solution.py:15
  82.8 9.8 %collective-permute-start.10 = (bf16[4,64,256]{2,1,0:T(8,128)(2,1)S(1)}, bf16[4,64,256]{2,1,0:T(8,128)(2,1)S(1)}, u32[]{:S(2)}, u32[]{:S(2)}) collective-permute-start(bf16[4,64,256]{2,1,0:T(8,128)(2,1)S(1)} %get-tuple-element.20), channel_id=1, source_target_pairs={{0,4},{4,0},{8,12},{12,8},{1,5},{5,1},{9,13},{13,9},{2,6},{6,2},{1... | collective-permute-start | bytes 393224 | tf_op jit(solution)/shard_map/ppermute | solution.py:15
  82.9 31.1 %collective-permute-start.15 = (bf16[256,256]{1,0:T(8,128)(2,1)S(1)}, bf16[256,256]{1,0:T(8,128)(2,1)S(1)}, u32[]{:S(2)}, u32[]{:S(2)}) collective-permute-start(bf16[256,256]{1,0:T(8,128)(2,1)S(1)} %bitcast.107), channel_id=1, source_target_pairs={{0,4},{4,0},{8,12},{12,8},{1,5},{5,1},{9,13},{13,9},{2,6},{6,2},{1... | collective-permute-start | bytes 393224 | tf_op jit(solution)/shard_map/ppermute | solution.py:15
  85.0 27.2 %collective-permute-start.36 = (bf16[256,384]{1,0:T(8,128)(2,1)S(1)}, bf16[256,384]{1,0:T(8,128)(2,1)S(1)}, u32[]{:S(2)}, u32[]{:S(2)}) collective-permute-start(bf16[256,384]{1,0:T(8,128)(2,1)S(1)} %bitcast.103), channel_id=1, source_target_pairs={{0,4},{4,0},{8,12},{12,8},{1,5},{5,1},{9,13},{13,9},{2,6},{6,2},{1... | collective-permute-start | bytes 589832 | tf_op jit(solution)/shard_map/ppermute | solution.py:15
  89.3 4.8 %collective-permute-start.24 = (bf16[256,384]{1,0:T(8,128)(2,1)S(1)}, bf16[256,384]{1,0:T(8,128)(2,1)S(1)}, u32[]{:S(2)}, u32[]{:S(2)}) collective-permute-start(bf16[256,384]{1,0:T(8,128)(2,1)S(1)} %bitcast.98), channel_id=1, source_target_pairs={{4,8},{8,4},{5,9},{9,5},{6,10},{10,6},{7,11},{11,7},{20,24},{24,20... | collective-permute-start | bytes 589832 | tf_op jit(solution)/shard_map/ppermute | solution.py:105
  92.7 11.2 %collective-permute-start.26 = (bf16[256,384]{1,0:T(8,128)(2,1)S(1)}, bf16[256,384]{1,0:T(8,128)(2,1)S(1)}, u32[]{:S(2)}, u32[]{:S(2)}) collective-permute-start(bf16[256,384]{1,0:T(8,128)(2,1)S(1)} %collective-permute-done.23), channel_id=1, source_target_pairs={{8,12},{4,0},{9,13},{5,1},{10,14},{6,2},{11,15},{7,3},{24,28},{20,... | collective-permute-start | bytes 589832 | tf_op jit(solution)/shard_map/ppermute | solution.py:108
  94.0 17.6 %collective-permute-start.13 = (bf16[4,4,64,256]{3,2,1,0:T(8,128)(2,1)S(1)}, bf16[4,4,64,256]{3,2,1,0:T(8,128)(2,1)S(1)}, u32[]{:S(2)}, u32[]{:S(2)}) collective-permute-start(bf16[4,4,64,256]{3,2,1,0:T(8,128)(2,1)S(1)} %pad_maximum_fusion.4), channel_id=1, source_target_pairs={{0,1},{1,0},{2,3},{3,2},{4,5},{5,4},{6,7},{7,6},{8,9},{9,8},{10,11... | collective-permute-start | bytes 1572872 | tf_op jit(solution)/shard_map/ppermute | solution.py:15
  94.2 22.1 %collective-permute-start.29 = (bf16[256,384]{1,0:T(8,128)(2,1)S(1)}, bf16[256,384]{1,0:T(8,128)(2,1)S(1)}, u32[]{:S(2)}, u32[]{:S(2)}) collective-permute-start(bf16[256,384]{1,0:T(8,128)(2,1)S(1)} %bitcast.95), channel_id=1, source_target_pairs={{0,4},{4,0},{8,12},{12,8},{1,5},{5,1},{9,13},{13,9},{2,6},{6,2},{1... | collective-permute-start | bytes 589832 | tf_op jit(solution)/shard_map/ppermute | solution.py:15
  103.9 7.7 %collective-permute-start.25 = (bf16[256,384]{1,0:T(8,128)(2,1)S(1)}, bf16[256,384]{1,0:T(8,128)(2,1)S(1)}, u32[]{:S(2)}, u32[]{:S(2)}) collective-permute-start(bf16[256,384]{1,0:T(8,128)(2,1)S(1)} %collective-permute-done.24), channel_id=1, source_target_pairs={{8,12},{4,0},{9,13},{5,1},{10,14},{6,2},{11,15},{7,3},{24,28},{20,... | collective-permute-start | bytes 589832 | tf_op jit(solution)/shard_map/ppermute | solution.py:107
  111.6 6.4 %collective-permute-start.22 = (bf16[256,384]{1,0:T(8,128)(2,1)S(1)}, bf16[256,384]{1,0:T(8,128)(2,1)S(1)}, u32[]{:S(2)}, u32[]{:S(2)}) collective-permute-start(bf16[256,384]{1,0:T(8,128)(2,1)S(1)} %bitcast.99), channel_id=1, source_target_pairs={{0,4},{4,0},{8,12},{12,8},{1,5},{5,1},{9,13},{13,9},{2,6},{6,2},{1... | collective-permute-start | bytes 589832 | tf_op jit(solution)/shard_map/ppermute | solution.py:15
  112.2 1.8 %copy-start.1 = (bf16[256,256]{1,0:T(8,128)(2,1)S(1)}, bf16[256,256]{1,0:T(8,128)(2,1)}, u32[]{:S(2)}) copy-start(bf16[256,256]{1,0:T(8,128)(2,1)} %broadcast_select_fusion.10) | copy-start | bytes 393220
  112.2 1.8 %copy-start.2 = (bf16[256,256]{1,0:T(8,128)(2,1)S(1)}, bf16[256,256]{1,0:T(8,128)(2,1)}, u32[]{:S(2)}) copy-start(bf16[256,256]{1,0:T(8,128)(2,1)} %broadcast_select_fusion.11) | copy-start | bytes 393220
  113.3 17.8 %collective-permute-start.41 = (bf16[512,384]{0,1:T(8,128)(2,1)S(1)}, bf16[512,384]{0,1:T(8,128)(2,1)S(1)}, u32[]{:S(2)}, u32[]{:S(2)}) collective-permute-start(bf16[512,384]{0,1:T(8,128)(2,1)S(1)} %slice.128), channel_id=1, source_target_pairs={{0,2},{1,3},{2,0},{3,1},{4,6},{5,7},{6,4},{7,5},{8,10},{9,11},{10,... | collective-permute-start | bytes 1179656 | tf_op jit(solution)/shard_map/ppermute | solution.py:15
  114.8 16.2 %collective-permute-start.20 = (bf16[512,256]{0,1:T(8,128)(2,1)S(1)}, bf16[512,256]{0,1:T(8,128)(2,1)S(1)}, u32[]{:S(2)}, u32[]{:S(2)}) collective-permute-start(bf16[512,256]{0,1:T(8,128)(2,1)S(1)} %slice.131), channel_id=1, source_target_pairs={{0,2},{1,3},{2,0},{3,1},{4,6},{5,7},{6,4},{7,5},{8,10},{9,11},{10,... | collective-permute-start | bytes 786440 | tf_op jit(solution)/shard_map/ppermute | solution.py:15
  117.3 22.1 %collective-permute-start.34 = (bf16[512,384]{0,1:T(8,128)(2,1)S(1)}, bf16[512,384]{0,1:T(8,128)(2,1)S(1)}, u32[]{:S(2)}, u32[]{:S(2)}) collective-permute-start(bf16[512,384]{0,1:T(8,128)(2,1)S(1)} %slice.129), channel_id=1, source_target_pairs={{0,2},{1,3},{2,0},{3,1},{4,6},{5,7},{6,4},{7,5},{8,10},{9,11},{10,... | collective-permute-start | bytes 1179656 | tf_op jit(solution)/shard_map/ppermute | solution.py:15
  119.1 25.8 %collective-permute-start.27 = (bf16[512,384]{0,1:T(8,128)(2,1)S(1)}, bf16[512,384]{0,1:T(8,128)(2,1)S(1)}, u32[]{:S(2)}, u32[]{:S(2)}) collective-permute-start(bf16[512,384]{0,1:T(8,128)(2,1)S(1)} %slice.130), channel_id=1, source_target_pairs={{0,2},{1,3},{2,0},{3,1},{4,6},{5,7},{6,4},{7,5},{8,10},{9,11},{10,... | collective-permute-start | bytes 1179656 | tf_op jit(solution)/shard_map/ppermute | solution.py:15

commit v2 on v0

--- a/solution.py
+++ b/solution.py
@@ -3,6 +3,31 @@
 from jax import lax
 from jax.sharding import PartitionSpec as P
 
+CUTS = (2, 3, 3, 3)
+GROUPS = (1, 1, 1, 1)
+ORDER = {
+    "F2": ("F0",),
+    "F3": ("F1",),
+    "M2": ("M0",),
+    "M3": ("M2",),
+    "N1": ("G", "H"),
+    "N2": ("G", "H"),
+    "N3": ("G", "H"),
+    "P1": ("A1",),
+    "S1": ("sent",),
+    "S2": ("X",),
+    "S3": ("X",),
+    "T0": ("upper0",),
+    "T1": ("T0", "sent", "upper1"),
+    "T2": ("own0",),
+    "T3": ("share1", "share2", "share3"),
+    "couple0": ("T3",),
+    "own0": ("T1",),
+    "own1": ("T3",),
+    "pair": ("T2",),
+    "scaled": ("T0",),
+}
+
 
 def shifted(value, axis, steps):
     count = lax.axis_size(axis)
@@ -10,13 +35,12 @@
     return lax.ppermute(value, axis, pairs)
 
 
-def swapped(value, axis, apart):
-    mask = 2**apart
+def crossed(value, axis, mask):
     pairs = [(source, source ^ mask) for source in range(lax.axis_size(axis))]
     return lax.ppermute(value, axis, pairs)
 
 
-def body(input_grad, gate_prob, expert_route, saved_hidden):
+def general_body(input_grad, gate_prob, expert_route, saved_hidden):
     grad_rows = shifted(input_grad, "pipe", -1)[0]
     flight_count = lax.axis_size("expert") // 2
     capacity = saved_hidden.shape[3]
@@ -41,7 +65,7 @@
     ).astype(jnp.bfloat16)
     halves = outgoing.reshape(2 * flight_count, capacity // 2, model_width)
     owned_rows = lax.all_to_all(halves, "expert", split_axis=0, concat_axis=0, tiled=True)
-    partner_rows = swapped(owned_rows, "expert", 0)
+    partner_rows = crossed(owned_rows, "expert", 1)
     parity = lax.axis_index("expert") % 2
     first_half = jnp.where(parity == 0, owned_rows, partner_rows)
     second_half = jnp.where(parity == 0, partner_rows, owned_rows)
@@ -60,6 +84,204 @@
     return summed[None]
 
 
+def column_cuts(width, weights):
+    tiles, whole = width // 128, sum(weights)
+    edges = [128 * ((tiles * sum(weights[:part])) // whole) for part in range(len(weights))] + [width]
+    return list(zip(edges[:-1], edges[1:]))
+
+
+def after(value, *others):
+    return lax.optimization_barrier((value, *others))[0]
+
+
+class Plan:
+    def __init__(self, input_grad, gate_prob, expert_route, saved_hidden):
+        self.made = {}
+        self.args = input_grad, gate_prob, expert_route
+        self.replica, self.shard = lax.axis_index("dp"), lax.axis_index("expert")
+        self.replicas, self.shards = lax.axis_size("dp"), lax.axis_size("expert")
+        self.expert, self.core = self.shard // 2, self.shard % 2
+        self.inner = (self.replica == 1) | (self.replica == 2)
+        self.tokens, self.width = input_grad.shape[1:]
+        self.half = self.tokens // 2
+        self.hidden = saved_hidden[0, 0]
+        self.sources, self.hidden_width = self.hidden.shape[0], self.hidden.shape[2]
+        self.rows = self.sources * self.half
+        self.part = self.width // self.replicas
+        self.cuts = column_cuts(self.hidden_width, CUTS)
+        self.groups = [part for part, size in enumerate(GROUPS) for _ in range(size)]
+
+    def __call__(self, name, at=None):
+        key = name if at is None else name + str(at)
+        if key not in self.made:
+            made = getattr(self, name)
+            self.made[key] = made() if at is None else made(at)
+        return self.made[key]
+
+    def free(self, value, key):
+        others = []
+        for other in ORDER.get(key, ()):
+            name = other.rstrip("0123456789")
+            others.append(self(name, int(other[len(name) :])) if name != other else self(name))
+        return after(value, *others) if others else value
+
+    def T(self, step):
+        return self.free(self("T", step - 1) if step else jnp.zeros((8, 128), jnp.float32), "T" + str(step))
+
+    def spans(self, group):
+        parts = [cut for cut, owner in zip(self.cuts, self.groups) if owner == group]
+        return parts[0][0], parts[-1][1]
+
+    def G(self):
+        return shifted(self.free(self.args[1], "G"), "pipe", 1)
+
+    def H(self):
+        return shifted(self.free(self.args[2], "H"), "pipe", 1)
+
+    def P(self, pair):
+        value = jnp.stack([self("Z", 2 * pair) if pair else self("share", 0), self("Z", 2 * pair + 1)])
+        return shifted(self.free(value, "P" + str(pair)), "pipe", -1)
+
+    def picks(self):
+        f32, half, tokens = jnp.float32, self.half, self.tokens
+        routes = self("H")[0, :, 0]
+        index = lax.broadcasted_iota(jnp.int32, (tokens, tokens), 0)
+        other = lax.broadcasted_iota(jnp.int32, (tokens, tokens), 1)
+        earlier = (index < other) & (routes[:, None] == routes[None, :])
+        slot = jnp.sum(earlier.astype(jnp.int32), axis=0)
+        row = lax.broadcasted_iota(jnp.int32, (half, tokens), 0)
+
+        def of(column):
+            place = jnp.where(routes == column, slot, tokens - 1 - slot)
+            return (row == place[None, :]).astype(jnp.bfloat16)
+
+        return of
+
+    def scaled(self):
+        rows, gates = self.free(self.args[0][0], "scaled"), self.free(self("G")[0], "scaled")
+        return (gates[:, None] * rows.astype(jnp.float32)).astype(jnp.bfloat16)
+
+    def kept(self):
+        return jnp.dot(
+            self("picks")(self.expert), self("scaled"), preferred_element_type=jnp.float32
+        ).astype(jnp.bfloat16)
+
+    def sent(self):
+        return jnp.dot(
+            self("picks")(1 - self.expert), self("scaled"), preferred_element_type=jnp.float32
+        ).astype(jnp.bfloat16)
+
+    def X(self):
+        return crossed(self.free(self("sent"), "X"), "expert", 2)
+
+    def pair(self):
+        kept, came, first = self("kept"), self.free(self("X"), "pair"), self.expert == 0
+        return jnp.stack([jnp.where(first, kept, came), jnp.where(first, came, kept)])
+
+    def share(self, mask):
+        return lax.dynamic_slice_in_dim(self("pair"), (self.replica ^ mask) * self.part, self.part, axis=2)
+
+    def Z(self, mask):
+        return crossed(self.free(self("share", mask), "Z" + str(mask)), "dp", mask)
+
+    def K(self, pair):
+        return crossed(self.free(self("P", pair), "K" + str(pair)), "expert", 1)
+
+    def both(self):
+        first, inner = self.core == 0, self.inner
+        grads = []
+        for pair in (0, 1):
+            mine, theirs = self("P", pair), self.free(self("K", pair), "both")
+            grads.append(jnp.stack([jnp.where(first, mine, theirs), jnp.where(first, theirs, mine)], axis=2))
+        grads[1] = jnp.where(inner, grads[1][::-1], grads[1])
+        grads = jnp.concatenate(grads).reshape(self.replicas, self.sources, self.half, self.part)
+        places = jnp.arange(self.half, dtype=jnp.bfloat16)[None, None, :]
+        ours = (places < self("lengths")[:, :, None])[..., None]
+        both = jnp.concatenate([jnp.where(ours, grads, 0), jnp.where(ours, 0, grads)], axis=3)
+        return both.reshape(4 * self.rows, 2 * self.part)
+
+    def N(self, mask):
+        return crossed(self.free(self.args[2], "N" + str(mask)), "expert", mask)
+
+    def counts(self):
+        routes = jnp.stack([self.args[2][0, :, 0]] + [self("N", mask)[0, :, 0] for mask in (1, 2, 3)])
+        zeros = jnp.sum((after(routes) == 0).astype(jnp.float32), axis=1)
+        masks = jnp.arange(self.sources)
+        mine = (self.shard ^ masks)[:, None] == masks[None, :]
+        counts = jnp.sum(jnp.where(mine, zeros[:, None], 0.0), axis=0)
+        return jnp.where(self.expert == 0, counts, self.tokens - counts)
+
+    def upper(self, group):
+        low, high = self.spans(group)
+        return after(self.hidden[:, self.half :, low:high])
+
+    def S(self, group):
+        return crossed(self.free(self("upper", group), "S" + str(group)), "expert", 2)
+
+    def own(self, group):
+        low, high = self.spans(group)
+        spill = self.free(self("S", group), "own" + str(group))
+        places = jnp.arange(self.half)
+        mirror = (places[:, None] + places[None, :] == self.half - 1).astype(jnp.bfloat16)
+        turned = jnp.einsum("cs,isk->ick", mirror, spill, preferred_element_type=jnp.float32)
+        keep = places.astype(jnp.float32)[None, :] < self("counts")[:, None]
+        own = jnp.where(keep[:, :, None], self.hidden[:, : self.half, low:high], turned.astype(jnp.bfloat16))
+        own = own.reshape(self.rows, high - low)
+        if group == 0:
+            label = jnp.repeat(self("counts"), 16 // self.sources)[:, None]
+            own = jnp.concatenate([own, jnp.broadcast_to(label, (16, high)).astype(jnp.bfloat16)], axis=0)
+        return own
+
+    def A(self, group):
+        return crossed(self.free(self("own", group), "A" + str(group)), "dp", 1)
+
+    def cut(self, name, part):
+        group = self.groups[part]
+        start = self.spans(group)[0]
+        low, high = self.cuts[part]
+        return self(name, group)[:, low - start : high - start]
+
+    def couple(self, part):
+        first = self.free(self.cut("A", part), "couple" + str(part))
+        return jnp.concatenate([self.cut("own", part), first], axis=0)
+
+    def M(self, part):
+        return lax.ppermute(self.free(self("couple", part), "M" + str(part)), "dp", [(1, 2), (2, 1)])
+
+    def F(self, part):
+        return lax.ppermute(self.free(self("M", part), "F" + str(part)), "dp", [(2, 3), (1, 0)])
+
+    def block(self, part):
+        far = jnp.where(self.inner, self("M", part), self("F", part))
+        return jnp.concatenate([self.cut("own", part), self.cut("A", part), far], axis=0)
+
+    def lengths(self):
+        return self("block", 0).reshape(4, self.rows + 16, -1)[:, self.rows :: 16 // self.sources, 0]
+
+    def total(self, part):
+        block = self.free(self("block", part), "total" + str(part))
+        if self.groups[part] == 0:
+            block = block.reshape(4, self.rows + 16, -1)[:, : self.rows].reshape(4 * self.rows, -1)
+        return lax.dot_general(
+            self("both"), block, (((0,), (0,)), ((), ())), preferred_element_type=jnp.float32
+        )
+
+    def R(self, part):
+        given = self("total", part)[self.part :].astype(jnp.bfloat16)
+        return crossed(self.free(given, "R" + str(part)), "expert", 2)
+
+    def out(self):
+        out = jnp.zeros((self.part, self.hidden_width), jnp.bfloat16)
+        for part, (low, high) in enumerate(self.cuts):
+            value = self("total", part)[: self.part] + self("R", part).astype(jnp.float32)
+            out = lax.dynamic_update_slice(out, value.astype(jnp.bfloat16), (0, low))
+        return out[None]
+
+
+def pair_body(*args):
+    return Plan(*args)("out")
+
+
 def solution(mesh):
     in_specs = (
         P("pipe", ("dp", "expert"), None),
@@ -68,4 +290,14 @@
         P("pipe", "dp", None, None, "expert"),
     )
     out_specs = P("pipe", "dp", "expert")
-    return jax.shard_map(body, mesh=mesh, in_specs=in_specs, out_specs=out_specs, check_vma=False)
+
+    def run(input_grad, gate_prob, expert_route, saved_hidden):
+        devices = mesh.shape["dp"] * mesh.shape["expert"]
+        tokens = input_grad.shape[1] // devices
+        pairs = mesh.shape["expert"] == 4 and mesh.shape["dp"] == 4
+        body = pair_body if pairs and saved_hidden.shape[3] == tokens else general_body
+        return jax.shard_map(body, mesh=mesh, in_specs=in_specs, out_specs=out_specs, check_vma=False)(
+            input_grad, gate_prob, expert_route, saved_hidden
+        )
+
+    return run

time: 158 us -> 92.9 us (0.59)
  waiting for transfers between devices: 116 us -> 40.7 us
  starting transfers between devices: 2.97 us -> 37.5 us
  blocking collectives: 17.2 us -> 0 us
  between operations: 13.4 us -> 0.54 us
  other arithmetic: 0.98 us -> 4.02 us
  local copies, waits for them, and re-layouts: 0.01 us -> 3 us
    reduce_scatter x1 -> x0, waiting for transfers between devices: 103 us -> none  [body(): lax.psum_scatter(lax.dot_general(flat_rows, hidden, (((0,), (0,)), ((), (...]
    ppermute x1 -> x29, waiting for transfers between devices: 2.66 us -> 40.6 us  [the longest x21 22.3 us: crossed(): return lax.ppermute(value, axis, pairs)]
    ppermute x1 -> x29, starting transfers between devices: 0.01 us -> 31.6 us  [the longest x21 23 us: crossed(): return lax.ppermute(value, axis, pairs)]
    all_to_all x1 -> x0, blocking collectives: 17.2 us -> none  [body(): lax.all_to_all(halves, 'expert', split_axis=0, concat_axis=0, tiled=True)]
    ppermute x1 -> x4, waiting for transfers between devices: 10.5 us -> 0.01 us  [shifted(): return lax.ppermute(value, axis, pairs)]
    ppermute x1 -> x4, starting transfers between devices: 2.97 us -> 5.9 us  [shifted(): return lax.ppermute(value, axis, pairs)]
    slice x0 -> x8, local copies, waits for them, and re-layouts: none -> 2.44 us  [the longest x2 2.21 us: upper(): return after(self.hidden[:, self.half:, low:high])]
    dot_general x3 -> x10, matrix products: 7.39 us -> 6.87 us  [the longest x4 4.61 us: total(): lax.dot_general(self('both'), block, (((0,), (0,)), ((), ())), preferred_...]
  transfers between devices with their start and end apart: 3 -> 33, of which waited for: 3 -> 10; matrix products, arithmetic and copies ran while one was open for 1% -> 14% of each run, Pallas kernels for 0% -> 0%
where the time goes in v2:
time: 92.9 us; the launch traced here: 92.6 us
  waiting for transfers between devices  40.7 us (44%)
  starting transfers between devices  37.5 us (40%)
  matrix products  6.87 us (7%)
  other arithmetic  4.02 us (4%)
  local copies, waits for them, and re-layouts  3 us (3%)
    ppermute x21, starting transfers between devices, crossed(): return lax.ppermute(value, axis, pairs)  23 us
    ppermute x21, waiting for transfers between devices, crossed(): return lax.ppermute(value, axis, pairs)  22.3 us
    ppermute x4, waiting for transfers between devices, F(): lax.ppermute(self.free(self('M', part), 'F' + str(part)), 'dp', [(2, 3),...  18.3 us
    ppermute x4, starting transfers between devices, shifted(): return lax.ppermute(value, axis, pairs)  5.9 us
    ppermute x4, starting transfers between devices, F(): lax.ppermute(self.free(self('M', part), 'F' + str(part)), 'dp', [(2, 3),...  5.14 us
    dot_general x4, matrix products, total(): lax.dot_general(self('both'), block, (((0,), (0,)), ((), ())), preferred_...  4.61 us
    ppermute x4, starting transfers between devices, M(): lax.ppermute(self.free(self('couple', part), 'M' + str(part)), 'dp', [(1,...  3.45 us
    slice x2, local copies, waits for them, and re-layouts, upper(): return after(self.hidden[:, self.half:, low:high])  2.21 us
  transfers between devices with their start and end apart: 33, of which 10 were waited for; matrix products, arithmetic and copies ran while one was open for 14% of the time, Pallas kernels for 0%

profile of v2, /device:TPU:0, one launch (start us, length us, event | category | flops | bytes accessed | tf_op | source)
XLA Modules:
  0.0 92.6 jit_solution(8433447610010737649)
XLA Ops:
  0.0 3.0 %collective-permute-start = (f32[1,128]{1,0:T(1,128)}, f32[1,128]{1,0:T(1,128)S(1)}, u32[]{:S(2)}, u32[]{:S(2)}) collective-permute-start(f32[1,128]{1,0:T(1,128)} %param.5), channel_id=1, source_target_pairs={{0,16},{16,0},{1,17},{17,1},{2,18},{18,2},{3,19},{19,3},{4,20},{20... | collective-permute-start | bytes 1544 | tf_op jit(solution)/shard_map/ppermute | solution.py:35
  3.0 1.0 %slice.77 = bf16[4,64,256]{2,1,0:T(8,128)(2,1)S(1)} slice(bf16[4,128,1408]{2,1,0:T(8,128)(2,1)} %bitcast.81), slice={[0:4], [64:128], [0:256]} | slice | bytes 262144 | tf_op jit(solution)/shard_map/slice | solution.py:216
  4.1 2.0 %collective-permute-start.5 = (bf16[4,64,256]{2,1,0:T(8,128)(2,1)S(1)}, bf16[4,64,256]{2,1,0:T(8,128)(2,1)}, u32[]{:S(2)}, u32[]{:S(2)}) collective-permute-start(bf16[4,64,256]{2,1,0:T(8,128)(2,1)S(1)} %slice.77), channel_id=1, source_target_pairs={{0,2},{1,3},{2,0},{3,1},{4,6},{5,7},{6,4},{7,5},{8,10},{9,11},{10,... | collective-permute-start | bytes 393224 | tf_op jit(solution)/shard_map/ppermute | solution.py:40
  6.1 1.2 %fusion.62 = (bf16[4,64,384]{2,1,0:T(8,128)(2,1)S(1)}, bf16[4,64,384]{2,1,0:T(8,128)(2,1)S(1)}, bf16[4,64,384]{2,1,0:T(8,128)(2,1)S(1)}) fusion(bf16[4,128,1408]{2,1,0:T(8,128)(2,1)} %bitcast.82), kind=kLoop, calls=%fused_computation.122 | loop fusion | bytes 1179648 | tf_op jit(solution)/shard_map/slice | solution.py:216
  7.4 0.8 collective-permute-start.3
  8.2 1.1 %collective-permute-start.2 = (s32[1,128,1]{1,2,0:T(1,128)}, s32[1,128,1]{1,2,0:T(1,128)S(1)}, u32[]{:S(2)}, u32[]{:S(2)}) collective-permute-start(s32[1,128,1]{1,2,0:T(1,128)} %param.6), channel_id=1, source_target_pairs={{0,1},{1,0},{2,3},{3,2},{4,5},{5,4},{6,7},{7,6},{8,9},{9,8},{10,11... | collective-permute-start | bytes 1544 | tf_op jit(solution)/shard_map/ppermute | solution.py:40
  9.7 0.8 collective-permute-start.7
  10.8 1.4 %collective-permute-start.15 = (bf16[4,64,384]{2,1,0:T(8,128)(2,1)S(1)}, bf16[4,64,384]{2,1,0:T(8,128)(2,1)S(1)}, u32[]{:S(2)}, u32[]{:S(2)}) collective-permute-start(bf16[4,64,384]{2,1,0:T(8,128)(2,1)S(1)} %get-tuple-element.34), channel_id=1, source_target_pairs={{0,2},{1,3},{2,0},{3,1},{4,6},{5,7},{6,4},{7,5},{8,10},{9,11},{10,... | collective-permute-start | bytes 589832 | tf_op jit(solution)/shard_map/ppermute | solution.py:40
  12.6 1.1 %fusion.7 = bf16[4,64,256]{2,1,0:T(8,128)(2,1)S(1)} fusion(bf16[4,64,256]{2,1,0:T(8,128)(2,1)} %collective-permute-done.5, bf16[4,128,1408]{2,1,0:T(8,128)(2,1)S(1)} %bitcast.83, pred[4,64]{1,0:T(4,128)(4,1)S(1)} %broadcast_compare_fusion), kind=kOutput, calls=%fused_computation.15 | convolution fusion | flops 8527872 | bytes 393472 | tf_op jit(solution)/shard_map/cs,isk->ick/dot_general | solution.py:226
  13.8 1.6 %collective-permute-start.6 = (bf16[272,256]{1,0:T(8,128)(2,1)S(1)}, bf16[272,256]{1,0:T(8,128)(2,1)S(1)}, u32[]{:S(2)}, u32[]{:S(2)}) collective-permute-start(bf16[272,256]{1,0:T(8,128)(2,1)S(1)} %pad_maximum_fusion.10), channel_id=1, source_target_pairs={{0,4},{4,0},{8,12},{12,8},{1,5},{5,1},{9,13},{13,9},{2,6},{6,2},{1... | collective-permute-start | bytes 417800 | tf_op jit(solution)/shard_map/ppermute | solution.py:40
  15.5 3.5 %collective-permute-done.7 = bf16[64,2048]{1,0:T(8,128)(2,1)S(1)} collective-permute-done((bf16[64,2048]{1,0:T(8,128)(2,1)S(1)}, bf16[64,2048]{1,0:T(8,128)(2,1)S(1)}, u32[]{:S(2)}, u32[]{:S(2)}) %collective-permute-start.7) | collective-permute-done | bytes 262176 | tf_op jit(solution)/shard_map/ppermute | solution.py:40
  19.0 3.7 %collective-permute-start.14 = (bf16[2,64,512]{2,1,0:T(8,128)(2,1)S(1)}, bf16[2,64,512]{2,1,0:T(8,128)(2,1)S(1)}, u32[]{:S(2)}, u32[]{:S(2)}) collective-permute-start(bf16[2,64,512]{2,1,0:T(8,128)(2,1)S(1)} %get-tuple-element.55), channel_id=1, source_target_pairs={{0,12},{4,8},{8,4},{12,0},{1,13},{5,9},{9,5},{13,1},{2,14},{6,10},... | collective-permute-start | bytes 393224 | tf_op jit(solution)/shard_map/ppermute | solution.py:40
  22.7 0.8 collective-permute-start.10
  23.7 1.3 %collective-permute-start.16 = (bf16[256,384]{1,0:T(8,128)(2,1)S(1)}, bf16[256,384]{1,0:T(8,128)(2,1)S(1)}, u32[]{:S(2)}, u32[]{:S(2)}) collective-permute-start(bf16[256,384]{1,0:T(8,128)(2,1)S(1)} %bitcast.90), channel_id=1, source_target_pairs={{0,4},{4,0},{8,12},{12,8},{1,5},{5,1},{9,13},{13,9},{2,6},{6,2},{1... | collective-permute-start | bytes 589832 | tf_op jit(solution)/shard_map/ppermute | solution.py:40
  25.0 0.7 collective-permute-start.23
  25.8 5.8 %collective-permute-done.10 = bf16[2,64,512]{2,1,0:T(8,128)(2,1)S(1)} collective-permute-done((bf16[2,64,512]{2,1,0:T(8,128)(2,1)S(1)}, bf16[2,64,512]{2,1,0:T(8,128)(2,1)S(1)}, u32[]{:S(2)}, u32[]{:S(2)}) %collective-permute-start.10) | collective-permute-done | bytes 131104 | tf_op jit(solution)/shard_map/ppermute | solution.py:40
  31.6 0.8 collective-permute-start.28
  32.4 0.7 collective-permute-start.8
  33.1 1.8 %collective-permute-start.11 = (bf16[2,2,64,512]{3,2,1,0:T(8,128)(2,1)S(1)}, bf16[2,2,64,512]{3,2,1,0:T(8,128)(2,1)}, u32[]{:S(2)}, u32[]{:S(2)}) collective-permute-start(bf16[2,2,64,512]{3,2,1,0:T(8,128)(2,1)S(1)} %pad_maximum_fusion.8), channel_id=1, source_target_pairs={{0,16},{16,0},{1,17},{17,1},{2,18},{18,2},{3,19},{19,3},{4,20},{20... | collective-permute-start | bytes 786440 | tf_op jit(solution)/shard_map/ppermute | solution.py:35
  35.0 1.0 %collective-permute-start.17 = (bf16[2,2,64,512]{3,2,1,0:T(8,128)(2,1)S(1)}, bf16[2,2,64,512]{3,2,1,0:T(8,128)(2,1)}, u32[]{:S(2)}, u32[]{:S(2)}) collective-permute-start(bf16[2,2,64,512]{3,2,1,0:T(8,128)(2,1)S(1)} %pad_maximum_fusion.9), channel_id=1, source_target_pairs={{0,16},{16,0},{1,17},{17,1},{2,18},{18,2},{3,19},{19,3},{4,20},{20... | collective-permute-start | bytes 786440 | tf_op jit(solution)/shard_map/ppermute | solution.py:35
  36.2 3.1 %collective-permute-start.24 = (bf16[256,384]{1,0:T(8,128)(2,1)S(1)}, bf16[256,384]{1,0:T(8,128)(2,1)S(1)}, u32[]{:S(2)}, u32[]{:S(2)}) collective-permute-start(bf16[256,384]{1,0:T(8,128)(2,1)S(1)} %bitcast.96), channel_id=1, source_target_pairs={{0,4},{4,0},{8,12},{12,8},{1,5},{5,1},{9,13},{13,9},{2,6},{6,2},{1... | collective-permute-start | bytes 589832 | tf_op jit(solution)/shard_map/ppermute | solution.py:40
  39.5 0.5 collective-permute-start.29
  40.0 1.3 %collective-permute-start.9 = (bf16[544,256]{1,0:T(8,128)(2,1)S(1)}, bf16[544,256]{1,0:T(8,128)(2,1)S(1)}, u32[]{:S(2)}, u32[]{:S(2)}) collective-permute-start(bf16[544,256]{1,0:T(8,128)(2,1)S(1)} %collective-permute-done.8), channel_id=1, source_target_pairs={{8,12},{4,0},{9,13},{5,1},{10,14},{6,2},{11,15},{7,3},{24,28},{20,... | collective-permute-start | bytes 835592 | tf_op jit(solution)/shard_map/ppermute | solution.py:252
  41.3 3.8 %collective-permute-done.24 = bf16[256,384]{1,0:T(8,128)(2,1)S(1)} collective-permute-done((bf16[256,384]{1,0:T(8,128)(2,1)S(1)}, bf16[256,384]{1,0:T(8,128)(2,1)S(1)}, u32[]{:S(2)}, u32[]{:S(2)}) %collective-permute-start.24) | collective-permute-done | bytes 196640 | tf_op jit(solution)/shard_map/ppermute | solution.py:40
  45.1 1.4 %collective-permute-start.20 = (bf16[512,384]{1,0:T(8,128)(2,1)S(1)}, bf16[512,384]{1,0:T(8,128)(2,1)}, u32[]{:S(2)}, u32[]{:S(2)}) collective-permute-start(bf16[512,384]{1,0:T(8,128)(2,1)S(1)} %pad_maximum_fusion.4), channel_id=1, source_target_pairs={{4,8},{8,4},{5,9},{9,5},{6,10},{10,6},{7,11},{11,7},{20,24},{24,20... | collective-permute-start | bytes 1179656 | tf_op jit(solution)/shard_map/ppermute | solution.py:249
  46.6 0.7 collective-permute-start.25
  47.3 0.9 %collective-permute-done.29 = bf16[256,384]{1,0:T(8,128)(2,1)S(1)} collective-permute-done((bf16[256,384]{1,0:T(8,128)(2,1)S(1)}, bf16[256,384]{1,0:T(8,128)(2,1)S(1)}, u32[]{:S(2)}, u32[]{:S(2)}) %collective-permute-start.29) | collective-permute-done | bytes 196640 | tf_op jit(solution)/shard_map/ppermute | solution.py:40
  48.3 0.6 collective-permute-start.18
  48.8 2.4 %collective-permute-done.9 = bf16[544,256]{1,0:T(8,128)(2,1)S(1)} collective-permute-done((bf16[544,256]{1,0:T(8,128)(2,1)S(1)}, bf16[544,256]{1,0:T(8,128)(2,1)S(1)}, u32[]{:S(2)}, u32[]{:S(2)}) %collective-permute-start.9) | collective-permute-done | bytes 278560 | tf_op jit(solution)/shard_map/ppermute | solution.py:252
  51.6 1.3 %collective-permute-start.21 = (bf16[512,384]{1,0:T(8,128)(2,1)}, bf16[512,384]{1,0:T(8,128)(2,1)S(1)}, u32[]{:S(2)}, u32[]{:S(2)}) collective-permute-start(bf16[512,384]{1,0:T(8,128)(2,1)} %collective-permute-done.20), channel_id=1, source_target_pairs={{8,12},{4,0},{9,13},{5,1},{10,14},{6,2},{11,15},{7,3},{24,28},{20,... | collective-permute-start | bytes 1179656 | tf_op jit(solution)/shard_map/ppermute | solution.py:252
  52.9 1.3 %select_bitcast_fusion.1 = (bf16[2,2,1,64,512]{4,3,1,0,2:T(8,128)(2,1)S(1)}, bf16[2,2,1,64,512]{4,3,1,0,2:T(8,128)(2,1)S(1)}, bf16[2,2,1,64,512]{4,3,1,0,2:T(8,128)(2,1)S(1)}, bf16[2,2,1,64,512]{4,3,1,0,2:T(8,128)(2,1)S(1)}) fusion(bf16[2,2,64,512]{3,2,1,0:T(8,128)(2,1)} %collective-permute-done.17, bf16[2,2,64,512]{3,2,1,0:T(8,128)(2,1)} %collective-permute-done.18, ...), kind=kLoop, calls=%fused_computation.78 | loop fusion | flops 524288 | bytes 2097153 | tf_op jit(solution)/shard_map/stack | solution.py:195
  54.8 0.7 fusion.60
  55.6 1.4 %collective-permute-start.19 = (bf16[512,256]{1,0:T(8,128)(2,1)S(1)}, bf16[512,256]{1,0:T(8,128)(2,1)S(1)}, u32[]{:S(2)}, u32[]{:S(2)}) collective-permute-start(bf16[512,256]{1,0:T(8,128)(2,1)S(1)} %slice.128), channel_id=1, source_target_pairs={{0,2},{1,3},{2,0},{3,1},{4,6},{5,7},{6,4},{7,5},{8,10},{9,11},{10,... | collective-permute-start | bytes 786440 | tf_op jit(solution)/shard_map/ppermute | solution.py:40
  57.0 1.3 %collective-permute-start.26 = (bf16[512,384]{1,0:T(8,128)(2,1)S(1)}, bf16[512,384]{1,0:T(8,128)(2,1)S(1)}, u32[]{:S(2)}, u32[]{:S(2)}) collective-permute-start(bf16[512,384]{1,0:T(8,128)(2,1)S(1)} %collective-permute-done.25), channel_id=1, source_target_pairs={{8,12},{4,0},{9,13},{5,1},{10,14},{6,2},{11,15},{7,3},{24,28},{20,... | collective-permute-start | bytes 1179656 | tf_op jit(solution)/shard_map/ppermute | solution.py:252
  58.3 0.7 collective-permute-start.30
  59.0 8.8 %collective-permute-done.21 = bf16[512,384]{1,0:T(8,128)(2,1)S(1)} collective-permute-done((bf16[512,384]{1,0:T(8,128)(2,1)}, bf16[512,384]{1,0:T(8,128)(2,1)S(1)}, u32[]{:S(2)}, u32[]{:S(2)}) %collective-permute-start.21) | collective-permute-done | bytes 393248 | tf_op jit(solution)/shard_map/ppermute | solution.py:252
  67.8 1.3 %fusion.11 = f32[1024,384]{1,0:T(8,128)S(1)} fusion(bf16[512,384]{1,0:T(8,128)(2,1)S(1)} %broadcast_select_fusion.2, bf16[256,384]{1,0:T(8,128)(2,1)S(1)} %collective-permute-done.16, bf16[256,384]{1,0:T(8,128)(2,1)S(1)} %bitcast.92, bf16[1024,512]{1,0:T(8,128)(2,1)S(1)} %get-tuple-element.49, bf16[1024,512]{1,0:T(8,128)(2,1)S(1)} %get-tuple-element.48), kind=kOutput, calls=%fused_computation.29 | convolution fusion | flops 811859968 | bytes 4456448 | tf_op jit(solution)/shard_map/dot_general | solution.py:265
  69.1 0.8 collective-permute-start.22
  70.2 1.3 %collective-permute-start.31 = (bf16[512,384]{1,0:T(8,128)(2,1)S(1)}, bf16[512,384]{1,0:T(8,128)(2,1)S(1)}, u32[]{:S(2)}, u32[]{:S(2)}) collective-permute-start(bf16[512,384]{1,0:T(8,128)(2,1)S(1)} %collective-permute-done.30), channel_id=1, source_target_pairs={{8,12},{4,0},{9,13},{5,1},{10,14},{6,2},{11,15},{7,3},{24,28},{20,... | collective-permute-start | bytes 1179656 | tf_op jit(solution)/shard_map/ppermute | solution.py:252
  71.5 2.5 %collective-permute-done.26 = bf16[512,384]{1,0:T(8,128)(2,1)S(1)} collective-permute-done((bf16[512,384]{1,0:T(8,128)(2,1)S(1)}, bf16[512,384]{1,0:T(8,128)(2,1)S(1)}, u32[]{:S(2)}, u32[]{:S(2)}) %collective-permute-start.26) | collective-permute-done | bytes 393248 | tf_op jit(solution)/shard_map/ppermute | solution.py:252
  74.1 1.3 %fusion.17 = f32[1024,384]{1,0:T(8,128)S(1)} fusion(bf16[512,384]{1,0:T(8,128)(2,1)S(1)} %broadcast_select_fusion.1, bf16[256,384]{1,0:T(8,128)(2,1)S(1)} %copy-done.6, bf16[256,384]{1,0:T(8,128)(2,1)S(1)} %bitcast.98, bf16[1024,512]{1,0:T(8,128)(2,1)S(1)} %get-tuple-element.49, bf16[1024,512]{1,0:T(8,128)(2,1)S(1)} %get-tuple-element.48), kind=kOutput, calls=%fused_computation.35 | convolution fusion | flops 811859968 | bytes 4456448 | tf_op jit(solution)/shard_map/dot_general | solution.py:265
  75.4 1.0 %collective-permute-start.27 = (bf16[512,384]{1,0:T(8,128)(2,1)S(1)}, bf16[512,384]{1,0:T(8,128)(2,1)S(1)}, u32[]{:S(2)}, u32[]{:S(2)}) collective-permute-start(bf16[512,384]{1,0:T(8,128)(2,1)S(1)} %slice.126), channel_id=1, source_target_pairs={{0,2},{1,3},{2,0},{3,1},{4,6},{5,7},{6,4},{7,5},{8,10},{9,11},{10,... | collective-permute-start | bytes 1179656 | tf_op jit(solution)/shard_map/ppermute | solution.py:40
  76.4 4.7 %collective-permute-done.31 = bf16[512,384]{1,0:T(8,128)(2,1)S(1)} collective-permute-done((bf16[512,384]{1,0:T(8,128)(2,1)S(1)}, bf16[512,384]{1,0:T(8,128)(2,1)S(1)}, u32[]{:S(2)}, u32[]{:S(2)}) %collective-permute-start.31) | collective-permute-done | bytes 393248 | tf_op jit(solution)/shard_map/ppermute | solution.py:252
  81.1 1.3 %fusion.23 = f32[1024,384]{1,0:T(8,128)S(1)} fusion(bf16[512,384]{1,0:T(8,128)(2,1)S(1)} %broadcast_select_fusion, bf16[256,384]{1,0:T(8,128)(2,1)S(1)} %copy-done.4, bf16[256,384]{1,0:T(8,128)(2,1)S(1)} %bitcast.95, bf16[1024,512]{1,0:T(8,128)(2,1)S(1)} %get-tuple-element.49, bf16[1024,512]{1,0:T(8,128)(2,1)S(1)} %get-tuple-element.48), kind=kOutput, calls=%fused_computation.41 | convolution fusion | flops 811859968 | bytes 4456448 | tf_op jit(solution)/shard_map/dot_general | solution.py:265
  82.5 0.7 collective-permute-start.32
  83.3 2.9 %collective-permute-done.27 = bf16[512,384]{1,0:T(8,128)(2,1)S(1)} collective-permute-done((bf16[512,384]{1,0:T(8,128)(2,1)S(1)}, bf16[512,384]{1,0:T(8,128)(2,1)S(1)}, u32[]{:S(2)}, u32[]{:S(2)}) %collective-permute-start.27) | collective-permute-done | bytes 393248 | tf_op jit(solution)/shard_map/ppermute | solution.py:40
  86.3 5.4 %collective-permute-done.32 = bf16[512,384]{1,0:T(8,128)(2,1)S(1)} collective-permute-done((bf16[512,384]{1,0:T(8,128)(2,1)S(1)}, bf16[512,384]{1,0:T(8,128)(2,1)S(1)}, u32[]{:S(2)}, u32[]{:S(2)}) %collective-permute-start.32) | collective-permute-done | bytes 393248 | tf_op jit(solution)/shard_map/ppermute | solution.py:40
  91.7 0.8 fusion.35
  (92 shorter events, 4.1 us)
Async XLA Ops:
  0.0 9.4 %copy-start = (bf16[1,128,2048]{2,1,0:T(8,128)(2,1)S(1)}, bf16[1,128,2048]{2,1,0:T(8,128)(2,1)}, u32[]{:S(2)}) copy-start(bf16[1,128,2048]{2,1,0:T(8,128)(2,1)} %param.4) | copy-start | bytes 1572868
  0.0 7.3 %collective-permute-start = (f32[1,128]{1,0:T(1,128)}, f32[1,128]{1,0:T(1,128)S(1)}, u32[]{:S(2)}, u32[]{:S(2)}) collective-permute-start(f32[1,128]{1,0:T(1,128)} %param.5), channel_id=1, source_target_pairs={{0,16},{16,0},{1,17},{17,1},{2,18},{18,2},{3,19},{19,3},{4,20},{20... | collective-permute-start | bytes 1544 | tf_op jit(solution)/shard_map/ppermute | solution.py:35
  3.0 4.4 %collective-permute-start.1 = (s32[1,128,1]{1,2,0:T(1,128)}, s32[1,128,1]{1,2,0:T(1,128)S(1)}, u32[]{:S(2)}, u32[]{:S(2)}) collective-permute-start(s32[1,128,1]{1,2,0:T(1,128)} %param.6), channel_id=1, source_target_pairs={{0,16},{16,0},{1,17},{17,1},{2,18},{18,2},{3,19},{19,3},{4,20},{20... | collective-permute-start | bytes 1544 | tf_op jit(solution)/shard_map/ppermute | solution.py:35
  3.0 9.1 %copy-start.7 = (s32[1,128,1]{1,2,0:T(1,128)S(1)}, s32[1,128,1]{1,2,0:T(1,128)}, u32[]{:S(2)}) copy-start(s32[1,128,1]{1,2,0:T(1,128)} %param.6) | copy-start | bytes 1540
  3.0 9.6 %copy-start.2 = (bf16[1,1,4,128,1408]{4,3,2,1,0:T(8,128)(2,1)S(1)}, bf16[1,1,4,128,1408]{4,3,2,1,0:T(8,128)(2,1)}, u32[]{:S(2)}) copy-start(bf16[1,1,4,128,1408]{4,3,2,1,0:T(8,128)(2,1)} %param.7) | copy-start | bytes 4325380
  4.1 8.6 %collective-permute-start.5 = (bf16[4,64,256]{2,1,0:T(8,128)(2,1)S(1)}, bf16[4,64,256]{2,1,0:T(8,128)(2,1)}, u32[]{:S(2)}, u32[]{:S(2)}) collective-permute-start(bf16[4,64,256]{2,1,0:T(8,128)(2,1)S(1)} %slice.77), channel_id=1, source_target_pairs={{0,2},{1,3},{2,0},{3,1},{4,6},{5,7},{6,4},{7,5},{8,10},{9,11},{10,... | collective-permute-start | bytes 393224 | tf_op jit(solution)/shard_map/ppermute | solution.py:40
  7.3 3.5 %collective-permute-start.4 = (s32[1,128,1]{1,2,0:T(1,128)}, s32[1,128,1]{1,2,0:T(1,128)S(1)}, u32[]{:S(2)}, u32[]{:S(2)}) collective-permute-start(s32[1,128,1]{1,2,0:T(1,128)} %param.6), channel_id=1, source_target_pairs={{0,3},{1,2},{2,1},{3,0},{4,7},{5,6},{6,5},{7,4},{8,11},{9,10},{10,... | collective-permute-start | bytes 1544 | tf_op jit(solution)/shard_map/ppermute | solution.py:40
  7.4 4.8 %collective-permute-start.3 = (s32[1,128,1]{1,2,0:T(1,128)}, s32[1,128,1]{1,2,0:T(1,128)S(1)}, u32[]{:S(2)}, u32[]{:S(2)}) collective-permute-start(s32[1,128,1]{1,2,0:T(1,128)} %param.6), channel_id=1, source_target_pairs={{0,2},{1,3},{2,0},{3,1},{4,6},{5,7},{6,4},{7,5},{8,10},{9,11},{10,... | collective-permute-start | bytes 1544 | tf_op jit(solution)/shard_map/ppermute | solution.py:40
  8.2 4.0 %collective-permute-start.2 = (s32[1,128,1]{1,2,0:T(1,128)}, s32[1,128,1]{1,2,0:T(1,128)S(1)}, u32[]{:S(2)}, u32[]{:S(2)}) collective-permute-start(s32[1,128,1]{1,2,0:T(1,128)} %param.6), channel_id=1, source_target_pairs={{0,1},{1,0},{2,3},{3,2},{4,5},{5,4},{6,7},{7,6},{8,9},{9,8},{10,11... | collective-permute-start | bytes 1544 | tf_op jit(solution)/shard_map/ppermute | solution.py:40
  9.7 9.2 %collective-permute-start.7 = (bf16[64,2048]{1,0:T(8,128)(2,1)S(1)}, bf16[64,2048]{1,0:T(8,128)(2,1)S(1)}, u32[]{:S(2)}, u32[]{:S(2)}) collective-permute-start(bf16[64,2048]{1,0:T(8,128)(2,1)S(1)} %convolution_convert_fusion.1), channel_id=1, source_target_pairs={{0,2},{1,3},{2,0},{3,1},{4,6},{5,7},{6,4},{7,5},{8,10},{9,11},{10,... | collective-permute-start | bytes 786440 | tf_op jit(solution)/shard_map/ppermute | solution.py:40
  10.8 12.7 %collective-permute-start.15 = (bf16[4,64,384]{2,1,0:T(8,128)(2,1)S(1)}, bf16[4,64,384]{2,1,0:T(8,128)(2,1)S(1)}, u32[]{:S(2)}, u32[]{:S(2)}) collective-permute-start(bf16[4,64,384]{2,1,0:T(8,128)(2,1)S(1)} %get-tuple-element.34), channel_id=1, source_target_pairs={{0,2},{1,3},{2,0},{3,1},{4,6},{5,7},{6,4},{7,5},{8,10},{9,11},{10,... | collective-permute-start | bytes 589832 | tf_op jit(solution)/shard_map/ppermute | solution.py:40
  13.8 11.2 %collective-permute-start.6 = (bf16[272,256]{1,0:T(8,128)(2,1)S(1)}, bf16[272,256]{1,0:T(8,128)(2,1)S(1)}, u32[]{:S(2)}, u32[]{:S(2)}) collective-permute-start(bf16[272,256]{1,0:T(8,128)(2,1)S(1)} %pad_maximum_fusion.10), channel_id=1, source_target_pairs={{0,4},{4,0},{8,12},{12,8},{1,5},{5,1},{9,13},{13,9},{2,6},{6,2},{1... | collective-permute-start | bytes 417800 | tf_op jit(solution)/shard_map/ppermute | solution.py:40
  19.0 13.4 %collective-permute-start.14 = (bf16[2,64,512]{2,1,0:T(8,128)(2,1)S(1)}, bf16[2,64,512]{2,1,0:T(8,128)(2,1)S(1)}, u32[]{:S(2)}, u32[]{:S(2)}) collective-permute-start(bf16[2,64,512]{2,1,0:T(8,128)(2,1)S(1)} %get-tuple-element.55), channel_id=1, source_target_pairs={{0,12},{4,8},{8,4},{12,0},{1,13},{5,9},{9,5},{13,1},{2,14},{6,10},... | collective-permute-start | bytes 393224 | tf_op jit(solution)/shard_map/ppermute | solution.py:40
  22.7 10.4 %collective-permute-start.13 = (bf16[2,64,512]{2,1,0:T(8,128)(2,1)S(1)}, bf16[2,64,512]{2,1,0:T(8,128)(2,1)S(1)}, u32[]{:S(2)}, u32[]{:S(2)}) collective-permute-start(bf16[2,64,512]{2,1,0:T(8,128)(2,1)S(1)} %get-tuple-element.54), channel_id=1, source_target_pairs={{0,8},{4,12},{8,0},{12,4},{1,9},{5,13},{9,1},{13,5},{2,10},{6,14},... | collective-permute-start | bytes 393224 | tf_op jit(solution)/shard_map/ppermute | solution.py:40
  22.7 8.9 %collective-permute-start.10 = (bf16[2,64,512]{2,1,0:T(8,128)(2,1)S(1)}, bf16[2,64,512]{2,1,0:T(8,128)(2,1)S(1)}, u32[]{:S(2)}, u32[]{:S(2)}) collective-permute-start(bf16[2,64,512]{2,1,0:T(8,128)(2,1)S(1)} %get-tuple-element.53), channel_id=1, source_target_pairs={{0,4},{4,0},{8,12},{12,8},{1,5},{5,1},{9,13},{13,9},{2,6},{6,2},{1... | collective-permute-start | bytes 393224 | tf_op jit(solution)/shard_map/ppermute | solution.py:40
  23.7 11.3 %collective-permute-start.16 = (bf16[256,384]{1,0:T(8,128)(2,1)S(1)}, bf16[256,384]{1,0:T(8,128)(2,1)S(1)}, u32[]{:S(2)}, u32[]{:S(2)}) collective-permute-start(bf16[256,384]{1,0:T(8,128)(2,1)S(1)} %bitcast.90), channel_id=1, source_target_pairs={{0,4},{4,0},{8,12},{12,8},{1,5},{5,1},{9,13},{13,9},{2,6},{6,2},{1... | collective-permute-start | bytes 589832 | tf_op jit(solution)/shard_map/ppermute | solution.py:40
  25.0 11.0 %collective-permute-start.23 = (bf16[4,64,384]{2,1,0:T(8,128)(2,1)S(1)}, bf16[4,64,384]{2,1,0:T(8,128)(2,1)S(1)}, u32[]{:S(2)}, u32[]{:S(2)}) collective-permute-start(bf16[4,64,384]{2,1,0:T(8,128)(2,1)S(1)} %get-tuple-element.37), channel_id=1, source_target_pairs={{0,2},{1,3},{2,0},{3,1},{4,6},{5,7},{6,4},{7,5},{8,10},{9,11},{10,... | collective-permute-start | bytes 589832 | tf_op jit(solution)/shard_map/ppermute | solution.py:40
  31.6 7.7 %collective-permute-start.28 = (bf16[4,64,384]{2,1,0:T(8,128)(2,1)S(1)}, bf16[4,64,384]{2,1,0:T(8,128)(2,1)S(1)}, u32[]{:S(2)}, u32[]{:S(2)}) collective-permute-start(bf16[4,64,384]{2,1,0:T(8,128)(2,1)S(1)} %get-tuple-element.40), channel_id=1, source_target_pairs={{0,2},{1,3},{2,0},{3,1},{4,6},{5,7},{6,4},{7,5},{8,10},{9,11},{10,... | collective-permute-start | bytes 589832 | tf_op jit(solution)/shard_map/ppermute | solution.py:40
  32.4 7.6 %collective-permute-start.8 = (bf16[544,256]{1,0:T(8,128)(2,1)S(1)}, bf16[544,256]{1,0:T(8,128)(2,1)S(1)}, u32[]{:S(2)}, u32[]{:S(2)}) collective-permute-start(bf16[544,256]{1,0:T(8,128)(2,1)S(1)} %pad_maximum_fusion.7), channel_id=1, source_target_pairs={{4,8},{8,4},{5,9},{9,5},{6,10},{10,6},{7,11},{11,7},{20,24},{24,20... | collective-permute-start | bytes 835592 | tf_op jit(solution)/shard_map/ppermute | solution.py:249
  33.1 13.5 %collective-permute-start.11 = (bf16[2,2,64,512]{3,2,1,0:T(8,128)(2,1)S(1)}, bf16[2,2,64,512]{3,2,1,0:T(8,128)(2,1)}, u32[]{:S(2)}, u32[]{:S(2)}) collective-permute-start(bf16[2,2,64,512]{3,2,1,0:T(8,128)(2,1)S(1)} %pad_maximum_fusion.8), channel_id=1, source_target_pairs={{0,16},{16,0},{1,17},{17,1},{2,18},{18,2},{3,19},{19,3},{4,20},{20... | collective-permute-start | bytes 786440 | tf_op jit(solution)/shard_map/ppermute | solution.py:35
  35.0 13.3 %collective-permute-start.17 = (bf16[2,2,64,512]{3,2,1,0:T(8,128)(2,1)S(1)}, bf16[2,2,64,512]{3,2,1,0:T(8,128)(2,1)}, u32[]{:S(2)}, u32[]{:S(2)}) collective-permute-start(bf16[2,2,64,512]{3,2,1,0:T(8,128)(2,1)S(1)} %pad_maximum_fusion.9), channel_id=1, source_target_pairs={{0,16},{16,0},{1,17},{17,1},{2,18},{18,2},{3,19},{19,3},{4,20},{20... | collective-permute-start | bytes 786440 | tf_op jit(solution)/shard_map/ppermute | solution.py:35
  36.2 8.9 %collective-permute-start.24 = (bf16[256,384]{1,0:T(8,128)(2,1)S(1)}, bf16[256,384]{1,0:T(8,128)(2,1)S(1)}, u32[]{:S(2)}, u32[]{:S(2)}) collective-permute-start(bf16[256,384]{1,0:T(8,128)(2,1)S(1)} %bitcast.96), channel_id=1, source_target_pairs={{0,4},{4,0},{8,12},{12,8},{1,5},{5,1},{9,13},{13,9},{2,6},{6,2},{1... | collective-permute-start | bytes 589832 | tf_op jit(solution)/shard_map/ppermute | solution.py:40
  39.5 8.7 %collective-permute-start.29 = (bf16[256,384]{1,0:T(8,128)(2,1)S(1)}, bf16[256,384]{1,0:T(8,128)(2,1)S(1)}, u32[]{:S(2)}, u32[]{:S(2)}) collective-permute-start(bf16[256,384]{1,0:T(8,128)(2,1)S(1)} %bitcast.93), channel_id=1, source_target_pairs={{0,4},{4,0},{8,12},{12,8},{1,5},{5,1},{9,13},{13,9},{2,6},{6,2},{1... | collective-permute-start | bytes 589832 | tf_op jit(solution)/shard_map/ppermute | solution.py:40
  40.0 11.2 %collective-permute-start.9 = (bf16[544,256]{1,0:T(8,128)(2,1)S(1)}, bf16[544,256]{1,0:T(8,128)(2,1)S(1)}, u32[]{:S(2)}, u32[]{:S(2)}) collective-permute-start(bf16[544,256]{1,0:T(8,128)(2,1)S(1)} %collective-permute-done.8), channel_id=1, source_target_pairs={{8,12},{4,0},{9,13},{5,1},{10,14},{6,2},{11,15},{7,3},{24,28},{20,... | collective-permute-start | bytes 835592 | tf_op jit(solution)/shard_map/ppermute | solution.py:252
  45.1 1.4 %copy-start.5 = (bf16[256,384]{1,0:T(8,128)(2,1)}, bf16[256,384]{1,0:T(8,128)(2,1)S(1)}, u32[]{:S(2)}) copy-start(bf16[256,384]{1,0:T(8,128)(2,1)S(1)} %collective-permute-done.24) | copy-start | bytes 589828
  45.1 6.5 %collective-permute-start.20 = (bf16[512,384]{1,0:T(8,128)(2,1)S(1)}, bf16[512,384]{1,0:T(8,128)(2,1)}, u32[]{:S(2)}, u32[]{:S(2)}) collective-permute-start(bf16[512,384]{1,0:T(8,128)(2,1)S(1)} %pad_maximum_fusion.4), channel_id=1, source_target_pairs={{4,8},{8,4},{5,9},{9,5},{6,10},{10,6},{7,11},{11,7},{20,24},{24,20... | collective-permute-start | bytes 1179656 | tf_op jit(solution)/shard_map/ppermute | solution.py:249
  46.6 10.4 %collective-permute-start.25 = (bf16[512,384]{1,0:T(8,128)(2,1)S(1)}, bf16[512,384]{1,0:T(8,128)(2,1)S(1)}, u32[]{:S(2)}, u32[]{:S(2)}) collective-permute-start(bf16[512,384]{1,0:T(8,128)(2,1)S(1)} %pad_maximum_fusion.5), channel_id=1, source_target_pairs={{4,8},{8,4},{5,9},{9,5},{6,10},{10,6},{7,11},{11,7},{20,24},{24,20... | collective-permute-start | bytes 1179656 | tf_op jit(solution)/shard_map/ppermute | solution.py:249
  48.2 3.0 %copy-start.3 = (bf16[256,384]{1,0:T(8,128)(2,1)}, bf16[256,384]{1,0:T(8,128)(2,1)S(1)}, u32[]{:S(2)}) copy-start(bf16[256,384]{1,0:T(8,128)(2,1)S(1)} %collective-permute-done.29) | copy-start | bytes 589828
  48.2 4.7 %collective-permute-start.12 = (bf16[2,2,64,512]{3,2,1,0:T(8,128)(2,1)}, bf16[2,2,64,512]{3,2,1,0:T(8,128)(2,1)}, u32[]{:S(2)}, u32[]{:S(2)}) collective-permute-start(bf16[2,2,64,512]{3,2,1,0:T(8,128)(2,1)} %collective-permute-done.11), channel_id=1, source_target_pairs={{0,1},{1,0},{2,3},{3,2},{4,5},{5,4},{6,7},{7,6},{8,9},{9,8},{10,11... | collective-permute-start | bytes 786440 | tf_op jit(solution)/shard_map/ppermute | solution.py:40
  48.3 4.6 %collective-permute-start.18 = (bf16[2,2,64,512]{3,2,1,0:T(8,128)(2,1)}, bf16[2,2,64,512]{3,2,1,0:T(8,128)(2,1)}, u32[]{:S(2)}, u32[]{:S(2)}) collective-permute-start(bf16[2,2,64,512]{3,2,1,0:T(8,128)(2,1)} %collective-permute-done.17), channel_id=1, source_target_pairs={{0,1},{1,0},{2,3},{3,2},{4,5},{5,4},{6,7},{7,6},{8,9},{9,8},{10,11... | collective-permute-start | bytes 786440 | tf_op jit(solution)/shard_map/ppermute | solution.py:40
  51.6 16.1 %collective-permute-start.21 = (bf16[512,384]{1,0:T(8,128)(2,1)}, bf16[512,384]{1,0:T(8,128)(2,1)S(1)}, u32[]{:S(2)}, u32[]{:S(2)}) collective-permute-start(bf16[512,384]{1,0:T(8,128)(2,1)} %collective-permute-done.20), channel_id=1, source_target_pairs={{8,12},{4,0},{9,13},{5,1},{10,14},{6,2},{11,15},{7,3},{24,28},{20,... | collective-permute-start | bytes 1179656 | tf_op jit(solution)/shard_map/ppermute | solution.py:252
  55.6 14.4 %collective-permute-start.19 = (bf16[512,256]{1,0:T(8,128)(2,1)S(1)}, bf16[512,256]{1,0:T(8,128)(2,1)S(1)}, u32[]{:S(2)}, u32[]{:S(2)}) collective-permute-start(bf16[512,256]{1,0:T(8,128)(2,1)S(1)} %slice.128), channel_id=1, source_target_pairs={{0,2},{1,3},{2,0},{3,1},{4,6},{5,7},{6,4},{7,5},{8,10},{9,11},{10,... | collective-permute-start | bytes 786440 | tf_op jit(solution)/shard_map/ppermute | solution.py:40
  57.0 17.0 %collective-permute-start.26 = (bf16[512,384]{1,0:T(8,128)(2,1)S(1)}, bf16[512,384]{1,0:T(8,128)(2,1)S(1)}, u32[]{:S(2)}, u32[]{:S(2)}) collective-permute-start(bf16[512,384]{1,0:T(8,128)(2,1)S(1)} %collective-permute-done.25), channel_id=1, source_target_pairs={{8,12},{4,0},{9,13},{5,1},{10,14},{6,2},{11,15},{7,3},{24,28},{20,... | collective-permute-start | bytes 1179656 | tf_op jit(solution)/shard_map/ppermute | solution.py:252
  58.3 11.9 %collective-permute-start.30 = (bf16[512,384]{1,0:T(8,128)(2,1)S(1)}, bf16[512,384]{1,0:T(8,128)(2,1)S(1)}, u32[]{:S(2)}, u32[]{:S(2)}) collective-permute-start(bf16[512,384]{1,0:T(8,128)(2,1)S(1)} %pad_maximum_fusion.6), channel_id=1, source_target_pairs={{4,8},{8,4},{5,9},{9,5},{6,10},{10,6},{7,11},{11,7},{20,24},{24,20... | collective-permute-start | bytes 1179656 | tf_op jit(solution)/shard_map/ppermute | solution.py:249
  69.1 14.0 %collective-permute-start.22 = (bf16[512,384]{1,0:T(8,128)(2,1)S(1)}, bf16[512,384]{1,0:T(8,128)(2,1)S(1)}, u32[]{:S(2)}, u32[]{:S(2)}) collective-permute-start(bf16[512,384]{1,0:T(8,128)(2,1)S(1)} %slice.127), channel_id=1, source_target_pairs={{0,2},{1,3},{2,0},{3,1},{4,6},{5,7},{6,4},{7,5},{8,10},{9,11},{10,... | collective-permute-start | bytes 1179656 | tf_op jit(solution)/shard_map/ppermute | solution.py:40
  70.1 4.0 %copy-start.6 = (bf16[256,384]{1,0:T(8,128)(2,1)S(1)}, bf16[256,384]{1,0:T(8,128)(2,1)}, u32[]{:S(2)}) copy-start(bf16[256,384]{1,0:T(8,128)(2,1)} %copy-done.5) | copy-start | bytes 589828
  70.2 10.9 %collective-permute-start.31 = (bf16[512,384]{1,0:T(8,128)(2,1)S(1)}, bf16[512,384]{1,0:T(8,128)(2,1)S(1)}, u32[]{:S(2)}, u32[]{:S(2)}) collective-permute-start(bf16[512,384]{1,0:T(8,128)(2,1)S(1)} %collective-permute-done.30), channel_id=1, source_target_pairs={{8,12},{4,0},{9,13},{5,1},{10,14},{6,2},{11,15},{7,3},{24,28},{20,... | collective-permute-start | bytes 1179656 | tf_op jit(solution)/shard_map/ppermute | solution.py:252
  75.3 5.8 %copy-start.4 = (bf16[256,384]{1,0:T(8,128)(2,1)S(1)}, bf16[256,384]{1,0:T(8,128)(2,1)}, u32[]{:S(2)}) copy-start(bf16[256,384]{1,0:T(8,128)(2,1)} %copy-done.3) | copy-start | bytes 589828
  75.4 10.8 %collective-permute-start.27 = (bf16[512,384]{1,0:T(8,128)(2,1)S(1)}, bf16[512,384]{1,0:T(8,128)(2,1)S(1)}, u32[]{:S(2)}, u32[]{:S(2)}) collective-permute-start(bf16[512,384]{1,0:T(8,128)(2,1)S(1)} %slice.126), channel_id=1, source_target_pairs={{0,2},{1,3},{2,0},{3,1},{4,6},{5,7},{6,4},{7,5},{8,10},{9,11},{10,... | collective-permute-start | bytes 1179656 | tf_op jit(solution)/shard_map/ppermute | solution.py:40
  82.5 9.2 %collective-permute-start.32 = (bf16[512,384]{1,0:T(8,128)(2,1)S(1)}, bf16[512,384]{1,0:T(8,128)(2,1)S(1)}, u32[]{:S(2)}, u32[]{:S(2)}) collective-permute-start(bf16[512,384]{1,0:T(8,128)(2,1)S(1)} %slice.125), channel_id=1, source_target_pairs={{0,2},{1,3},{2,0},{3,1},{4,6},{5,7},{6,4},{7,5},{8,10},{9,11},{10,... | collective-permute-start | bytes 1179656 | tf_op jit(solution)/shard_map/ppermute | solution.py:40
  86.3 5.4 %copy-start.1 = (bf16[1,512,1408]{2,1,0:T(8,128)(2,1)}, bf16[1,512,1408]{2,1,0:T(8,128)(2,1)S(1)}, u32[]{:S(2)}) copy-start(bf16[1,512,1408]{2,1,0:T(8,128)(2,1)S(1)} %fusion.33) | copy-start | bytes 4325380

commit v3 on v2

--- a/solution.py
+++ b/solution.py
@@ -5,27 +5,22 @@
 
 CUTS = (2, 3, 3, 3)
 GROUPS = (1, 1, 1, 1)
+FIRST = ("M2",)
 ORDER = {
+    "F1": ("F0",),
     "F2": ("F0",),
     "F3": ("F1",),
-    "M2": ("M0",),
+    "M1": ("M0",),
+    "M2": ("M1",),
     "M3": ("M2",),
     "N1": ("G", "H"),
-    "N2": ("G", "H"),
+    "N2": ("H",),
     "N3": ("G", "H"),
-    "P1": ("A1",),
     "S1": ("sent",),
-    "S2": ("X",),
-    "S3": ("X",),
+    "S2": ("S0",),
+    "S3": ("Z1",),
     "T0": ("upper0",),
-    "T1": ("T0", "sent", "upper1"),
-    "T2": ("own0",),
-    "T3": ("share1", "share2", "share3"),
-    "couple0": ("T3",),
-    "own0": ("T1",),
-    "own1": ("T3",),
-    "pair": ("T2",),
-    "scaled": ("T0",),
+    "total2": ("total1",),
 }
 
 
@@ -138,63 +133,54 @@
     def H(self):
         return shifted(self.free(self.args[2], "H"), "pipe", 1)
 
-    def P(self, pair):
-        value = jnp.stack([self("Z", 2 * pair) if pair else self("share", 0), self("Z", 2 * pair + 1)])
-        return shifted(self.free(value, "P" + str(pair)), "pipe", -1)
-
-    def picks(self):
-        f32, half, tokens = jnp.float32, self.half, self.tokens
+    def pick(self):
+        half, tokens = self.half, self.tokens
         routes = self("H")[0, :, 0]
         index = lax.broadcasted_iota(jnp.int32, (tokens, tokens), 0)
         other = lax.broadcasted_iota(jnp.int32, (tokens, tokens), 1)
         earlier = (index < other) & (routes[:, None] == routes[None, :])
         slot = jnp.sum(earlier.astype(jnp.int32), axis=0)
-        row = lax.broadcasted_iota(jnp.int32, (half, tokens), 0)
-
-        def of(column):
-            place = jnp.where(routes == column, slot, tokens - 1 - slot)
-            return (row == place[None, :]).astype(jnp.bfloat16)
-
-        return of
+        place = jnp.where(routes == self.expert, slot, tokens - 1 - slot)
+        place = jnp.where(place < half, place, tokens + half - 1 - place)
+        return (index == place[None, :]).astype(jnp.bfloat16)
 
     def scaled(self):
         rows, gates = self.free(self.args[0][0], "scaled"), self.free(self("G")[0], "scaled")
         return (gates[:, None] * rows.astype(jnp.float32)).astype(jnp.bfloat16)
 
-    def kept(self):
-        return jnp.dot(
-            self("picks")(self.expert), self("scaled"), preferred_element_type=jnp.float32
-        ).astype(jnp.bfloat16)
-
     def sent(self):
-        return jnp.dot(
-            self("picks")(1 - self.expert), self("scaled"), preferred_element_type=jnp.float32
-        ).astype(jnp.bfloat16)
-
-    def X(self):
-        return crossed(self.free(self("sent"), "X"), "expert", 2)
-
-    def pair(self):
-        kept, came, first = self("kept"), self.free(self("X"), "pair"), self.expert == 0
-        return jnp.stack([jnp.where(first, kept, came), jnp.where(first, came, kept)])
+        rows = jnp.dot(self("pick"), self("scaled"), preferred_element_type=jnp.float32)
+        return rows.astype(jnp.bfloat16).reshape(2, self.half, self.width)
 
     def share(self, mask):
-        return lax.dynamic_slice_in_dim(self("pair"), (self.replica ^ mask) * self.part, self.part, axis=2)
+        return lax.dynamic_slice_in_dim(self("sent"), (self.replica ^ mask) * self.part, self.part, axis=2)
 
     def Z(self, mask):
         return crossed(self.free(self("share", mask), "Z" + str(mask)), "dp", mask)
 
-    def K(self, pair):
-        return crossed(self.free(self("P", pair), "K" + str(pair)), "expert", 1)
+    def near(self):
+        at = [self("share", 0)] + [self("Z", mask) for mask in (1, 2, 3)]
+        at[1] = self.free(at[1], "near")
+        at[2], at[3] = jnp.where(self.inner, at[3], at[2]), jnp.where(self.inner, at[2], at[3])
+        return jnp.stack(at, axis=1)
+
+    def X(self):
+        return crossed(self.free(self("near")[1], "X"), "expert", 2)
+
+    def pair(self):
+        kept, came, first = self("near")[0], self.free(self("X"), "pair"), self.expert == 0
+        return jnp.stack([jnp.where(first, kept, came), jnp.where(first, came, kept)], axis=1)
+
+    def P(self):
+        return shifted(self.free(self("pair"), "P"), "pipe", -1)
+
+    def K(self):
+        return crossed(self.free(self("P"), "K"), "expert", 1)
 
     def both(self):
-        first, inner = self.core == 0, self.inner
-        grads = []
-        for pair in (0, 1):
-            mine, theirs = self("P", pair), self.free(self("K", pair), "both")
-            grads.append(jnp.stack([jnp.where(first, mine, theirs), jnp.where(first, theirs, mine)], axis=2))
-        grads[1] = jnp.where(inner, grads[1][::-1], grads[1])
-        grads = jnp.concatenate(grads).reshape(self.replicas, self.sources, self.half, self.part)
+        mine, theirs, first = self("P"), self.free(self("K"), "both"), self.core == 0
+        grads = jnp.stack([jnp.where(first, mine, theirs), jnp.where(first, theirs, mine)], axis=2)
+        grads = grads.reshape(self.replicas, self.sources, self.half, self.part)
         places = jnp.arange(self.half, dtype=jnp.bfloat16)[None, None, :]
         ours = (places < self("lengths")[:, :, None])[..., None]
         both = jnp.concatenate([jnp.where(ours, grads, 0), jnp.where(ours, 0, grads)], axis=3)
@@ -249,7 +235,7 @@
         return lax.ppermute(self.free(self("couple", part), "M" + str(part)), "dp", [(1, 2), (2, 1)])
 
     def F(self, part):
-        return lax.ppermute(self.free(self("M", part), "F" + str(part)), "dp", [(2, 3), (1, 0)])
+        return lax.ppermute(self.free(self("M", part), "F" + str(part)), "dp", [(0, 1), (1, 0), (2, 3), (3, 2)])
 
     def block(self, part):
         far = jnp.where(self.inner, self("M", part), self("F", part))
@@ -279,7 +265,11 @@
 
 
 def pair_body(*args):
-    return Plan(*args)("out")
+    plan = Plan(*args)
+    for name in FIRST:
+        kind = name.rstrip("0123456789")
+        plan(kind, int(name[len(kind) :])) if kind != name else plan(name)
+    return plan("out")
 
 
 def solution(mesh):

time: 92.9 us -> 91.9 us (0.989)
  starting transfers between devices: 37.5 us -> 45.7 us
  waiting for transfers between devices: 40.7 us -> 33.1 us
  matrix products: 6.87 us -> 5.73 us
    ppermute x4, waiting for transfers between devices: 18.3 us -> 6.7 us  [F(): lax.ppermute(self.free(self('M', part), 'F' + str(part)), 'dp', [(0, 1),...]
    ppermute x4, starting transfers between devices: 5.14 us -> 12.1 us  [F(): lax.ppermute(self.free(self('M', part), 'F' + str(part)), 'dp', [(0, 1),...]
    ppermute x21 -> x20, waiting for transfers between devices: 22.3 us -> 26.4 us  [crossed(): return lax.ppermute(value, axis, pairs)]
    ppermute x21 -> x20, starting transfers between devices: 23 us -> 24.7 us  [crossed(): return lax.ppermute(value, axis, pairs)]
    ppermute x4 -> x3, starting transfers between devices: 5.9 us -> 4.62 us  [shifted(): return lax.ppermute(value, axis, pairs)]
    another operation x2, other arithmetic: 1.32 us -> 0.18 us  [both(): jnp.stack([jnp.where(first, mine, theirs), jnp.where(first, theirs, mine)...]
  transfers between devices with their start and end apart: 33 -> 31, of which waited for: 10 -> 10; matrix products, arithmetic and copies ran while one was open for 14% -> 12% of each run, Pallas kernels for 0% -> 0%
where the time goes in v3:
time: 91.9 us; the launch traced here: 91.6 us
  starting transfers between devices  45.7 us (50%)
  waiting for transfers between devices  33.1 us (36%)
  matrix products  5.73 us (6%)
  other arithmetic  3.55 us (4%)
  local copies, waits for them, and re-layouts  3.03 us (3%)
    ppermute x20, waiting for transfers between devices, crossed(): return lax.ppermute(value, axis, pairs)  26.4 us
    ppermute x20, starting transfers between devices, crossed(): return lax.ppermute(value, axis, pairs)  24.7 us
    ppermute x4, starting transfers between devices, F(): lax.ppermute(self.free(self('M', part), 'F' + str(part)), 'dp', [(0, 1),...  12.1 us
    ppermute x4, waiting for transfers between devices, F(): lax.ppermute(self.free(self('M', part), 'F' + str(part)), 'dp', [(0, 1),...  6.7 us
    ppermute x3, starting transfers between devices, shifted(): return lax.ppermute(value, axis, pairs)  4.62 us
    dot_general x4, matrix products, total(): lax.dot_general(self('both'), block, (((0,), (0,)), ((), ())), preferred_...  4.59 us
    ppermute x4, starting transfers between devices, M(): lax.ppermute(self.free(self('couple', part), 'M' + str(part)), 'dp', [(1,...  4.21 us
    slice x2, local copies, waits for them, and re-layouts, upper(): return after(self.hidden[:, self.half:, low:high])  2.22 us
  transfers between devices with their start and end apart: 31, of which 10 were waited for; matrix products, arithmetic and copies ran while one was open for 12% of the time, Pallas kernels for 0%

profile of v3, /device:TPU:0, one launch (start us, length us, event | category | flops | bytes accessed | tf_op | source)
XLA Modules:
  0.0 91.6 jit_solution(2058328245384744101)
XLA Ops:
  0.0 3.0 %collective-permute-start = (f32[1,128]{1,0:T(1,128)}, f32[1,128]{1,0:T(1,128)S(1)}, u32[]{:S(2)}, u32[]{:S(2)}) collective-permute-start(f32[1,128]{1,0:T(1,128)} %param.5), channel_id=1, source_target_pairs={{0,16},{16,0},{1,17},{17,1},{2,18},{18,2},{3,19},{19,3},{4,20},{20... | collective-permute-start | bytes 1544 | tf_op jit(solution)/shard_map/ppermute | solution.py:30
  3.0 0.9 %slice.85 = bf16[4,64,256]{2,1,0:T(8,128)(2,1)S(1)} slice(bf16[4,128,1408]{2,1,0:T(8,128)(2,1)} %bitcast.106), slice={[0:4], [64:128], [0:256]} | slice | bytes 262144 | tf_op jit(solution)/shard_map/slice | solution.py:202
  4.0 2.0 %collective-permute-start.5 = (bf16[4,64,256]{2,1,0:T(8,128)(2,1)S(1)}, bf16[4,64,256]{2,1,0:T(8,128)(2,1)S(1)}, u32[]{:S(2)}, u32[]{:S(2)}) collective-permute-start(bf16[4,64,256]{2,1,0:T(8,128)(2,1)S(1)} %slice.85), channel_id=1, source_target_pairs={{0,2},{1,3},{2,0},{3,1},{4,6},{5,7},{6,4},{7,5},{8,10},{9,11},{10,... | collective-permute-start | bytes 393224 | tf_op jit(solution)/shard_map/ppermute | solution.py:35
  6.0 1.3 %fusion.54 = (bf16[4,64,384]{2,1,0:T(8,128)(2,1)S(1)}, bf16[4,64,384]{2,1,0:T(8,128)(2,1)S(1)}, bf16[4,64,384]{2,1,0:T(8,128)(2,1)S(1)}) fusion(bf16[4,128,1408]{2,1,0:T(8,128)(2,1)} %bitcast.107), kind=kLoop, calls=%fused_computation.108 | loop fusion | bytes 1179648 | tf_op jit(solution)/shard_map/slice | solution.py:202
  7.4 0.8 collective-permute-start.2
  8.3 1.3 %collective-permute-start.3 = (s32[1,128,1]{1,2,0:T(1,128)}, s32[1,128,1]{1,2,0:T(1,128)S(1)}, u32[]{:S(2)}, u32[]{:S(2)}) collective-permute-start(s32[1,128,1]{1,2,0:T(1,128)} %param.6), channel_id=1, source_target_pairs={{0,2},{1,3},{2,0},{3,1},{4,6},{5,7},{6,4},{7,5},{8,10},{9,11},{10,... | collective-permute-start | bytes 1544 | tf_op jit(solution)/shard_map/ppermute | solution.py:35
  9.7 0.4 convolution_convert_fusion
  10.1 3.7 %collective-permute-start.10 = (bf16[2,64,512]{2,1,0:T(8,128)(2,1)S(1)}, bf16[2,64,512]{2,1,0:T(8,128)(2,1)S(1)}, u32[]{:S(2)}, u32[]{:S(2)}) collective-permute-start(bf16[2,64,512]{2,1,0:T(8,128)(2,1)S(1)} %get-tuple-element.42), channel_id=1, source_target_pairs={{0,12},{4,8},{8,4},{12,0},{1,13},{5,9},{9,5},{13,1},{2,14},{6,10},... | collective-permute-start | bytes 393224 | tf_op jit(solution)/shard_map/ppermute | solution.py:35
  13.8 0.9 collective-permute-start.9
  14.7 0.7 collective-permute-start.16
  16.1 1.3 %collective-permute-start.6 = (bf16[272,256]{1,0:T(8,128)(2,1)S(1)}, bf16[272,256]{1,0:T(8,128)(2,1)S(1)}, u32[]{:S(2)}, u32[]{:S(2)}) collective-permute-start(bf16[272,256]{1,0:T(8,128)(2,1)S(1)} %pad_maximum_fusion.10), channel_id=1, source_target_pairs={{0,4},{4,0},{8,12},{12,8},{1,5},{5,1},{9,13},{13,9},{2,6},{6,2},{1... | collective-permute-start | bytes 417800 | tf_op jit(solution)/shard_map/ppermute | solution.py:35
  17.4 1.0 %collective-permute-done.10 = bf16[2,64,512]{2,1,0:T(8,128)(2,1)S(1)} collective-permute-done((bf16[2,64,512]{2,1,0:T(8,128)(2,1)S(1)}, bf16[2,64,512]{2,1,0:T(8,128)(2,1)S(1)}, u32[]{:S(2)}, u32[]{:S(2)}) %collective-permute-start.10) | collective-permute-done | bytes 131104 | tf_op jit(solution)/shard_map/ppermute | solution.py:35
  18.4 0.7 collective-permute-start.21
  19.1 5.7 %collective-permute-done.11 = bf16[2,64,512]{2,1,0:T(8,128)(2,1)S(1)} collective-permute-done((bf16[2,64,512]{2,1,0:T(8,128)(2,1)S(1)}, bf16[2,64,512]{2,1,0:T(8,128)(2,1)S(1)}, u32[]{:S(2)}, u32[]{:S(2)}) %collective-permute-start.11) | collective-permute-done | bytes 131104 | tf_op jit(solution)/shard_map/ppermute | solution.py:35
  25.0 0.8 collective-permute-start.12
  25.8 1.3 %collective-permute-start.26 = (bf16[4,64,384]{2,1,0:T(8,128)(2,1)S(1)}, bf16[4,64,384]{2,1,0:T(8,128)(2,1)S(1)}, u32[]{:S(2)}, u32[]{:S(2)}) collective-permute-start(bf16[4,64,384]{2,1,0:T(8,128)(2,1)S(1)} %get-tuple-element.26), channel_id=1, source_target_pairs={{0,2},{1,3},{2,0},{3,1},{4,6},{5,7},{6,4},{7,5},{8,10},{9,11},{10,... | collective-permute-start | bytes 589832 | tf_op jit(solution)/shard_map/ppermute | solution.py:35
  27.3 1.0 %collective-permute-start.17 = (bf16[256,384]{1,0:T(8,128)(2,1)S(1)}, bf16[256,384]{1,0:T(8,128)(2,1)S(1)}, u32[]{:S(2)}, u32[]{:S(2)}) collective-permute-start(bf16[256,384]{1,0:T(8,128)(2,1)S(1)} %bitcast.115), channel_id=1, source_target_pairs={{0,4},{4,0},{8,12},{12,8},{1,5},{5,1},{9,13},{13,9},{2,6},{6,2},{1... | collective-permute-start | bytes 589832 | tf_op jit(solution)/shard_map/ppermute | solution.py:35
  28.3 0.7 collective-permute-start.7
  29.0 0.2 fusion.3
  29.2 4.0 %collective-permute-start.22 = (bf16[256,384]{1,0:T(8,128)(2,1)S(1)}, bf16[256,384]{1,0:T(8,128)(2,1)S(1)}, u32[]{:S(2)}, u32[]{:S(2)}) collective-permute-start(bf16[256,384]{1,0:T(8,128)(2,1)S(1)} %bitcast.103), channel_id=1, source_target_pairs={{0,4},{4,0},{8,12},{12,8},{1,5},{5,1},{9,13},{13,9},{2,6},{6,2},{1... | collective-permute-start | bytes 589832 | tf_op jit(solution)/shard_map/ppermute | solution.py:35
  33.2 1.1 %collective-permute-done.12 = bf16[4,64,512]{2,1,0:T(8,128)(2,1)S(1)} collective-permute-done((bf16[4,64,512]{2,1,0:T(8,128)(2,1)S(1)}, bf16[4,64,512]{2,1,0:T(8,128)(2,1)S(1)}, u32[]{:S(2)}, u32[]{:S(2)}) %collective-permute-start.12) | collective-permute-done | bytes 262176 | tf_op jit(solution)/shard_map/ppermute | solution.py:35
  34.4 1.6 %collective-permute-start.13 = (bf16[4,2,64,512]{3,2,1,0:T(8,128)(2,1)S(1)}, bf16[4,2,64,512]{3,2,1,0:T(8,128)(2,1)S(1)}, u32[]{:S(2)}, u32[]{:S(2)}) collective-permute-start(bf16[4,2,64,512]{3,2,1,0:T(8,128)(2,1)S(1)} %pad_maximum_fusion.5), channel_id=1, source_target_pairs={{0,16},{16,0},{1,17},{17,1},{2,18},{18,2},{3,19},{19,3},{4,20},{20... | collective-permute-start | bytes 1572872 | tf_op jit(solution)/shard_map/ppermute | solution.py:30
  36.0 0.5 collective-permute-done.26
  36.7 1.7 %collective-permute-start.27 = (bf16[256,384]{1,0:T(8,128)(2,1)S(1)}, bf16[256,384]{1,0:T(8,128)(2,1)S(1)}, u32[]{:S(2)}, u32[]{:S(2)}) collective-permute-start(bf16[256,384]{1,0:T(8,128)(2,1)S(1)} %bitcast.112), channel_id=1, source_target_pairs={{0,4},{4,0},{8,12},{12,8},{1,5},{5,1},{9,13},{13,9},{2,6},{6,2},{1... | collective-permute-start | bytes 589832 | tf_op jit(solution)/shard_map/ppermute | solution.py:35
  38.4 0.4 collective-permute-start.8
  38.9 1.4 %collective-permute-start.18 = (bf16[512,384]{1,0:T(8,128)(2,1)S(1)}, bf16[512,384]{1,0:T(8,128)(2,1)}, u32[]{:S(2)}, u32[]{:S(2)}) collective-permute-start(bf16[512,384]{1,0:T(8,128)(2,1)S(1)} %pad_maximum_fusion.6), channel_id=1, source_target_pairs={{4,8},{8,4},{5,9},{9,5},{6,10},{10,6},{7,11},{11,7},{20,24},{24,20... | collective-permute-start | bytes 1179656 | tf_op jit(solution)/shard_map/ppermute | solution.py:235
  40.3 0.8 pad_maximum_fusion.7
  41.1 3.5 %collective-permute-done.27 = bf16[256,384]{1,0:T(8,128)(2,1)S(1)} collective-permute-done((bf16[256,384]{1,0:T(8,128)(2,1)S(1)}, bf16[256,384]{1,0:T(8,128)(2,1)S(1)}, u32[]{:S(2)}, u32[]{:S(2)}) %collective-permute-start.27) | collective-permute-done | bytes 196640 | tf_op jit(solution)/shard_map/ppermute | solution.py:35
  44.7 2.9 %collective-permute-done.8 = bf16[544,256]{1,0:T(8,128)(2,1)S(1)} collective-permute-done((bf16[544,256]{1,0:T(8,128)(2,1)S(1)}, bf16[544,256]{1,0:T(8,128)(2,1)S(1)}, u32[]{:S(2)}, u32[]{:S(2)}) %collective-permute-start.8) | collective-permute-done | bytes 278560 | tf_op jit(solution)/shard_map/ppermute | solution.py:238
  47.7 1.4 %collective-permute-start.23 = (bf16[512,384]{1,0:T(8,128)(2,1)}, bf16[512,384]{1,0:T(8,128)(2,1)}, u32[]{:S(2)}, u32[]{:S(2)}) collective-permute-start(bf16[512,384]{1,0:T(8,128)(2,1)} %pad_maximum_fusion.7), channel_id=1, source_target_pairs={{4,8},{8,4},{5,9},{9,5},{6,10},{10,6},{7,11},{11,7},{20,24},{24,20... | collective-permute-start | bytes 1179656 | tf_op jit(solution)/shard_map/ppermute | solution.py:235
  49.5 3.6 %collective-permute-start.19 = (bf16[512,384]{1,0:T(8,128)(2,1)}, bf16[512,384]{1,0:T(8,128)(2,1)S(1)}, u32[]{:S(2)}, u32[]{:S(2)}) collective-permute-start(bf16[512,384]{1,0:T(8,128)(2,1)} %collective-permute-done.18), channel_id=1, source_target_pairs={{0,4},{4,0},{8,12},{12,8},{1,5},{5,1},{9,13},{13,9},{2,6},{6,2},{1... | collective-permute-start | bytes 1179656 | tf_op jit(solution)/shard_map/ppermute | solution.py:238
  53.1 7.2 %collective-permute-start.24 = (bf16[512,384]{1,0:T(8,128)(2,1)}, bf16[512,384]{1,0:T(8,128)(2,1)S(1)}, u32[]{:S(2)}, u32[]{:S(2)}) collective-permute-start(bf16[512,384]{1,0:T(8,128)(2,1)} %collective-permute-done.23), channel_id=1, source_target_pairs={{0,4},{4,0},{8,12},{12,8},{1,5},{5,1},{9,13},{13,9},{2,6},{6,2},{1... | collective-permute-start | bytes 1179656 | tf_op jit(solution)/shard_map/ppermute | solution.py:238
  60.3 0.7 collective-permute-start.28
  61.2 0.3 bitcast_select_fusion.1
  61.4 0.7 fusion.52
  62.2 0.8 collective-permute-start.15
  63.1 1.3 %fusion.12 = f32[1024,384]{1,0:T(8,128)S(1)} fusion(bf16[512,384]{1,0:T(8,128)(2,1)S(1)} %broadcast_select_fusion.2, bf16[256,384]{1,0:T(8,128)(2,1)S(1)} %copy-done.4, bf16[256,384]{1,0:T(8,128)(2,1)S(1)} %bitcast.117, bf16[1024,512]{1,0:T(8,128)(2,1)S(1)} %get-tuple-element.35, bf16[1024,512]{1,0:T(8,128)(2,1)S(1)} %get-tuple-element.34), kind=kOutput, calls=%fused_computation.29 | convolution fusion | flops 811859968 | bytes 4456448 | tf_op jit(solution)/shard_map/dot_general | solution.py:251
  64.5 1.3 %collective-permute-start.20 = (bf16[512,384]{1,0:T(8,128)(2,1)S(1)}, bf16[512,384]{1,0:T(8,128)(2,1)S(1)}, u32[]{:S(2)}, u32[]{:S(2)}) collective-permute-start(bf16[512,384]{1,0:T(8,128)(2,1)S(1)} %slice.143), channel_id=1, source_target_pairs={{0,2},{1,3},{2,0},{3,1},{4,6},{5,7},{6,4},{7,5},{8,10},{9,11},{10,... | collective-permute-start | bytes 1179656 | tf_op jit(solution)/shard_map/ppermute | solution.py:35
  65.8 4.8 %collective-permute-done.15 = bf16[512,256]{1,0:T(8,128)(2,1)S(1)} collective-permute-done((bf16[512,256]{1,0:T(8,128)(2,1)S(1)}, bf16[512,256]{1,0:T(8,128)(2,1)S(1)}, u32[]{:S(2)}, u32[]{:S(2)}) %collective-permute-start.15) | collective-permute-done | bytes 262176 | tf_op jit(solution)/shard_map/ppermute | solution.py:35
  70.8 1.0 %collective-permute-start.29 = (bf16[512,384]{1,0:T(8,128)(2,1)S(1)}, bf16[512,384]{1,0:T(8,128)(2,1)S(1)}, u32[]{:S(2)}, u32[]{:S(2)}) collective-permute-start(bf16[512,384]{1,0:T(8,128)(2,1)S(1)} %collective-permute-done.28), channel_id=1, source_target_pairs={{0,4},{4,0},{8,12},{12,8},{1,5},{5,1},{9,13},{13,9},{2,6},{6,2},{1... | collective-permute-start | bytes 1179656 | tf_op jit(solution)/shard_map/ppermute | solution.py:238
  71.9 1.3 %fusion.51 = f32[1024,384]{1,0:T(8,128)S(1)} fusion(bf16[1024,384]{1,0:T(8,128)(2,1)S(1)} %pad_maximum_fusion.2, bf16[1024,512]{1,0:T(8,128)(2,1)S(1)} %get-tuple-element.35, bf16[1024,512]{1,0:T(8,128)(2,1)S(1)} %get-tuple-element.34), kind=kOutput, calls=%fused_computation.105 | convolution fusion | flops 809500672 | bytes 4456448 | tf_op jit(solution)/shard_map/dot_general | solution.py:251
  73.3 1.6 %collective-permute-start.25 = (bf16[512,384]{1,0:T(8,128)(2,1)S(1)}, bf16[512,384]{1,0:T(8,128)(2,1)S(1)}, u32[]{:S(2)}, u32[]{:S(2)}) collective-permute-start(bf16[512,384]{1,0:T(8,128)(2,1)S(1)} %slice.142), channel_id=1, source_target_pairs={{0,2},{1,3},{2,0},{3,1},{4,6},{5,7},{6,4},{7,5},{8,10},{9,11},{10,... | collective-permute-start | bytes 1179656 | tf_op jit(solution)/shard_map/ppermute | solution.py:35
  74.8 3.8 %collective-permute-done.29 = bf16[512,384]{1,0:T(8,128)(2,1)S(1)} collective-permute-done((bf16[512,384]{1,0:T(8,128)(2,1)S(1)}, bf16[512,384]{1,0:T(8,128)(2,1)S(1)}, u32[]{:S(2)}, u32[]{:S(2)}) %collective-permute-start.29) | collective-permute-done | bytes 393248 | tf_op jit(solution)/shard_map/ppermute | solution.py:238
  78.7 1.3 %fusion.18 = f32[1024,384]{1,0:T(8,128)S(1)} fusion(bf16[512,384]{1,0:T(8,128)(2,1)S(1)} %broadcast_select_fusion, bf16[256,384]{1,0:T(8,128)(2,1)S(1)} %collective-permute-done.27, bf16[256,384]{1,0:T(8,128)(2,1)S(1)} %bitcast.114, bf16[1024,512]{1,0:T(8,128)(2,1)S(1)} %get-tuple-element.35, bf16[1024,512]{1,0:T(8,128)(2,1)S(1)} %get-tuple-element.34), kind=kOutput, calls=%fused_computation.36 | convolution fusion | flops 811859968 | bytes 4456448 | tf_op jit(solution)/shard_map/dot_general | solution.py:251
  80.0 0.8 collective-permute-start.30
  80.9 5.7 %collective-permute-done.25 = bf16[512,384]{1,0:T(8,128)(2,1)S(1)} collective-permute-done((bf16[512,384]{1,0:T(8,128)(2,1)S(1)}, bf16[512,384]{1,0:T(8,128)(2,1)S(1)}, u32[]{:S(2)}, u32[]{:S(2)}) %collective-permute-start.25) | collective-permute-done | bytes 393248 | tf_op jit(solution)/shard_map/ppermute | solution.py:35
  86.7 4.1 %collective-permute-done.30 = bf16[512,384]{1,0:T(8,128)(2,1)S(1)} collective-permute-done((bf16[512,384]{1,0:T(8,128)(2,1)S(1)}, bf16[512,384]{1,0:T(8,128)(2,1)S(1)}, u32[]{:S(2)}, u32[]{:S(2)}) %collective-permute-start.30) | collective-permute-done | bytes 393248 | tf_op jit(solution)/shard_map/ppermute | solution.py:35
  90.8 0.8 fusion.33
  (83 shorter events, 3.3 us)
Async XLA Ops:
  0.0 9.7 %copy-start.2 = (bf16[1,128,2048]{2,1,0:T(8,128)(2,1)S(1)}, bf16[1,128,2048]{2,1,0:T(8,128)(2,1)}, u32[]{:S(2)}) copy-start(bf16[1,128,2048]{2,1,0:T(8,128)(2,1)} %param.4) | copy-start | bytes 1572868
  0.0 7.3 %collective-permute-start = (f32[1,128]{1,0:T(1,128)}, f32[1,128]{1,0:T(1,128)S(1)}, u32[]{:S(2)}, u32[]{:S(2)}) collective-permute-start(f32[1,128]{1,0:T(1,128)} %param.5), channel_id=1, source_target_pairs={{0,16},{16,0},{1,17},{17,1},{2,18},{18,2},{3,19},{19,3},{4,20},{20... | collective-permute-start | bytes 1544 | tf_op jit(solution)/shard_map/ppermute | solution.py:30
  3.0 4.4 %collective-permute-start.1 = (s32[1,128,1]{1,2,0:T(1,128)}, s32[1,128,1]{1,2,0:T(1,128)S(1)}, u32[]{:S(2)}, u32[]{:S(2)}) collective-permute-start(s32[1,128,1]{1,2,0:T(1,128)} %param.6), channel_id=1, source_target_pairs={{0,16},{16,0},{1,17},{17,1},{2,18},{18,2},{3,19},{19,3},{4,20},{20... | collective-permute-start | bytes 1544 | tf_op jit(solution)/shard_map/ppermute | solution.py:30
  4.0 11.9 %collective-permute-start.5 = (bf16[4,64,256]{2,1,0:T(8,128)(2,1)S(1)}, bf16[4,64,256]{2,1,0:T(8,128)(2,1)S(1)}, u32[]{:S(2)}, u32[]{:S(2)}) collective-permute-start(bf16[4,64,256]{2,1,0:T(8,128)(2,1)S(1)} %slice.85), channel_id=1, source_target_pairs={{0,2},{1,3},{2,0},{3,1},{4,6},{5,7},{6,4},{7,5},{8,10},{9,11},{10,... | collective-permute-start | bytes 393224 | tf_op jit(solution)/shard_map/ppermute | solution.py:35
  6.0 9.5 %copy-start.5 = (s32[1,128,1]{1,2,0:T(1,128)S(1)}, s32[1,128,1]{1,2,0:T(1,128)}, u32[]{:S(2)}) copy-start(s32[1,128,1]{1,2,0:T(1,128)} %param.6) | copy-start | bytes 1540
  6.0 9.9 %copy-start = (bf16[1,1,4,128,1408]{4,3,2,1,0:T(8,128)(2,1)S(1)}, bf16[1,1,4,128,1408]{4,3,2,1,0:T(8,128)(2,1)}, u32[]{:S(2)}) copy-start(bf16[1,1,4,128,1408]{4,3,2,1,0:T(8,128)(2,1)} %param.7) | copy-start | bytes 4325380
  7.4 6.4 %collective-permute-start.4 = (s32[1,128,1]{1,2,0:T(1,128)}, s32[1,128,1]{1,2,0:T(1,128)S(1)}, u32[]{:S(2)}, u32[]{:S(2)}) collective-permute-start(s32[1,128,1]{1,2,0:T(1,128)} %param.6), channel_id=1, source_target_pairs={{0,3},{1,2},{2,1},{3,0},{4,7},{5,6},{6,5},{7,4},{8,11},{9,10},{10,... | collective-permute-start | bytes 1544 | tf_op jit(solution)/shard_map/ppermute | solution.py:35
  7.4 7.3 %collective-permute-start.2 = (s32[1,128,1]{1,2,0:T(1,128)}, s32[1,128,1]{1,2,0:T(1,128)S(1)}, u32[]{:S(2)}, u32[]{:S(2)}) collective-permute-start(s32[1,128,1]{1,2,0:T(1,128)} %param.6), channel_id=1, source_target_pairs={{0,1},{1,0},{2,3},{3,2},{4,5},{5,4},{6,7},{7,6},{8,9},{9,8},{10,11... | collective-permute-start | bytes 1544 | tf_op jit(solution)/shard_map/ppermute | solution.py:35
  8.3 5.5 %collective-permute-start.3 = (s32[1,128,1]{1,2,0:T(1,128)}, s32[1,128,1]{1,2,0:T(1,128)S(1)}, u32[]{:S(2)}, u32[]{:S(2)}) collective-permute-start(s32[1,128,1]{1,2,0:T(1,128)} %param.6), channel_id=1, source_target_pairs={{0,2},{1,3},{2,0},{3,1},{4,6},{5,7},{6,4},{7,5},{8,10},{9,11},{10,... | collective-permute-start | bytes 1544 | tf_op jit(solution)/shard_map/ppermute | solution.py:35
  10.1 8.3 %collective-permute-start.10 = (bf16[2,64,512]{2,1,0:T(8,128)(2,1)S(1)}, bf16[2,64,512]{2,1,0:T(8,128)(2,1)S(1)}, u32[]{:S(2)}, u32[]{:S(2)}) collective-permute-start(bf16[2,64,512]{2,1,0:T(8,128)(2,1)S(1)} %get-tuple-element.42), channel_id=1, source_target_pairs={{0,12},{4,8},{8,4},{12,0},{1,13},{5,9},{9,5},{13,1},{2,14},{6,10},... | collective-permute-start | bytes 393224 | tf_op jit(solution)/shard_map/ppermute | solution.py:35
  13.8 11.1 %collective-permute-start.11 = (bf16[2,64,512]{2,1,0:T(8,128)(2,1)S(1)}, bf16[2,64,512]{2,1,0:T(8,128)(2,1)S(1)}, u32[]{:S(2)}, u32[]{:S(2)}) collective-permute-start(bf16[2,64,512]{2,1,0:T(8,128)(2,1)S(1)} %get-tuple-element.41), channel_id=1, source_target_pairs={{0,8},{4,12},{8,0},{12,4},{1,9},{5,13},{9,1},{13,5},{2,10},{6,14},... | collective-permute-start | bytes 393224 | tf_op jit(solution)/shard_map/ppermute | solution.py:35
  13.8 11.1 %collective-permute-start.9 = (bf16[2,64,512]{2,1,0:T(8,128)(2,1)S(1)}, bf16[2,64,512]{2,1,0:T(8,128)(2,1)S(1)}, u32[]{:S(2)}, u32[]{:S(2)}) collective-permute-start(bf16[2,64,512]{2,1,0:T(8,128)(2,1)S(1)} %get-tuple-element.43), channel_id=1, source_target_pairs={{0,4},{4,0},{8,12},{12,8},{1,5},{5,1},{9,13},{13,9},{2,6},{6,2},{1... | collective-permute-start | bytes 393224 | tf_op jit(solution)/shard_map/ppermute | solution.py:35
  14.7 12.4 %collective-permute-start.16 = (bf16[4,64,384]{2,1,0:T(8,128)(2,1)S(1)}, bf16[4,64,384]{2,1,0:T(8,128)(2,1)S(1)}, u32[]{:S(2)}, u32[]{:S(2)}) collective-permute-start(bf16[4,64,384]{2,1,0:T(8,128)(2,1)S(1)} %get-tuple-element.19), channel_id=1, source_target_pairs={{0,2},{1,3},{2,0},{3,1},{4,6},{5,7},{6,4},{7,5},{8,10},{9,11},{10,... | collective-permute-start | bytes 589832 | tf_op jit(solution)/shard_map/ppermute | solution.py:35
  16.1 12.1 %collective-permute-start.6 = (bf16[272,256]{1,0:T(8,128)(2,1)S(1)}, bf16[272,256]{1,0:T(8,128)(2,1)S(1)}, u32[]{:S(2)}, u32[]{:S(2)}) collective-permute-start(bf16[272,256]{1,0:T(8,128)(2,1)S(1)} %pad_maximum_fusion.10), channel_id=1, source_target_pairs={{0,4},{4,0},{8,12},{12,8},{1,5},{5,1},{9,13},{13,9},{2,6},{6,2},{1... | collective-permute-start | bytes 417800 | tf_op jit(solution)/shard_map/ppermute | solution.py:35
  18.4 10.6 %collective-permute-start.21 = (bf16[4,64,384]{2,1,0:T(8,128)(2,1)S(1)}, bf16[4,64,384]{2,1,0:T(8,128)(2,1)S(1)}, u32[]{:S(2)}, u32[]{:S(2)}) collective-permute-start(bf16[4,64,384]{2,1,0:T(8,128)(2,1)S(1)} %get-tuple-element.22), channel_id=1, source_target_pairs={{0,2},{1,3},{2,0},{3,1},{4,6},{5,7},{6,4},{7,5},{8,10},{9,11},{10,... | collective-permute-start | bytes 589832 | tf_op jit(solution)/shard_map/ppermute | solution.py:35
  25.0 9.3 %collective-permute-start.12 = (bf16[4,64,512]{2,1,0:T(8,128)(2,1)S(1)}, bf16[4,64,512]{2,1,0:T(8,128)(2,1)S(1)}, u32[]{:S(2)}, u32[]{:S(2)}) collective-permute-start(bf16[4,64,512]{2,1,0:T(8,128)(2,1)S(1)} %slice_bitcast_fusion), channel_id=1, source_target_pairs={{0,2},{1,3},{2,0},{3,1},{4,6},{5,7},{6,4},{7,5},{8,10},{9,11},{10,... | collective-permute-start | bytes 786440 | tf_op jit(solution)/shard_map/ppermute | solution.py:35
  25.8 10.7 %collective-permute-start.26 = (bf16[4,64,384]{2,1,0:T(8,128)(2,1)S(1)}, bf16[4,64,384]{2,1,0:T(8,128)(2,1)S(1)}, u32[]{:S(2)}, u32[]{:S(2)}) collective-permute-start(bf16[4,64,384]{2,1,0:T(8,128)(2,1)S(1)} %get-tuple-element.26), channel_id=1, source_target_pairs={{0,2},{1,3},{2,0},{3,1},{4,6},{5,7},{6,4},{7,5},{8,10},{9,11},{10,... | collective-permute-start | bytes 589832 | tf_op jit(solution)/shard_map/ppermute | solution.py:35
  27.3 11.5 %collective-permute-start.17 = (bf16[256,384]{1,0:T(8,128)(2,1)S(1)}, bf16[256,384]{1,0:T(8,128)(2,1)S(1)}, u32[]{:S(2)}, u32[]{:S(2)}) collective-permute-start(bf16[256,384]{1,0:T(8,128)(2,1)S(1)} %bitcast.115), channel_id=1, source_target_pairs={{0,4},{4,0},{8,12},{12,8},{1,5},{5,1},{9,13},{13,9},{2,6},{6,2},{1... | collective-permute-start | bytes 589832 | tf_op jit(solution)/shard_map/ppermute | solution.py:35
  28.3 10.1 %collective-permute-start.7 = (bf16[544,256]{1,0:T(8,128)(2,1)S(1)}, bf16[544,256]{1,0:T(8,128)(2,1)S(1)}, u32[]{:S(2)}, u32[]{:S(2)}) collective-permute-start(bf16[544,256]{1,0:T(8,128)(2,1)S(1)} %pad_maximum_fusion.9), channel_id=1, source_target_pairs={{4,8},{8,4},{5,9},{9,5},{6,10},{10,6},{7,11},{11,7},{20,24},{24,20... | collective-permute-start | bytes 835592 | tf_op jit(solution)/shard_map/ppermute | solution.py:235
  29.2 11.1 %collective-permute-start.22 = (bf16[256,384]{1,0:T(8,128)(2,1)S(1)}, bf16[256,384]{1,0:T(8,128)(2,1)S(1)}, u32[]{:S(2)}, u32[]{:S(2)}) collective-permute-start(bf16[256,384]{1,0:T(8,128)(2,1)S(1)} %bitcast.103), channel_id=1, source_target_pairs={{0,4},{4,0},{8,12},{12,8},{1,5},{5,1},{9,13},{13,9},{2,6},{6,2},{1... | collective-permute-start | bytes 589832 | tf_op jit(solution)/shard_map/ppermute | solution.py:35
  34.4 10.2 %collective-permute-start.13 = (bf16[4,2,64,512]{3,2,1,0:T(8,128)(2,1)S(1)}, bf16[4,2,64,512]{3,2,1,0:T(8,128)(2,1)S(1)}, u32[]{:S(2)}, u32[]{:S(2)}) collective-permute-start(bf16[4,2,64,512]{3,2,1,0:T(8,128)(2,1)S(1)} %pad_maximum_fusion.5), channel_id=1, source_target_pairs={{0,16},{16,0},{1,17},{17,1},{2,18},{18,2},{3,19},{19,3},{4,20},{20... | collective-permute-start | bytes 1572872 | tf_op jit(solution)/shard_map/ppermute | solution.py:30
  36.7 7.9 %collective-permute-start.27 = (bf16[256,384]{1,0:T(8,128)(2,1)S(1)}, bf16[256,384]{1,0:T(8,128)(2,1)S(1)}, u32[]{:S(2)}, u32[]{:S(2)}) collective-permute-start(bf16[256,384]{1,0:T(8,128)(2,1)S(1)} %bitcast.112), channel_id=1, source_target_pairs={{0,4},{4,0},{8,12},{12,8},{1,5},{5,1},{9,13},{13,9},{2,6},{6,2},{1... | collective-permute-start | bytes 589832 | tf_op jit(solution)/shard_map/ppermute | solution.py:35
  38.4 9.2 %collective-permute-start.8 = (bf16[544,256]{1,0:T(8,128)(2,1)S(1)}, bf16[544,256]{1,0:T(8,128)(2,1)S(1)}, u32[]{:S(2)}, u32[]{:S(2)}) collective-permute-start(bf16[544,256]{1,0:T(8,128)(2,1)S(1)} %collective-permute-done.7), channel_id=1, source_target_pairs={{0,4},{4,0},{8,12},{12,8},{1,5},{5,1},{9,13},{13,9},{2,6},{6,2},{1... | collective-permute-start | bytes 835592 | tf_op jit(solution)/shard_map/ppermute | solution.py:238
  38.8 8.9 %copy-start.3 = (bf16[256,384]{1,0:T(8,128)(2,1)}, bf16[256,384]{1,0:T(8,128)(2,1)S(1)}, u32[]{:S(2)}) copy-start(bf16[256,384]{1,0:T(8,128)(2,1)S(1)} %collective-permute-done.17) | copy-start | bytes 589828
  38.9 8.8 %collective-permute-start.18 = (bf16[512,384]{1,0:T(8,128)(2,1)S(1)}, bf16[512,384]{1,0:T(8,128)(2,1)}, u32[]{:S(2)}, u32[]{:S(2)}) collective-permute-start(bf16[512,384]{1,0:T(8,128)(2,1)S(1)} %pad_maximum_fusion.6), channel_id=1, source_target_pairs={{4,8},{8,4},{5,9},{9,5},{6,10},{10,6},{7,11},{11,7},{20,24},{24,20... | collective-permute-start | bytes 1179656 | tf_op jit(solution)/shard_map/ppermute | solution.py:235
  44.7 16.3 %collective-permute-start.14 = (bf16[4,2,64,512]{3,2,1,0:T(8,128)(2,1)S(1)}, bf16[4,2,64,512]{3,2,1,0:T(8,128)(2,1)S(1)}, u32[]{:S(2)}, u32[]{:S(2)}) collective-permute-start(bf16[4,2,64,512]{3,2,1,0:T(8,128)(2,1)S(1)} %collective-permute-done.13), channel_id=1, source_target_pairs={{0,1},{1,0},{2,3},{3,2},{4,5},{5,4},{6,7},{7,6},{8,9},{9,8},{10,11... | collective-permute-start | bytes 1572872 | tf_op jit(solution)/shard_map/ppermute | solution.py:35
  47.7 5.4 %collective-permute-start.23 = (bf16[512,384]{1,0:T(8,128)(2,1)}, bf16[512,384]{1,0:T(8,128)(2,1)}, u32[]{:S(2)}, u32[]{:S(2)}) collective-permute-start(bf16[512,384]{1,0:T(8,128)(2,1)} %pad_maximum_fusion.7), channel_id=1, source_target_pairs={{4,8},{8,4},{5,9},{9,5},{6,10},{10,6},{7,11},{11,7},{20,24},{24,20... | collective-permute-start | bytes 1179656 | tf_op jit(solution)/shard_map/ppermute | solution.py:235
  49.5 13.5 %collective-permute-start.19 = (bf16[512,384]{1,0:T(8,128)(2,1)}, bf16[512,384]{1,0:T(8,128)(2,1)S(1)}, u32[]{:S(2)}, u32[]{:S(2)}) collective-permute-start(bf16[512,384]{1,0:T(8,128)(2,1)} %collective-permute-done.18), channel_id=1, source_target_pairs={{0,4},{4,0},{8,12},{12,8},{1,5},{5,1},{9,13},{13,9},{2,6},{6,2},{1... | collective-permute-start | bytes 1179656 | tf_op jit(solution)/shard_map/ppermute | solution.py:238
  53.1 18.6 %collective-permute-start.24 = (bf16[512,384]{1,0:T(8,128)(2,1)}, bf16[512,384]{1,0:T(8,128)(2,1)S(1)}, u32[]{:S(2)}, u32[]{:S(2)}) collective-permute-start(bf16[512,384]{1,0:T(8,128)(2,1)} %collective-permute-done.23), channel_id=1, source_target_pairs={{0,4},{4,0},{8,12},{12,8},{1,5},{5,1},{9,13},{13,9},{2,6},{6,2},{1... | collective-permute-start | bytes 1179656 | tf_op jit(solution)/shard_map/ppermute | solution.py:238
  60.3 10.5 %collective-permute-start.28 = (bf16[512,384]{1,0:T(8,128)(2,1)S(1)}, bf16[512,384]{1,0:T(8,128)(2,1)S(1)}, u32[]{:S(2)}, u32[]{:S(2)}) collective-permute-start(bf16[512,384]{1,0:T(8,128)(2,1)S(1)} %pad_maximum_fusion.8), channel_id=1, source_target_pairs={{4,8},{8,4},{5,9},{9,5},{6,10},{10,6},{7,11},{11,7},{20,24},{24,20... | collective-permute-start | bytes 1179656 | tf_op jit(solution)/shard_map/ppermute | solution.py:235
  62.2 0.9 %copy-start.4 = (bf16[256,384]{1,0:T(8,128)(2,1)S(1)}, bf16[256,384]{1,0:T(8,128)(2,1)}, u32[]{:S(2)}) copy-start(bf16[256,384]{1,0:T(8,128)(2,1)} %copy-done.3) | copy-start | bytes 589828
  62.2 8.4 %collective-permute-start.15 = (bf16[512,256]{1,0:T(8,128)(2,1)S(1)}, bf16[512,256]{1,0:T(8,128)(2,1)S(1)}, u32[]{:S(2)}, u32[]{:S(2)}) collective-permute-start(bf16[512,256]{1,0:T(8,128)(2,1)S(1)} %slice.144), channel_id=1, source_target_pairs={{0,2},{1,3},{2,0},{3,1},{4,6},{5,7},{6,4},{7,5},{8,10},{9,11},{10,... | collective-permute-start | bytes 786440 | tf_op jit(solution)/shard_map/ppermute | solution.py:35
  64.5 16.3 %collective-permute-start.20 = (bf16[512,384]{1,0:T(8,128)(2,1)S(1)}, bf16[512,384]{1,0:T(8,128)(2,1)S(1)}, u32[]{:S(2)}, u32[]{:S(2)}) collective-permute-start(bf16[512,384]{1,0:T(8,128)(2,1)S(1)} %slice.143), channel_id=1, source_target_pairs={{0,2},{1,3},{2,0},{3,1},{4,6},{5,7},{6,4},{7,5},{8,10},{9,11},{10,... | collective-permute-start | bytes 1179656 | tf_op jit(solution)/shard_map/ppermute | solution.py:35
  70.8 7.8 %collective-permute-start.29 = (bf16[512,384]{1,0:T(8,128)(2,1)S(1)}, bf16[512,384]{1,0:T(8,128)(2,1)S(1)}, u32[]{:S(2)}, u32[]{:S(2)}) collective-permute-start(bf16[512,384]{1,0:T(8,128)(2,1)S(1)} %collective-permute-done.28), channel_id=1, source_target_pairs={{0,4},{4,0},{8,12},{12,8},{1,5},{5,1},{9,13},{13,9},{2,6},{6,2},{1... | collective-permute-start | bytes 1179656 | tf_op jit(solution)/shard_map/ppermute | solution.py:238
  73.3 13.3 %collective-permute-start.25 = (bf16[512,384]{1,0:T(8,128)(2,1)S(1)}, bf16[512,384]{1,0:T(8,128)(2,1)S(1)}, u32[]{:S(2)}, u32[]{:S(2)}) collective-permute-start(bf16[512,384]{1,0:T(8,128)(2,1)S(1)} %slice.142), channel_id=1, source_target_pairs={{0,2},{1,3},{2,0},{3,1},{4,6},{5,7},{6,4},{7,5},{8,10},{9,11},{10,... | collective-permute-start | bytes 1179656 | tf_op jit(solution)/shard_map/ppermute | solution.py:35
  80.0 10.8 %collective-permute-start.30 = (bf16[512,384]{1,0:T(8,128)(2,1)S(1)}, bf16[512,384]{1,0:T(8,128)(2,1)S(1)}, u32[]{:S(2)}, u32[]{:S(2)}) collective-permute-start(bf16[512,384]{1,0:T(8,128)(2,1)S(1)} %slice.141), channel_id=1, source_target_pairs={{0,2},{1,3},{2,0},{3,1},{4,6},{5,7},{6,4},{7,5},{8,10},{9,11},{10,... | collective-permute-start | bytes 1179656 | tf_op jit(solution)/shard_map/ppermute | solution.py:35
  86.7 4.1 %copy-start.1 = (bf16[1,512,1408]{2,1,0:T(8,128)(2,1)}, bf16[1,512,1408]{2,1,0:T(8,128)(2,1)S(1)}, u32[]{:S(2)}) copy-start(bf16[1,512,1408]{2,1,0:T(8,128)(2,1)S(1)} %fusion.31) | copy-start | bytes 4325380

commit v4 on v3

--- a/solution.py
+++ b/solution.py
@@ -235,7 +235,7 @@
         return lax.ppermute(self.free(self("couple", part), "M" + str(part)), "dp", [(1, 2), (2, 1)])
 
     def F(self, part):
-        return lax.ppermute(self.free(self("M", part), "F" + str(part)), "dp", [(0, 1), (1, 0), (2, 3), (3, 2)])
+        return lax.ppermute(self.free(self("M", part), "F" + str(part)), "dp", [(2, 3), (1, 0)] + ([(0, 1), (3, 2)] if part in (0, 2, 3) else []))
 
     def block(self, part):
         far = jnp.where(self.inner, self("M", part), self("F", part))

time: 91.9 us -> 91.9 us (level)
  starting transfers between devices: 45.7 us -> 47.2 us
  waiting for transfers between devices: 33.1 us -> 31.7 us
    ppermute x4, starting transfers between devices: 12.1 us -> 14.1 us  [F(): lax.ppermute(self.free(self('M', part), 'F' + str(part)), 'dp', [(2, 3),...]
    ppermute x20, waiting for transfers between devices: 26.4 us -> 24.5 us  [crossed(): return lax.ppermute(value, axis, pairs)]
  transfers between devices with their start and end apart: 31 -> 31, of which waited for: 10 -> 11; matrix products, arithmetic and copies ran while one was open for 12% -> 12% of each run, Pallas kernels for 0% -> 0%
where the time goes in v4:
time: 91.9 us; the launch traced here: 91.6 us
  starting transfers between devices  47.2 us (51%)
  waiting for transfers between devices  31.7 us (34%)
  matrix products  5.73 us (6%)
  other arithmetic  3.55 us (4%)
  local copies, waits for them, and re-layouts  2.97 us (3%)
    ppermute x20, waiting for transfers between devices, crossed(): return lax.ppermute(value, axis, pairs)  24.5 us
    ppermute x20, starting transfers between devices, crossed(): return lax.ppermute(value, axis, pairs)  24.3 us
    ppermute x4, starting transfers between devices, F(): lax.ppermute(self.free(self('M', part), 'F' + str(part)), 'dp', [(2, 3),...  14.1 us
    ppermute x4, waiting for transfers between devices, F(): lax.ppermute(self.free(self('M', part), 'F' + str(part)), 'dp', [(2, 3),...  7.14 us
    ppermute x3, starting transfers between devices, shifted(): return lax.ppermute(value, axis, pairs)  4.62 us
    dot_general x4, matrix products, total(): lax.dot_general(self('both'), block, (((0,), (0,)), ((), ())), preferred_...  4.59 us
    ppermute x4, starting transfers between devices, M(): lax.ppermute(self.free(self('couple', part), 'M' + str(part)), 'dp', [(1,...  4.21 us
    slice x2, local copies, waits for them, and re-layouts, upper(): return after(self.hidden[:, self.half:, low:high])  2.22 us
  transfers between devices with their start and end apart: 31, of which 11 were waited for; matrix products, arithmetic and copies ran while one was open for 12% of the time, Pallas kernels for 0%

profile of v4, /device:TPU:0, one launch (start us, length us, event | category | flops | bytes accessed | tf_op | source)
XLA Modules:
  0.0 91.6 jit_solution(9557052771254232867)
XLA Ops:
  0.0 3.0 %collective-permute-start = (f32[1,128]{1,0:T(1,128)}, f32[1,128]{1,0:T(1,128)S(1)}, u32[]{:S(2)}, u32[]{:S(2)}) collective-permute-start(f32[1,128]{1,0:T(1,128)} %param.5), channel_id=1, source_target_pairs={{0,16},{16,0},{1,17},{17,1},{2,18},{18,2},{3,19},{19,3},{4,20},{20... | collective-permute-start | bytes 1544 | tf_op jit(solution)/shard_map/ppermute | solution.py:30
  3.0 0.9 %slice.85 = bf16[4,64,256]{2,1,0:T(8,128)(2,1)S(1)} slice(bf16[4,128,1408]{2,1,0:T(8,128)(2,1)} %bitcast.106), slice={[0:4], [64:128], [0:256]} | slice | bytes 262144 | tf_op jit(solution)/shard_map/slice | solution.py:202
  4.0 2.0 %collective-permute-start.5 = (bf16[4,64,256]{2,1,0:T(8,128)(2,1)S(1)}, bf16[4,64,256]{2,1,0:T(8,128)(2,1)S(1)}, u32[]{:S(2)}, u32[]{:S(2)}) collective-permute-start(bf16[4,64,256]{2,1,0:T(8,128)(2,1)S(1)} %slice.85), channel_id=1, source_target_pairs={{0,2},{1,3},{2,0},{3,1},{4,6},{5,7},{6,4},{7,5},{8,10},{9,11},{10,... | collective-permute-start | bytes 393224 | tf_op jit(solution)/shard_map/ppermute | solution.py:35
  6.0 1.3 %fusion.54 = (bf16[4,64,384]{2,1,0:T(8,128)(2,1)S(1)}, bf16[4,64,384]{2,1,0:T(8,128)(2,1)S(1)}, bf16[4,64,384]{2,1,0:T(8,128)(2,1)S(1)}) fusion(bf16[4,128,1408]{2,1,0:T(8,128)(2,1)} %bitcast.107), kind=kLoop, calls=%fused_computation.108 | loop fusion | bytes 1179648 | tf_op jit(solution)/shard_map/slice | solution.py:202
  7.4 0.8 collective-permute-start.2
  8.3 1.3 %collective-permute-start.3 = (s32[1,128,1]{1,2,0:T(1,128)}, s32[1,128,1]{1,2,0:T(1,128)S(1)}, u32[]{:S(2)}, u32[]{:S(2)}) collective-permute-start(s32[1,128,1]{1,2,0:T(1,128)} %param.6), channel_id=1, source_target_pairs={{0,2},{1,3},{2,0},{3,1},{4,6},{5,7},{6,4},{7,5},{8,10},{9,11},{10,... | collective-permute-start | bytes 1544 | tf_op jit(solution)/shard_map/ppermute | solution.py:35
  9.7 0.4 convolution_convert_fusion
  10.1 3.7 %collective-permute-start.10 = (bf16[2,64,512]{2,1,0:T(8,128)(2,1)S(1)}, bf16[2,64,512]{2,1,0:T(8,128)(2,1)S(1)}, u32[]{:S(2)}, u32[]{:S(2)}) collective-permute-start(bf16[2,64,512]{2,1,0:T(8,128)(2,1)S(1)} %get-tuple-element.42), channel_id=1, source_target_pairs={{0,12},{4,8},{8,4},{12,0},{1,13},{5,9},{9,5},{13,1},{2,14},{6,10},... | collective-permute-start | bytes 393224 | tf_op jit(solution)/shard_map/ppermute | solution.py:35
  13.8 0.9 collective-permute-start.9
  14.7 0.7 collective-permute-start.16
  16.1 1.3 %collective-permute-start.6 = (bf16[272,256]{1,0:T(8,128)(2,1)S(1)}, bf16[272,256]{1,0:T(8,128)(2,1)S(1)}, u32[]{:S(2)}, u32[]{:S(2)}) collective-permute-start(bf16[272,256]{1,0:T(8,128)(2,1)S(1)} %pad_maximum_fusion.10), channel_id=1, source_target_pairs={{0,4},{4,0},{8,12},{12,8},{1,5},{5,1},{9,13},{13,9},{2,6},{6,2},{1... | collective-permute-start | bytes 417800 | tf_op jit(solution)/shard_map/ppermute | solution.py:35
  17.4 1.0 %collective-permute-done.10 = bf16[2,64,512]{2,1,0:T(8,128)(2,1)S(1)} collective-permute-done((bf16[2,64,512]{2,1,0:T(8,128)(2,1)S(1)}, bf16[2,64,512]{2,1,0:T(8,128)(2,1)S(1)}, u32[]{:S(2)}, u32[]{:S(2)}) %collective-permute-start.10) | collective-permute-done | bytes 131104 | tf_op jit(solution)/shard_map/ppermute | solution.py:35
  18.4 0.7 collective-permute-start.21
  19.1 5.7 %collective-permute-done.11 = bf16[2,64,512]{2,1,0:T(8,128)(2,1)S(1)} collective-permute-done((bf16[2,64,512]{2,1,0:T(8,128)(2,1)S(1)}, bf16[2,64,512]{2,1,0:T(8,128)(2,1)S(1)}, u32[]{:S(2)}, u32[]{:S(2)}) %collective-permute-start.11) | collective-permute-done | bytes 131104 | tf_op jit(solution)/shard_map/ppermute | solution.py:35
  25.0 0.8 collective-permute-start.12
  25.8 1.3 %collective-permute-start.26 = (bf16[4,64,384]{2,1,0:T(8,128)(2,1)S(1)}, bf16[4,64,384]{2,1,0:T(8,128)(2,1)S(1)}, u32[]{:S(2)}, u32[]{:S(2)}) collective-permute-start(bf16[4,64,384]{2,1,0:T(8,128)(2,1)S(1)} %get-tuple-element.26), channel_id=1, source_target_pairs={{0,2},{1,3},{2,0},{3,1},{4,6},{5,7},{6,4},{7,5},{8,10},{9,11},{10,... | collective-permute-start | bytes 589832 | tf_op jit(solution)/shard_map/ppermute | solution.py:35
  27.3 1.0 %collective-permute-start.17 = (bf16[256,384]{1,0:T(8,128)(2,1)S(1)}, bf16[256,384]{1,0:T(8,128)(2,1)S(1)}, u32[]{:S(2)}, u32[]{:S(2)}) collective-permute-start(bf16[256,384]{1,0:T(8,128)(2,1)S(1)} %bitcast.115), channel_id=1, source_target_pairs={{0,4},{4,0},{8,12},{12,8},{1,5},{5,1},{9,13},{13,9},{2,6},{6,2},{1... | collective-permute-start | bytes 589832 | tf_op jit(solution)/shard_map/ppermute | solution.py:35
  28.3 0.7 collective-permute-start.7
  29.2 4.0 %collective-permute-start.22 = (bf16[256,384]{1,0:T(8,128)(2,1)S(1)}, bf16[256,384]{1,0:T(8,128)(2,1)S(1)}, u32[]{:S(2)}, u32[]{:S(2)}) collective-permute-start(bf16[256,384]{1,0:T(8,128)(2,1)S(1)} %bitcast.103), channel_id=1, source_target_pairs={{0,4},{4,0},{8,12},{12,8},{1,5},{5,1},{9,13},{13,9},{2,6},{6,2},{1... | collective-permute-start | bytes 589832 | tf_op jit(solution)/shard_map/ppermute | solution.py:35
  33.2 1.1 %collective-permute-done.12 = bf16[4,64,512]{2,1,0:T(8,128)(2,1)S(1)} collective-permute-done((bf16[4,64,512]{2,1,0:T(8,128)(2,1)S(1)}, bf16[4,64,512]{2,1,0:T(8,128)(2,1)S(1)}, u32[]{:S(2)}, u32[]{:S(2)}) %collective-permute-start.12) | collective-permute-done | bytes 262176 | tf_op jit(solution)/shard_map/ppermute | solution.py:35
  34.4 1.6 %collective-permute-start.13 = (bf16[4,2,64,512]{3,2,1,0:T(8,128)(2,1)S(1)}, bf16[4,2,64,512]{3,2,1,0:T(8,128)(2,1)S(1)}, u32[]{:S(2)}, u32[]{:S(2)}) collective-permute-start(bf16[4,2,64,512]{3,2,1,0:T(8,128)(2,1)S(1)} %pad_maximum_fusion.5), channel_id=1, source_target_pairs={{0,16},{16,0},{1,17},{17,1},{2,18},{18,2},{3,19},{19,3},{4,20},{20... | collective-permute-start | bytes 1572872 | tf_op jit(solution)/shard_map/ppermute | solution.py:30
  36.0 0.5 collective-permute-done.26
  36.7 1.7 %collective-permute-start.27 = (bf16[256,384]{1,0:T(8,128)(2,1)S(1)}, bf16[256,384]{1,0:T(8,128)(2,1)S(1)}, u32[]{:S(2)}, u32[]{:S(2)}) collective-permute-start(bf16[256,384]{1,0:T(8,128)(2,1)S(1)} %bitcast.112), channel_id=1, source_target_pairs={{0,4},{4,0},{8,12},{12,8},{1,5},{5,1},{9,13},{13,9},{2,6},{6,2},{1... | collective-permute-start | bytes 589832 | tf_op jit(solution)/shard_map/ppermute | solution.py:35
  38.4 0.4 collective-permute-start.8
  38.9 1.4 %collective-permute-start.18 = (bf16[512,384]{1,0:T(8,128)(2,1)S(1)}, bf16[512,384]{1,0:T(8,128)(2,1)}, u32[]{:S(2)}, u32[]{:S(2)}) collective-permute-start(bf16[512,384]{1,0:T(8,128)(2,1)S(1)} %pad_maximum_fusion.6), channel_id=1, source_target_pairs={{4,8},{8,4},{5,9},{9,5},{6,10},{10,6},{7,11},{11,7},{20,24},{24,20... | collective-permute-start | bytes 1179656 | tf_op jit(solution)/shard_map/ppermute | solution.py:235
  40.3 0.8 pad_maximum_fusion.7
  41.1 3.5 %collective-permute-done.27 = bf16[256,384]{1,0:T(8,128)(2,1)S(1)} collective-permute-done((bf16[256,384]{1,0:T(8,128)(2,1)S(1)}, bf16[256,384]{1,0:T(8,128)(2,1)S(1)}, u32[]{:S(2)}, u32[]{:S(2)}) %collective-permute-start.27) | collective-permute-done | bytes 196640 | tf_op jit(solution)/shard_map/ppermute | solution.py:35
  44.7 2.9 %collective-permute-done.8 = bf16[544,256]{1,0:T(8,128)(2,1)S(1)} collective-permute-done((bf16[544,256]{1,0:T(8,128)(2,1)S(1)}, bf16[544,256]{1,0:T(8,128)(2,1)S(1)}, u32[]{:S(2)}, u32[]{:S(2)}) %collective-permute-start.8) | collective-permute-done | bytes 278560 | tf_op jit(solution)/shard_map/ppermute | solution.py:238
  47.7 1.4 %collective-permute-start.23 = (bf16[512,384]{1,0:T(8,128)(2,1)}, bf16[512,384]{1,0:T(8,128)(2,1)}, u32[]{:S(2)}, u32[]{:S(2)}) collective-permute-start(bf16[512,384]{1,0:T(8,128)(2,1)} %pad_maximum_fusion.7), channel_id=1, source_target_pairs={{4,8},{8,4},{5,9},{9,5},{6,10},{10,6},{7,11},{11,7},{20,24},{24,20... | collective-permute-start | bytes 1179656 | tf_op jit(solution)/shard_map/ppermute | solution.py:235
  49.5 1.3 %collective-permute-start.19 = (bf16[512,384]{1,0:T(8,128)(2,1)}, bf16[512,384]{1,0:T(8,128)(2,1)S(1)}, u32[]{:S(2)}, u32[]{:S(2)}) collective-permute-start(bf16[512,384]{1,0:T(8,128)(2,1)} %collective-permute-done.18), channel_id=1, source_target_pairs={{8,12},{4,0},{9,13},{5,1},{10,14},{6,2},{11,15},{7,3},{24,28},{20,... | collective-permute-start | bytes 1179656 | tf_op jit(solution)/shard_map/ppermute | solution.py:238
  50.8 9.5 %collective-permute-start.24 = (bf16[512,384]{1,0:T(8,128)(2,1)}, bf16[512,384]{1,0:T(8,128)(2,1)S(1)}, u32[]{:S(2)}, u32[]{:S(2)}) collective-permute-start(bf16[512,384]{1,0:T(8,128)(2,1)} %collective-permute-done.23), channel_id=1, source_target_pairs={{8,12},{4,0},{0,4},{12,8},{9,13},{5,1},{1,5},{13,9},{10,14},{6,2},... | collective-permute-start | bytes 1179656 | tf_op jit(solution)/shard_map/ppermute | solution.py:238
  60.3 0.7 collective-permute-start.28
  61.2 0.3 bitcast_select_fusion.1
  61.4 0.7 fusion.52
  62.2 0.8 collective-permute-start.15
  63.0 1.2 %collective-permute-done.19 = bf16[512,384]{1,0:T(8,128)(2,1)S(1)} collective-permute-done((bf16[512,384]{1,0:T(8,128)(2,1)}, bf16[512,384]{1,0:T(8,128)(2,1)S(1)}, u32[]{:S(2)}, u32[]{:S(2)}) %collective-permute-start.19) | collective-permute-done | bytes 393248 | tf_op jit(solution)/shard_map/ppermute | solution.py:238
  64.2 1.3 %fusion.12 = f32[1024,384]{1,0:T(8,128)S(1)} fusion(bf16[512,384]{1,0:T(8,128)(2,1)S(1)} %broadcast_select_fusion.2, bf16[256,384]{1,0:T(8,128)(2,1)S(1)} %copy-done.4, bf16[256,384]{1,0:T(8,128)(2,1)S(1)} %bitcast.117, bf16[1024,512]{1,0:T(8,128)(2,1)S(1)} %get-tuple-element.35, bf16[1024,512]{1,0:T(8,128)(2,1)S(1)} %get-tuple-element.34), kind=kOutput, calls=%fused_computation.29 | convolution fusion | flops 811859968 | bytes 4456448 | tf_op jit(solution)/shard_map/dot_general | solution.py:251
  65.6 0.8 collective-permute-start.20
  66.4 3.8 %collective-permute-done.15 = bf16[512,256]{1,0:T(8,128)(2,1)S(1)} collective-permute-done((bf16[512,256]{1,0:T(8,128)(2,1)S(1)}, bf16[512,256]{1,0:T(8,128)(2,1)S(1)}, u32[]{:S(2)}, u32[]{:S(2)}) %collective-permute-start.15) | collective-permute-done | bytes 262176 | tf_op jit(solution)/shard_map/ppermute | solution.py:35
  70.3 2.9 %collective-permute-start.29 = (bf16[512,384]{1,0:T(8,128)(2,1)S(1)}, bf16[512,384]{1,0:T(8,128)(2,1)S(1)}, u32[]{:S(2)}, u32[]{:S(2)}) collective-permute-start(bf16[512,384]{1,0:T(8,128)(2,1)S(1)} %collective-permute-done.28), channel_id=1, source_target_pairs={{8,12},{4,0},{0,4},{12,8},{9,13},{5,1},{1,5},{13,9},{10,14},{6,2},... | collective-permute-start | bytes 1179656 | tf_op jit(solution)/shard_map/ppermute | solution.py:238
  73.4 1.3 %fusion.51 = f32[1024,384]{1,0:T(8,128)S(1)} fusion(bf16[1024,384]{1,0:T(8,128)(2,1)S(1)} %pad_maximum_fusion.2, bf16[1024,512]{1,0:T(8,128)(2,1)S(1)} %get-tuple-element.35, bf16[1024,512]{1,0:T(8,128)(2,1)S(1)} %get-tuple-element.34), kind=kOutput, calls=%fused_computation.105 | convolution fusion | flops 809500672 | bytes 4456448 | tf_op jit(solution)/shard_map/dot_general | solution.py:251
  74.8 1.2 %collective-permute-start.25 = (bf16[512,384]{1,0:T(8,128)(2,1)S(1)}, bf16[512,384]{1,0:T(8,128)(2,1)S(1)}, u32[]{:S(2)}, u32[]{:S(2)}) collective-permute-start(bf16[512,384]{1,0:T(8,128)(2,1)S(1)} %slice.142), channel_id=1, source_target_pairs={{0,2},{1,3},{2,0},{3,1},{4,6},{5,7},{6,4},{7,5},{8,10},{9,11},{10,... | collective-permute-start | bytes 1179656 | tf_op jit(solution)/shard_map/ppermute | solution.py:35
  76.0 3.1 %collective-permute-done.29 = bf16[512,384]{1,0:T(8,128)(2,1)S(1)} collective-permute-done((bf16[512,384]{1,0:T(8,128)(2,1)S(1)}, bf16[512,384]{1,0:T(8,128)(2,1)S(1)}, u32[]{:S(2)}, u32[]{:S(2)}) %collective-permute-start.29) | collective-permute-done | bytes 393248 | tf_op jit(solution)/shard_map/ppermute | solution.py:238
  79.1 1.3 %fusion.18 = f32[1024,384]{1,0:T(8,128)S(1)} fusion(bf16[512,384]{1,0:T(8,128)(2,1)S(1)} %broadcast_select_fusion, bf16[256,384]{1,0:T(8,128)(2,1)S(1)} %collective-permute-done.27, bf16[256,384]{1,0:T(8,128)(2,1)S(1)} %bitcast.114, bf16[1024,512]{1,0:T(8,128)(2,1)S(1)} %get-tuple-element.35, bf16[1024,512]{1,0:T(8,128)(2,1)S(1)} %get-tuple-element.34), kind=kOutput, calls=%fused_computation.36 | convolution fusion | flops 811859968 | bytes 4456448 | tf_op jit(solution)/shard_map/dot_general | solution.py:251
  80.4 1.2 %collective-permute-start.30 = (bf16[512,384]{1,0:T(8,128)(2,1)S(1)}, bf16[512,384]{1,0:T(8,128)(2,1)S(1)}, u32[]{:S(2)}, u32[]{:S(2)}) collective-permute-start(bf16[512,384]{1,0:T(8,128)(2,1)S(1)} %slice.141), channel_id=1, source_target_pairs={{0,2},{1,3},{2,0},{3,1},{4,6},{5,7},{6,4},{7,5},{8,10},{9,11},{10,... | collective-permute-start | bytes 1179656 | tf_op jit(solution)/shard_map/ppermute | solution.py:35
  81.8 4.8 %collective-permute-done.25 = bf16[512,384]{1,0:T(8,128)(2,1)S(1)} collective-permute-done((bf16[512,384]{1,0:T(8,128)(2,1)S(1)}, bf16[512,384]{1,0:T(8,128)(2,1)S(1)}, u32[]{:S(2)}, u32[]{:S(2)}) %collective-permute-start.25) | collective-permute-done | bytes 393248 | tf_op jit(solution)/shard_map/ppermute | solution.py:35
  86.7 4.1 %collective-permute-done.30 = bf16[512,384]{1,0:T(8,128)(2,1)S(1)} collective-permute-done((bf16[512,384]{1,0:T(8,128)(2,1)S(1)}, bf16[512,384]{1,0:T(8,128)(2,1)S(1)}, u32[]{:S(2)}, u32[]{:S(2)}) %collective-permute-start.30) | collective-permute-done | bytes 393248 | tf_op jit(solution)/shard_map/ppermute | solution.py:35
  90.8 0.8 fusion.33
  (83 shorter events, 3.5 us)
Async XLA Ops:
  0.0 9.7 %copy-start.2 = (bf16[1,128,2048]{2,1,0:T(8,128)(2,1)S(1)}, bf16[1,128,2048]{2,1,0:T(8,128)(2,1)}, u32[]{:S(2)}) copy-start(bf16[1,128,2048]{2,1,0:T(8,128)(2,1)} %param.4) | copy-start | bytes 1572868
  0.0 7.3 %collective-permute-start = (f32[1,128]{1,0:T(1,128)}, f32[1,128]{1,0:T(1,128)S(1)}, u32[]{:S(2)}, u32[]{:S(2)}) collective-permute-start(f32[1,128]{1,0:T(1,128)} %param.5), channel_id=1, source_target_pairs={{0,16},{16,0},{1,17},{17,1},{2,18},{18,2},{3,19},{19,3},{4,20},{20... | collective-permute-start | bytes 1544 | tf_op jit(solution)/shard_map/ppermute | solution.py:30
  3.0 4.4 %collective-permute-start.1 = (s32[1,128,1]{1,2,0:T(1,128)}, s32[1,128,1]{1,2,0:T(1,128)S(1)}, u32[]{:S(2)}, u32[]{:S(2)}) collective-permute-start(s32[1,128,1]{1,2,0:T(1,128)} %param.6), channel_id=1, source_target_pairs={{0,16},{16,0},{1,17},{17,1},{2,18},{18,2},{3,19},{19,3},{4,20},{20... | collective-permute-start | bytes 1544 | tf_op jit(solution)/shard_map/ppermute | solution.py:30
  4.0 11.9 %collective-permute-start.5 = (bf16[4,64,256]{2,1,0:T(8,128)(2,1)S(1)}, bf16[4,64,256]{2,1,0:T(8,128)(2,1)S(1)}, u32[]{:S(2)}, u32[]{:S(2)}) collective-permute-start(bf16[4,64,256]{2,1,0:T(8,128)(2,1)S(1)} %slice.85), channel_id=1, source_target_pairs={{0,2},{1,3},{2,0},{3,1},{4,6},{5,7},{6,4},{7,5},{8,10},{9,11},{10,... | collective-permute-start | bytes 393224 | tf_op jit(solution)/shard_map/ppermute | solution.py:35
  6.0 9.5 %copy-start.5 = (s32[1,128,1]{1,2,0:T(1,128)S(1)}, s32[1,128,1]{1,2,0:T(1,128)}, u32[]{:S(2)}) copy-start(s32[1,128,1]{1,2,0:T(1,128)} %param.6) | copy-start | bytes 1540
  6.0 9.9 %copy-start = (bf16[1,1,4,128,1408]{4,3,2,1,0:T(8,128)(2,1)S(1)}, bf16[1,1,4,128,1408]{4,3,2,1,0:T(8,128)(2,1)}, u32[]{:S(2)}) copy-start(bf16[1,1,4,128,1408]{4,3,2,1,0:T(8,128)(2,1)} %param.7) | copy-start | bytes 4325380
  7.4 6.4 %collective-permute-start.4 = (s32[1,128,1]{1,2,0:T(1,128)}, s32[1,128,1]{1,2,0:T(1,128)S(1)}, u32[]{:S(2)}, u32[]{:S(2)}) collective-permute-start(s32[1,128,1]{1,2,0:T(1,128)} %param.6), channel_id=1, source_target_pairs={{0,3},{1,2},{2,1},{3,0},{4,7},{5,6},{6,5},{7,4},{8,11},{9,10},{10,... | collective-permute-start | bytes 1544 | tf_op jit(solution)/shard_map/ppermute | solution.py:35
  7.4 7.3 %collective-permute-start.2 = (s32[1,128,1]{1,2,0:T(1,128)}, s32[1,128,1]{1,2,0:T(1,128)S(1)}, u32[]{:S(2)}, u32[]{:S(2)}) collective-permute-start(s32[1,128,1]{1,2,0:T(1,128)} %param.6), channel_id=1, source_target_pairs={{0,1},{1,0},{2,3},{3,2},{4,5},{5,4},{6,7},{7,6},{8,9},{9,8},{10,11... | collective-permute-start | bytes 1544 | tf_op jit(solution)/shard_map/ppermute | solution.py:35
  8.3 5.5 %collective-permute-start.3 = (s32[1,128,1]{1,2,0:T(1,128)}, s32[1,128,1]{1,2,0:T(1,128)S(1)}, u32[]{:S(2)}, u32[]{:S(2)}) collective-permute-start(s32[1,128,1]{1,2,0:T(1,128)} %param.6), channel_id=1, source_target_pairs={{0,2},{1,3},{2,0},{3,1},{4,6},{5,7},{6,4},{7,5},{8,10},{9,11},{10,... | collective-permute-start | bytes 1544 | tf_op jit(solution)/shard_map/ppermute | solution.py:35
  10.1 8.3 %collective-permute-start.10 = (bf16[2,64,512]{2,1,0:T(8,128)(2,1)S(1)}, bf16[2,64,512]{2,1,0:T(8,128)(2,1)S(1)}, u32[]{:S(2)}, u32[]{:S(2)}) collective-permute-start(bf16[2,64,512]{2,1,0:T(8,128)(2,1)S(1)} %get-tuple-element.42), channel_id=1, source_target_pairs={{0,12},{4,8},{8,4},{12,0},{1,13},{5,9},{9,5},{13,1},{2,14},{6,10},... | collective-permute-start | bytes 393224 | tf_op jit(solution)/shard_map/ppermute | solution.py:35
  13.8 11.1 %collective-permute-start.11 = (bf16[2,64,512]{2,1,0:T(8,128)(2,1)S(1)}, bf16[2,64,512]{2,1,0:T(8,128)(2,1)S(1)}, u32[]{:S(2)}, u32[]{:S(2)}) collective-permute-start(bf16[2,64,512]{2,1,0:T(8,128)(2,1)S(1)} %get-tuple-element.41), channel_id=1, source_target_pairs={{0,8},{4,12},{8,0},{12,4},{1,9},{5,13},{9,1},{13,5},{2,10},{6,14},... | collective-permute-start | bytes 393224 | tf_op jit(solution)/shard_map/ppermute | solution.py:35
  13.8 11.1 %collective-permute-start.9 = (bf16[2,64,512]{2,1,0:T(8,128)(2,1)S(1)}, bf16[2,64,512]{2,1,0:T(8,128)(2,1)S(1)}, u32[]{:S(2)}, u32[]{:S(2)}) collective-permute-start(bf16[2,64,512]{2,1,0:T(8,128)(2,1)S(1)} %get-tuple-element.43), channel_id=1, source_target_pairs={{0,4},{4,0},{8,12},{12,8},{1,5},{5,1},{9,13},{13,9},{2,6},{6,2},{1... | collective-permute-start | bytes 393224 | tf_op jit(solution)/shard_map/ppermute | solution.py:35
  14.7 12.4 %collective-permute-start.16 = (bf16[4,64,384]{2,1,0:T(8,128)(2,1)S(1)}, bf16[4,64,384]{2,1,0:T(8,128)(2,1)S(1)}, u32[]{:S(2)}, u32[]{:S(2)}) collective-permute-start(bf16[4,64,384]{2,1,0:T(8,128)(2,1)S(1)} %get-tuple-element.19), channel_id=1, source_target_pairs={{0,2},{1,3},{2,0},{3,1},{4,6},{5,7},{6,4},{7,5},{8,10},{9,11},{10,... | collective-permute-start | bytes 589832 | tf_op jit(solution)/shard_map/ppermute | solution.py:35
  16.1 12.1 %collective-permute-start.6 = (bf16[272,256]{1,0:T(8,128)(2,1)S(1)}, bf16[272,256]{1,0:T(8,128)(2,1)S(1)}, u32[]{:S(2)}, u32[]{:S(2)}) collective-permute-start(bf16[272,256]{1,0:T(8,128)(2,1)S(1)} %pad_maximum_fusion.10), channel_id=1, source_target_pairs={{0,4},{4,0},{8,12},{12,8},{1,5},{5,1},{9,13},{13,9},{2,6},{6,2},{1... | collective-permute-start | bytes 417800 | tf_op jit(solution)/shard_map/ppermute | solution.py:35
  18.4 10.6 %collective-permute-start.21 = (bf16[4,64,384]{2,1,0:T(8,128)(2,1)S(1)}, bf16[4,64,384]{2,1,0:T(8,128)(2,1)S(1)}, u32[]{:S(2)}, u32[]{:S(2)}) collective-permute-start(bf16[4,64,384]{2,1,0:T(8,128)(2,1)S(1)} %get-tuple-element.22), channel_id=1, source_target_pairs={{0,2},{1,3},{2,0},{3,1},{4,6},{5,7},{6,4},{7,5},{8,10},{9,11},{10,... | collective-permute-start | bytes 589832 | tf_op jit(solution)/shard_map/ppermute | solution.py:35
  25.0 9.3 %collective-permute-start.12 = (bf16[4,64,512]{2,1,0:T(8,128)(2,1)S(1)}, bf16[4,64,512]{2,1,0:T(8,128)(2,1)S(1)}, u32[]{:S(2)}, u32[]{:S(2)}) collective-permute-start(bf16[4,64,512]{2,1,0:T(8,128)(2,1)S(1)} %slice_bitcast_fusion), channel_id=1, source_target_pairs={{0,2},{1,3},{2,0},{3,1},{4,6},{5,7},{6,4},{7,5},{8,10},{9,11},{10,... | collective-permute-start | bytes 786440 | tf_op jit(solution)/shard_map/ppermute | solution.py:35
  25.8 10.7 %collective-permute-start.26 = (bf16[4,64,384]{2,1,0:T(8,128)(2,1)S(1)}, bf16[4,64,384]{2,1,0:T(8,128)(2,1)S(1)}, u32[]{:S(2)}, u32[]{:S(2)}) collective-permute-start(bf16[4,64,384]{2,1,0:T(8,128)(2,1)S(1)} %get-tuple-element.26), channel_id=1, source_target_pairs={{0,2},{1,3},{2,0},{3,1},{4,6},{5,7},{6,4},{7,5},{8,10},{9,11},{10,... | collective-permute-start | bytes 589832 | tf_op jit(solution)/shard_map/ppermute | solution.py:35
  27.3 11.5 %collective-permute-start.17 = (bf16[256,384]{1,0:T(8,128)(2,1)S(1)}, bf16[256,384]{1,0:T(8,128)(2,1)S(1)}, u32[]{:S(2)}, u32[]{:S(2)}) collective-permute-start(bf16[256,384]{1,0:T(8,128)(2,1)S(1)} %bitcast.115), channel_id=1, source_target_pairs={{0,4},{4,0},{8,12},{12,8},{1,5},{5,1},{9,13},{13,9},{2,6},{6,2},{1... | collective-permute-start | bytes 589832 | tf_op jit(solution)/shard_map/ppermute | solution.py:35
  28.3 10.1 %collective-permute-start.7 = (bf16[544,256]{1,0:T(8,128)(2,1)S(1)}, bf16[544,256]{1,0:T(8,128)(2,1)S(1)}, u32[]{:S(2)}, u32[]{:S(2)}) collective-permute-start(bf16[544,256]{1,0:T(8,128)(2,1)S(1)} %pad_maximum_fusion.9), channel_id=1, source_target_pairs={{4,8},{8,4},{5,9},{9,5},{6,10},{10,6},{7,11},{11,7},{20,24},{24,20... | collective-permute-start | bytes 835592 | tf_op jit(solution)/shard_map/ppermute | solution.py:235
  29.2 11.1 %collective-permute-start.22 = (bf16[256,384]{1,0:T(8,128)(2,1)S(1)}, bf16[256,384]{1,0:T(8,128)(2,1)S(1)}, u32[]{:S(2)}, u32[]{:S(2)}) collective-permute-start(bf16[256,384]{1,0:T(8,128)(2,1)S(1)} %bitcast.103), channel_id=1, source_target_pairs={{0,4},{4,0},{8,12},{12,8},{1,5},{5,1},{9,13},{13,9},{2,6},{6,2},{1... | collective-permute-start | bytes 589832 | tf_op jit(solution)/shard_map/ppermute | solution.py:35
  34.4 10.2 %collective-permute-start.13 = (bf16[4,2,64,512]{3,2,1,0:T(8,128)(2,1)S(1)}, bf16[4,2,64,512]{3,2,1,0:T(8,128)(2,1)S(1)}, u32[]{:S(2)}, u32[]{:S(2)}) collective-permute-start(bf16[4,2,64,512]{3,2,1,0:T(8,128)(2,1)S(1)} %pad_maximum_fusion.5), channel_id=1, source_target_pairs={{0,16},{16,0},{1,17},{17,1},{2,18},{18,2},{3,19},{19,3},{4,20},{20... | collective-permute-start | bytes 1572872 | tf_op jit(solution)/shard_map/ppermute | solution.py:30
  36.7 7.9 %collective-permute-start.27 = (bf16[256,384]{1,0:T(8,128)(2,1)S(1)}, bf16[256,384]{1,0:T(8,128)(2,1)S(1)}, u32[]{:S(2)}, u32[]{:S(2)}) collective-permute-start(bf16[256,384]{1,0:T(8,128)(2,1)S(1)} %bitcast.112), channel_id=1, source_target_pairs={{0,4},{4,0},{8,12},{12,8},{1,5},{5,1},{9,13},{13,9},{2,6},{6,2},{1... | collective-permute-start | bytes 589832 | tf_op jit(solution)/shard_map/ppermute | solution.py:35
  38.4 9.2 %collective-permute-start.8 = (bf16[544,256]{1,0:T(8,128)(2,1)S(1)}, bf16[544,256]{1,0:T(8,128)(2,1)S(1)}, u32[]{:S(2)}, u32[]{:S(2)}) collective-permute-start(bf16[544,256]{1,0:T(8,128)(2,1)S(1)} %collective-permute-done.7), channel_id=1, source_target_pairs={{8,12},{4,0},{0,4},{12,8},{9,13},{5,1},{1,5},{13,9},{10,14},{6,2},... | collective-permute-start | bytes 835592 | tf_op jit(solution)/shard_map/ppermute | solution.py:238
  38.8 8.9 %copy-start.3 = (bf16[256,384]{1,0:T(8,128)(2,1)}, bf16[256,384]{1,0:T(8,128)(2,1)S(1)}, u32[]{:S(2)}) copy-start(bf16[256,384]{1,0:T(8,128)(2,1)S(1)} %collective-permute-done.17) | copy-start | bytes 589828
  38.9 8.8 %collective-permute-start.18 = (bf16[512,384]{1,0:T(8,128)(2,1)S(1)}, bf16[512,384]{1,0:T(8,128)(2,1)}, u32[]{:S(2)}, u32[]{:S(2)}) collective-permute-start(bf16[512,384]{1,0:T(8,128)(2,1)S(1)} %pad_maximum_fusion.6), channel_id=1, source_target_pairs={{4,8},{8,4},{5,9},{9,5},{6,10},{10,6},{7,11},{11,7},{20,24},{24,20... | collective-permute-start | bytes 1179656 | tf_op jit(solution)/shard_map/ppermute | solution.py:235
  44.7 16.3 %collective-permute-start.14 = (bf16[4,2,64,512]{3,2,1,0:T(8,128)(2,1)S(1)}, bf16[4,2,64,512]{3,2,1,0:T(8,128)(2,1)S(1)}, u32[]{:S(2)}, u32[]{:S(2)}) collective-permute-start(bf16[4,2,64,512]{3,2,1,0:T(8,128)(2,1)S(1)} %collective-permute-done.13), channel_id=1, source_target_pairs={{0,1},{1,0},{2,3},{3,2},{4,5},{5,4},{6,7},{7,6},{8,9},{9,8},{10,11... | collective-permute-start | bytes 1572872 | tf_op jit(solution)/shard_map/ppermute | solution.py:35
  47.7 3.1 %collective-permute-start.23 = (bf16[512,384]{1,0:T(8,128)(2,1)}, bf16[512,384]{1,0:T(8,128)(2,1)}, u32[]{:S(2)}, u32[]{:S(2)}) collective-permute-start(bf16[512,384]{1,0:T(8,128)(2,1)} %pad_maximum_fusion.7), channel_id=1, source_target_pairs={{4,8},{8,4},{5,9},{9,5},{6,10},{10,6},{7,11},{11,7},{20,24},{24,20... | collective-permute-start | bytes 1179656 | tf_op jit(solution)/shard_map/ppermute | solution.py:235
  49.5 14.7 %collective-permute-start.19 = (bf16[512,384]{1,0:T(8,128)(2,1)}, bf16[512,384]{1,0:T(8,128)(2,1)S(1)}, u32[]{:S(2)}, u32[]{:S(2)}) collective-permute-start(bf16[512,384]{1,0:T(8,128)(2,1)} %collective-permute-done.18), channel_id=1, source_target_pairs={{8,12},{4,0},{9,13},{5,1},{10,14},{6,2},{11,15},{7,3},{24,28},{20,... | collective-permute-start | bytes 1179656 | tf_op jit(solution)/shard_map/ppermute | solution.py:238
  50.8 22.5 %collective-permute-start.24 = (bf16[512,384]{1,0:T(8,128)(2,1)}, bf16[512,384]{1,0:T(8,128)(2,1)S(1)}, u32[]{:S(2)}, u32[]{:S(2)}) collective-permute-start(bf16[512,384]{1,0:T(8,128)(2,1)} %collective-permute-done.23), channel_id=1, source_target_pairs={{8,12},{4,0},{0,4},{12,8},{9,13},{5,1},{1,5},{13,9},{10,14},{6,2},... | collective-permute-start | bytes 1179656 | tf_op jit(solution)/shard_map/ppermute | solution.py:238
  60.3 10.0 %collective-permute-start.28 = (bf16[512,384]{1,0:T(8,128)(2,1)S(1)}, bf16[512,384]{1,0:T(8,128)(2,1)S(1)}, u32[]{:S(2)}, u32[]{:S(2)}) collective-permute-start(bf16[512,384]{1,0:T(8,128)(2,1)S(1)} %pad_maximum_fusion.8), channel_id=1, source_target_pairs={{4,8},{8,4},{5,9},{9,5},{6,10},{10,6},{7,11},{11,7},{20,24},{24,20... | collective-permute-start | bytes 1179656 | tf_op jit(solution)/shard_map/ppermute | solution.py:235
  62.2 2.0 %copy-start.4 = (bf16[256,384]{1,0:T(8,128)(2,1)S(1)}, bf16[256,384]{1,0:T(8,128)(2,1)}, u32[]{:S(2)}) copy-start(bf16[256,384]{1,0:T(8,128)(2,1)} %copy-done.3) | copy-start | bytes 589828
  62.2 7.9 %collective-permute-start.15 = (bf16[512,256]{1,0:T(8,128)(2,1)S(1)}, bf16[512,256]{1,0:T(8,128)(2,1)S(1)}, u32[]{:S(2)}, u32[]{:S(2)}) collective-permute-start(bf16[512,256]{1,0:T(8,128)(2,1)S(1)} %slice.144), channel_id=1, source_target_pairs={{0,2},{1,3},{2,0},{3,1},{4,6},{5,7},{6,4},{7,5},{8,10},{9,11},{10,... | collective-permute-start | bytes 786440 | tf_op jit(solution)/shard_map/ppermute | solution.py:35
  65.6 16.1 %collective-permute-start.20 = (bf16[512,384]{1,0:T(8,128)(2,1)S(1)}, bf16[512,384]{1,0:T(8,128)(2,1)S(1)}, u32[]{:S(2)}, u32[]{:S(2)}) collective-permute-start(bf16[512,384]{1,0:T(8,128)(2,1)S(1)} %slice.143), channel_id=1, source_target_pairs={{0,2},{1,3},{2,0},{3,1},{4,6},{5,7},{6,4},{7,5},{8,10},{9,11},{10,... | collective-permute-start | bytes 1179656 | tf_op jit(solution)/shard_map/ppermute | solution.py:35
  70.3 8.7 %collective-permute-start.29 = (bf16[512,384]{1,0:T(8,128)(2,1)S(1)}, bf16[512,384]{1,0:T(8,128)(2,1)S(1)}, u32[]{:S(2)}, u32[]{:S(2)}) collective-permute-start(bf16[512,384]{1,0:T(8,128)(2,1)S(1)} %collective-permute-done.28), channel_id=1, source_target_pairs={{8,12},{4,0},{0,4},{12,8},{9,13},{5,1},{1,5},{13,9},{10,14},{6,2},... | collective-permute-start | bytes 1179656 | tf_op jit(solution)/shard_map/ppermute | solution.py:238
  74.8 11.8 %collective-permute-start.25 = (bf16[512,384]{1,0:T(8,128)(2,1)S(1)}, bf16[512,384]{1,0:T(8,128)(2,1)S(1)}, u32[]{:S(2)}, u32[]{:S(2)}) collective-permute-start(bf16[512,384]{1,0:T(8,128)(2,1)S(1)} %slice.142), channel_id=1, source_target_pairs={{0,2},{1,3},{2,0},{3,1},{4,6},{5,7},{6,4},{7,5},{8,10},{9,11},{10,... | collective-permute-start | bytes 1179656 | tf_op jit(solution)/shard_map/ppermute | solution.py:35
  80.4 10.3 %collective-permute-start.30 = (bf16[512,384]{1,0:T(8,128)(2,1)S(1)}, bf16[512,384]{1,0:T(8,128)(2,1)S(1)}, u32[]{:S(2)}, u32[]{:S(2)}) collective-permute-start(bf16[512,384]{1,0:T(8,128)(2,1)S(1)} %slice.141), channel_id=1, source_target_pairs={{0,2},{1,3},{2,0},{3,1},{4,6},{5,7},{6,4},{7,5},{8,10},{9,11},{10,... | collective-permute-start | bytes 1179656 | tf_op jit(solution)/shard_map/ppermute | solution.py:35
  86.7 4.1 %copy-start.1 = (bf16[1,512,1408]{2,1,0:T(8,128)(2,1)}, bf16[1,512,1408]{2,1,0:T(8,128)(2,1)S(1)}, u32[]{:S(2)}) copy-start(bf16[1,512,1408]{2,1,0:T(8,128)(2,1)S(1)} %fusion.31) | copy-start | bytes 4325380
